TPU v7x, 256 devices: a whole 4x4x8 slice. The times are simulated.
256 devices in a mesh: ex: 32 (over y_hi, z, core), lb: 8 (over y_lo, x).
Axes of the slice: x: 4, y: 4 (y_hi: 2, y_lo: 2; y = y_hi * 2 + y_lo), z: 8, core: 2. Of those that a mesh axis runs over, the one named last changes fastest.
Arguments:
- train_grads: bfloat16 [65536, 16384], P('ex', 'lb'), may hold values from -6 to 6
- query_grads: bfloat16 [1024, 16384], P('ex', 'lb'), may hold values from -0.046875 to 0.046875
- precond: bfloat16 [32, 512, 512], P('lb'), as said below
Outputs:
- scores: float32 [1024, 65536], P('lb', 'ex')
Inputs may be any that keep to these rules, and one draw needn't show every extreme that they name: `precond`: each block is symmetric with its diagonal between 0.5 and 2.
All inputs are finite; a program needn't handle non-finite values.
Results may differ from a plain program's by a relative error of at most 0.015.
Values may be sent and summed in bfloat16 or wider, within the bound.
No kernel may reach another device: no remote copies, remote signals or barrier semaphores. Data moves between devices by JAX's collectives and lax.ppermute only.
A program may use at most 64 MiB of HBM per device.

v0:
```python
import jax
import jax.numpy as jnp
from jax import lax
from jax.sharding import PartitionSpec as P


def prepare(rows, blocks):
    count = rows.shape[0]
    split = rows.reshape(count, blocks.shape[0], blocks.shape[1])
    mixed = jnp.einsum("rbi,bij->rbj", split, blocks, preferred_element_type=jnp.float32)
    return mixed.reshape(count, -1).astype(jnp.bfloat16)


def score_rows(ready, train_grads):
    return lax.dot_general(
        ready, train_grads, (((1,), (1,)), ((), ())), preferred_element_type=jnp.float32
    )


def on_device(train_grads, query_grads, precond):
    moving = prepare(query_grads, precond)
    gathered = lax.all_gather(moving, "ex", axis=0, tiled=True)
    partial_value = score_rows(gathered, train_grads)
    scores = lax.psum_scatter(
        partial_value.astype(jnp.bfloat16), "lb", scatter_dimension=0, tiled=True
    ).astype(jnp.float32)
    return scores


def solution(mesh):
    placed = (P("ex", "lb"), P("ex", "lb"), P("lb", None, None))
    return jax.shard_map(
        on_device, mesh=mesh, in_specs=placed, out_specs=P("lb", "ex"), check_vma=False
    )
```

profile of v0, /device:TPU:16, one launch (start us, length us, event | category | flops | bytes accessed | tf_op | source)
XLA Modules:
  0.0 174.9 jit_solution(13776324374581515294)
XLA Ops:
  6.5 0.0 copy-start
  6.5 0.0 all-gather.2.cloned.1.call-start
  6.5 1.6 copy-done
  8.1 1.3 fusion
  9.5 0.7 copy.8
  10.1 0.0 all-gather.2.cloned.1.call-update
  10.2 0.0 reduce-scatter.2.cloned.1.call-start
  10.2 87.4 %all-gather.2.cloned.1.call-done = bf16[1024,2048]{1,0:T(8,128)(2,1)} async-done(((bf16[32,2048]{1,0:T(8,128)(2,1)}), bf16[1024,2048]{1,0:T(8,128)(2,1)}) %all-gather.2.cloned.1.call-update) | async-done | bytes 4194320 | tf_op jit(solution)/shard_map/all_gather | solution.py:22
  97.6 13.9 %convolution_convert_fusion = bf16[1024,2048]{1,0:T(8,128)(2,1)} fusion(bf16[1024,2048]{1,0:T(8,128)(2,1)} %all-gather.2.cloned.1.call-done, bf16[2048,2048]{1,0:T(8,128)(2,1)} %param.3), kind=kOutput, calls=%fused_computation | convolution fusion | flops 8592031744 | bytes 16777216 | tf_op jit(solution)/shard_map/dot_general | solution.py:15
  111.4 0.0 reduce-scatter.2.cloned.1.call-update
  111.5 54.5 %reduce-scatter.2.cloned.1.call-done = bf16[128,2048]{1,0:T(8,128)(2,1)} async-done(((bf16[1024,2048]{1,0:T(8,128)(2,1)}), bf16[128,2048]{1,0:T(8,128)(2,1)}) %reduce-scatter.2.cloned.1.call-update) | async-done | bytes 524304 | tf_op jit(solution)/shard_map/reduce_scatter | solution.py:24
  165.9 2.1 %convert_element_type.19 = f32[128,2048]{1,0:T(8,128)} convert(bf16[128,2048]{1,0:T(8,128)(2,1)} %reduce-scatter.2.cloned.1.call-done) | non-fusion elementwise | flops 262144 | bytes 1572864 | tf_op jit(solution)/shard_map/convert_element_type | solution.py:26
Async XLA Ops:
  6.5 1.6 copy-start
  6.5 91.0 %all-gather.2.cloned.1.call-start = ((), (), s32[]{:S(2)}) async-start(), calls=%async_computation.1 | async-start | bytes 4325376 | tf_op jit(solution)/shard_map/all_gather | solution.py:22
  10.2 155.7 %reduce-scatter.2.cloned.1.call-start = ((), (), s32[]{:S(2)}) async-start(), calls=%async_computation.2 | async-start | bytes 4718592 | tf_op jit(solution)/shard_map/reduce_scatter | solution.py:24
Sparse Core Ops, SparseCore 0:
  10.3 87.2 all-gather.1
  111.6 54.2 reduce-scatter.1
where the time goes:
time: 176 us; the launch traced here: 175 us
  waiting for transfers between devices  142 us (81%)
  matrix products  15.2 us (9%)
  between operations  13.4 us (8%)
  local copies, waits for them, and re-layouts  2.27 us (1%)
  other arithmetic  2.12 us (1%)
    all_gather x1, waiting for transfers between devices, on_device(): gathered = lax.all_gather(moving, 'ex', axis=0, tiled=True)  87.4 us
    reduce_scatter x1, waiting for transfers between devices, on_device(): lax.psum_scatter(partial_value.astype(jnp.bfloat16), 'lb', scatter_dimens...  54.5 us
    dot_general x1, matrix products, score_rows(): lax.dot_general(ready, train_grads, (((1,), (1,)), ((), ())), preferred_e...  13.9 us
  transfers between devices with their start and end apart: 2, of which 2 were waited for; matrix products, arithmetic and copies ran while one was open for 0% of the time, Pallas kernels for 0%

commit v1 on v0

v1 whole, which is shorter than its diff:
```python
import itertools

import jax
import jax.numpy as jnp
from jax import lax
from jax.sharding import Mesh, PartitionSpec as P

NAMES = ("h", "z", "c", "l", "x")
SIZES = (2, 8, 2, 2, 4)


def move(value, target):
    pairs = []
    for place in itertools.product(*map(range, SIZES)):
        to = target(*place)
        if to is not None:
            pairs.append((flat(place), flat(to)))
    return lax.ppermute(value, NAMES, pairs)


def flat(place):
    index = 0
    for at, size in zip(place, SIZES, strict=True):
        index = index * size + at % size
    return index


def other_core(value):
    return move(value, lambda h, z, c, l, x: (h, z, 1 - c, l, x))


def other_half(value):
    return move(value, lambda h, z, c, l, x: (1 - h, z, c, l, x))


def other_run(value):
    return move(value, lambda h, z, c, l, x: (h, z, c, 1 - l, x))


def along_z(value):
    return move(value, lambda h, z, c, l, x: (h, z + (1 if c == 0 else -1), c, l, x))


def first_x(value):
    return move(value, lambda h, z, c, l, x: (h, z, c, l, x ^ (1 if c == 0 else 3)))


def second_x(value):
    return move(value, lambda h, z, c, l, x: (h, z, c, l, x ^ (3 if c == 0 else 1)))


def prepare(rows, blocks):
    size = blocks.shape[1]
    parts = [
        jnp.dot(
            rows[:, b * size : (b + 1) * size], blocks[b], preferred_element_type=jnp.float32
        ).astype(jnp.bfloat16)
        for b in range(blocks.shape[0])
    ]
    return jnp.concatenate(parts, axis=1)


def score_rows(ready, train_grads):
    return lax.dot_general(
        ready, train_grads, (((1,), (1,)), ((), ())), preferred_element_type=jnp.float32
    )


def both_cores(c, mine, theirs):
    return jnp.where(
        c == 0, jnp.concatenate([mine, theirs]), jnp.concatenate([theirs, mine])
    )


def gather_planes(c, plane):
    rows = plane.shape[0]
    one = along_z(plane)
    two = along_z(one)
    three = along_z(two)
    half = lax.dynamic_slice_in_dim(three, c * (rows // 2), rows // 2)
    four = along_z(half)
    odd = jnp.concatenate([one, three])
    odd_theirs = other_core(odd)
    even = jnp.concatenate([two, four])
    even_theirs = other_core(even)
    far = both_cores(c, even[rows:], even_theirs[rows:])
    odd_set = jnp.concatenate([odd, odd_theirs])
    even_set = jnp.concatenate([plane, even[:rows], even_theirs[:rows], far])
    return odd_set, even_set


def reduce_x(x, c, block, train_grads):
    m1 = jnp.where(c == 0, 1, 3)
    m2 = jnp.where(c == 0, 3, 1)
    sent = jnp.concatenate([block(x ^ m1), block(x ^ 2)])
    kept = jnp.concatenate([block(x), block(x ^ m2)])
    rows = kept.shape[0] // 2
    come = first_x(score_rows(sent, train_grads).astype(jnp.bfloat16))
    kept = lax.optimization_barrier(score_rows(kept, train_grads))
    total = kept + come.astype(jnp.float32)
    come = second_x(total[rows:].astype(jnp.bfloat16))
    return total[:rows] + come.astype(jnp.float32)


def on_device(train_grads, query_grads, precond):
    h, z, c, l, x = (lax.axis_index(name) for name in NAMES)
    mine = prepare(query_grads, precond)
    rows = 2 * mine.shape[0]
    across = other_half(mine)
    plane = both_cores(c, mine, other_core(mine))
    plane_across = both_cores(c, across, other_core(across))

    def odd_place(owner):
        step = (2 * owner + 1 - z % 2 - z) % 8
        near = (step == 1) | (step == 7)
        above = step < 4
        own = above == (c == 1)
        return jnp.where(own, 0, 2) + jnp.where(near, 0, 1)

    def even_place(owner):
        step = (2 * owner + z % 2 - z) % 8
        own = (step == 2) == (c == 1)
        return jnp.where(step == 0, 0, jnp.where(step == 4, 3, jnp.where(own, 1, 2)))

    sums = []
    for start in (plane, plane_across):
        odd_set, even_set = gather_planes(c, start)
        for held, place in ((odd_set, odd_place), (even_set, even_place)):
            block = lambda owner: lax.dynamic_slice_in_dim(held, place(owner) * rows, rows)
            sums.append(reduce_x(x, c, block, train_grads))
    odd, even, odd_across, even_across = sums

    def over_runs(own, across):
        sent = jnp.where(l == h, across, own).astype(jnp.bfloat16)
        kept = jnp.where(l == h, own, across)
        return kept + other_run(sent).astype(jnp.float32)

    odd = over_runs(odd, odd_across)
    even = over_runs(even, even_across)
    return jnp.where(z % 2 == 0, jnp.concatenate([even, odd]), jnp.concatenate([odd, even]))


def solution(mesh):
    wide = Mesh(mesh.devices.reshape(SIZES), NAMES)
    ex, lb = NAMES[:3], NAMES[3:]
    placed = (P(ex, lb), P(ex, lb), P(lb, None, None))
    return jax.shard_map(
        on_device, mesh=wide, in_specs=placed, out_specs=P(lb, ex), check_vma=False
    )
```

time: 176 us -> 103 us (0.59)
  waiting for transfers between devices: 142 us -> 48.4 us
  starting transfers between devices: 0.04 us -> 22.5 us
  between operations: 13.4 us -> 0.43 us
  matrix products: 15.2 us -> 28.1 us
    all_gather x1 -> x0, waiting for transfers between devices: 87.4 us -> none  [on_device(): gathered = lax.all_gather(moving, 'ex', axis=0, tiled=True)]
    reduce_scatter x1 -> x0, waiting for transfers between devices: 54.5 us -> none  [on_device(): lax.psum_scatter(partial_value.astype(jnp.bfloat16), 'lb', scatter_dimens...]
    ppermute x0 -> x25, waiting for transfers between devices: none -> 48.4 us  [move(): return lax.ppermute(value, NAMES, pairs)]
    ppermute x0 -> x25, starting transfers between devices: none -> 22.5 us  [move(): return lax.ppermute(value, NAMES, pairs)]
    dot_general x1 -> x8, matrix products: 13.9 us -> 23 us  [score_rows(): lax.dot_general(ready, train_grads, (((1,), (1,)), ((), ())), preferred_e...]
    dot_general x1 -> x4, matrix products: 1.33 us -> 5.02 us  [prepare(): jnp.dot(rows[:, b * size:(b + 1) * size], blocks[b], preferred_element_ty...]
    convert_element_type x1 -> x2, other arithmetic: 2.12 us -> 0.2 us  [over_runs(): sent = jnp.where(l == h, across, own).astype(jnp.bfloat16)]
  transfers between devices with their start and end apart: 2 -> 25, of which waited for: 2 -> 15; matrix products, arithmetic and copies ran while one was open for 0% -> 24% of each run, Pallas kernels for 0% -> 0%
where the time goes in v1:
time: 103 us
  waiting for transfers between devices  48.4 us (47%)
  matrix products  28.1 us (27%)
  starting transfers between devices  22.5 us (22%)
  other arithmetic  2.46 us (2%)
    ppermute x25, waiting for transfers between devices, move(): return lax.ppermute(value, NAMES, pairs)  48.4 us
    dot_general x8, matrix products, score_rows(): lax.dot_general(ready, train_grads, (((1,), (1,)), ((), ())), preferred_e...  23 us
    ppermute x25, starting transfers between devices, move(): return lax.ppermute(value, NAMES, pairs)  22.5 us
    dot_general x4, matrix products, prepare(): jnp.dot(rows[:, b * size:(b + 1) * size], blocks[b], preferred_element_ty...  5.02 us
  transfers between devices with their start and end apart: 25, of which 15 were waited for; matrix products, arithmetic and copies ran while one was open for 24% of the time, Pallas kernels for 0%

profile of v1, /device:TPU:16, one launch (start us, length us, event | category | flops | bytes accessed | tf_op | source)
XLA Modules:
  0.0 102.6 jit_solution(16730255033333465220)
XLA Ops:
  0.0 1.2 %convolution_convert_fusion.4 = bf16[32,512]{1,0:T(8,128)(2,1)S(1)} fusion(bf16[4,512,512]{2,1,0:T(8,128)(2,1)} %param.5, bf16[32,2048]{1,0:T(8,128)(2,1)} %param.4), kind=kOutput, calls=%fused_computation.4 | convolution fusion | flops 16793600 | bytes 589824 | tf_op jit(solution)/shard_map/dot_general | solution.py:55
  1.2 1.3 %convolution_convert_fusion.5 = bf16[32,512]{1,0:T(8,128)(2,1)S(1)} fusion(bf16[4,512,512]{2,1,0:T(8,128)(2,1)} %param.5, bf16[32,2048]{1,0:T(8,128)(2,1)} %param.4), kind=kOutput, calls=%fused_computation.5 | convolution fusion | flops 16793600 | bytes 589824 | tf_op jit(solution)/shard_map/dot_general | solution.py:55
  2.5 1.3 %convolution_convert_fusion.6 = bf16[32,512]{1,0:T(8,128)(2,1)S(1)} fusion(bf16[4,512,512]{2,1,0:T(8,128)(2,1)} %param.5, bf16[32,2048]{1,0:T(8,128)(2,1)} %param.4), kind=kOutput, calls=%fused_computation.6 | convolution fusion | flops 16793600 | bytes 589824 | tf_op jit(solution)/shard_map/dot_general | solution.py:55
  3.8 1.3 %convolution_convert_fusion.7 = bf16[32,512]{1,0:T(8,128)(2,1)S(1)} fusion(bf16[4,512,512]{2,1,0:T(8,128)(2,1)} %param.5, bf16[32,2048]{1,0:T(8,128)(2,1)} %param.4), kind=kOutput, calls=%fused_computation.7 | convolution fusion | flops 16793600 | bytes 589824 | tf_op jit(solution)/shard_map/dot_general | solution.py:55
  5.1 2.2 %collective-permute-start.8 = (bf16[32,2048]{1,0:T(8,128)(2,1)S(1)}, bf16[32,2048]{1,0:T(8,128)(2,1)S(1)}, u32[]{:S(2)}, u32[]{:S(2)}) collective-permute-start(bf16[32,2048]{1,0:T(8,128)(2,1)S(1)} %pad_maximum_fusion.6), channel_id=1, source_target_pairs={{0,128},{1,129},{2,130},{3,131},{4,132},{5,133},{6,134},{7,135},{8... | collective-permute-start | bytes 393224 | tf_op jit(solution)/shard_map/ppermute | solution.py:18
  7.2 0.0 collective-permute-start
  7.2 4.7 %collective-permute-done.8 = bf16[32,2048]{1,0:T(8,128)(2,1)S(1)} collective-permute-done((bf16[32,2048]{1,0:T(8,128)(2,1)S(1)}, bf16[32,2048]{1,0:T(8,128)(2,1)S(1)}, u32[]{:S(2)}, u32[]{:S(2)}) %collective-permute-start.8) | collective-permute-done | bytes 131104 | tf_op jit(solution)/shard_map/ppermute | solution.py:18
  11.9 0.0 collective-permute-start.9
  11.9 0.0 collective-permute-done
  11.9 2.0 %collective-permute-start.1 = (bf16[64,2048]{1,0:T(8,128)(2,1)S(1)}, bf16[64,2048]{1,0:T(8,128)(2,1)S(1)}, u32[]{:S(2)}, u32[]{:S(2)}) collective-permute-start(bf16[64,2048]{1,0:T(8,128)(2,1)S(1)} %maximum_select_fusion.1), channel_id=1, source_target_pairs={{0,16},{1,17},{2,18},{3,19},{4,20},{5,21},{6,22},{7,23},{8,120},{9... | collective-permute-start | bytes 786440 | tf_op jit(solution)/shard_map/ppermute | solution.py:18
  13.9 0.0 collective-permute-done.9
  14.0 2.0 %collective-permute-start.10 = (bf16[64,2048]{1,0:T(8,128)(2,1)S(1)}, bf16[64,2048]{1,0:T(8,128)(2,1)S(1)}, u32[]{:S(2)}, u32[]{:S(2)}) collective-permute-start(bf16[64,2048]{1,0:T(8,128)(2,1)S(1)} %maximum_select_fusion.3), channel_id=1, source_target_pairs={{0,16},{1,17},{2,18},{3,19},{4,20},{5,21},{6,22},{7,23},{8,120},{9... | collective-permute-start | bytes 786440 | tf_op jit(solution)/shard_map/ppermute | solution.py:18
  16.0 6.2 %collective-permute-done.1 = bf16[64,2048]{1,0:T(8,128)(2,1)S(1)} collective-permute-done((bf16[64,2048]{1,0:T(8,128)(2,1)S(1)}, bf16[64,2048]{1,0:T(8,128)(2,1)S(1)}, u32[]{:S(2)}, u32[]{:S(2)}) %collective-permute-start.1) | collective-permute-done | bytes 262176 | tf_op jit(solution)/shard_map/ppermute | solution.py:18
  22.2 2.8 %collective-permute-done.10 = bf16[64,2048]{1,0:T(8,128)(2,1)S(1)} collective-permute-done((bf16[64,2048]{1,0:T(8,128)(2,1)S(1)}, bf16[64,2048]{1,0:T(8,128)(2,1)S(1)}, u32[]{:S(2)}, u32[]{:S(2)}) %collective-permute-start.10) | collective-permute-done | bytes 262176 | tf_op jit(solution)/shard_map/ppermute | solution.py:18
  25.0 4.8 %collective-permute-done.2 = bf16[64,2048]{1,0:T(8,128)(2,1)S(1)} collective-permute-done((bf16[64,2048]{1,0:T(8,128)(2,1)S(1)}, bf16[64,2048]{1,0:T(8,128)(2,1)S(1)}, u32[]{:S(2)}, u32[]{:S(2)}) %collective-permute-start.2) | collective-permute-done | bytes 262176 | tf_op jit(solution)/shard_map/ppermute | solution.py:18
  29.9 2.8 %collective-permute-done.11 = bf16[64,2048]{1,0:T(8,128)(2,1)S(1)} collective-permute-done((bf16[64,2048]{1,0:T(8,128)(2,1)S(1)}, bf16[64,2048]{1,0:T(8,128)(2,1)S(1)}, u32[]{:S(2)}, u32[]{:S(2)}) %collective-permute-start.11) | collective-permute-done | bytes 262176 | tf_op jit(solution)/shard_map/ppermute | solution.py:18
  32.6 4.8 %collective-permute-done.3 = bf16[64,2048]{1,0:T(8,128)(2,1)S(1)} collective-permute-done((bf16[64,2048]{1,0:T(8,128)(2,1)S(1)}, bf16[64,2048]{1,0:T(8,128)(2,1)S(1)}, u32[]{:S(2)}, u32[]{:S(2)}) %collective-permute-start.3) | collective-permute-done | bytes 262176 | tf_op jit(solution)/shard_map/ppermute | solution.py:18
  37.4 0.1 collective-permute-start.4
  37.6 0.1 collective-permute-start.18
  37.7 2.5 %collective-permute-done.12 = bf16[64,2048]{1,0:T(8,128)(2,1)S(1)} collective-permute-done((bf16[64,2048]{1,0:T(8,128)(2,1)S(1)}, bf16[64,2048]{1,0:T(8,128)(2,1)S(1)}, u32[]{:S(2)}, u32[]{:S(2)}) %collective-permute-start.12) | collective-permute-done | bytes 262176 | tf_op jit(solution)/shard_map/ppermute | solution.py:18
  40.2 0.1 collective-permute-start.13
  40.3 3.4 %collective-permute-done.4 = bf16[32,2048]{1,0:T(8,128)(2,1)S(1)} collective-permute-done((bf16[32,2048]{1,0:T(8,128)(2,1)S(1)}, bf16[32,2048]{1,0:T(8,128)(2,1)S(1)}, u32[]{:S(2)}, u32[]{:S(2)}) %collective-permute-start.4) | collective-permute-done | bytes 131104 | tf_op jit(solution)/shard_map/ppermute | solution.py:18
  43.7 0.1 collective-permute-start.5
  43.9 0.6 collective-permute-start.21
  44.5 2.0 %collective-permute-done.13 = bf16[32,2048]{1,0:T(8,128)(2,1)S(1)} collective-permute-done((bf16[32,2048]{1,0:T(8,128)(2,1)S(1)}, bf16[32,2048]{1,0:T(8,128)(2,1)S(1)}, u32[]{:S(2)}, u32[]{:S(2)}) %collective-permute-start.13) | collective-permute-done | bytes 131104 | tf_op jit(solution)/shard_map/ppermute | solution.py:18
  46.5 0.3 collective-permute-start.14
  46.9 0.1 pad_maximum_fusion
  47.0 0.1 constant_dynamic-slice_fusion.14
  47.1 2.9 %convolution_convert_fusion.3 = bf16[128,2048]{1,0:T(8,128)(2,1)S(1)} fusion(bf16[2048,2048]{1,0:T(8,128)(2,1)S(1)} %copy-done, bf16[64,2048]{1,0:T(8,128)(2,1)S(1)} %get-tuple-element.10, bf16[64,2048]{1,0:T(8,128)(2,1)S(1)} %get-tuple-element.9), kind=kOutput, calls=%fused_computation.3 | convolution fusion | flops 1075052544 | bytes 9437184 | tf_op jit(solution)/shard_map/dot_general | solution.py:64
  50.0 1.6 %collective-permute-start.6 = (bf16[128,2048]{1,0:T(8,128)(2,1)S(1)}, bf16[128,2048]{1,0:T(8,128)(2,1)S(1)}, u32[]{:S(2)}, u32[]{:S(2)}) collective-permute-start(bf16[128,2048]{1,0:T(8,128)(2,1)S(1)} %convolution_convert_fusion.3), channel_id=1, source_target_pairs={{0,1},{1,0},{2,3},{3,2},{4,5},{5,4},{6,7},{7,6},{8,11},{9,10},{10,... | collective-permute-start | bytes 1572872 | tf_op jit(solution)/shard_map/ppermute | solution.py:18
  51.6 2.9 %fusion = f32[128,2048]{1,0:T(8,128)S(1)} fusion(bf16[2048,2048]{1,0:T(8,128)(2,1)S(1)} %copy-done, bf16[64,2048]{1,0:T(8,128)(2,1)S(1)} %get-tuple-element.11, bf16[64,2048]{1,0:T(8,128)(2,1)S(1)} %get-tuple-element.12), kind=kOutput, calls=%fused_computation.23 | convolution fusion | flops 1074790400 | bytes 9961472 | tf_op jit(solution)/shard_map/dot_general | solution.py:64
  54.6 0.1 pad_maximum_fusion.1
  54.7 0.1 constant_dynamic-slice_fusion.9
  54.8 2.9 %convolution_convert_fusion.2 = bf16[128,2048]{1,0:T(8,128)(2,1)S(1)} fusion(bf16[2048,2048]{1,0:T(8,128)(2,1)S(1)} %copy-done, bf16[64,2048]{1,0:T(8,128)(2,1)S(1)} %get-tuple-element.6, bf16[64,2048]{1,0:T(8,128)(2,1)S(1)} %get-tuple-element.5), kind=kOutput, calls=%fused_computation.2 | convolution fusion | flops 1075052544 | bytes 9437184 | tf_op jit(solution)/shard_map/dot_general | solution.py:64
  57.7 0.6 collective-permute-start.15
  58.3 2.9 %fusion.7 = f32[128,2048]{1,0:T(8,128)S(1)} fusion(bf16[2048,2048]{1,0:T(8,128)(2,1)S(1)} %copy-done, bf16[64,2048]{1,0:T(8,128)(2,1)S(1)} %get-tuple-element.7, bf16[64,2048]{1,0:T(8,128)(2,1)S(1)} %get-tuple-element.8), kind=kOutput, calls=%fused_computation.30 | convolution fusion | flops 1074790400 | bytes 9961472 | tf_op jit(solution)/shard_map/dot_general | solution.py:64
  61.2 0.3 constant_dynamic-slice_fusion.1
  61.5 2.9 %convolution_convert_fusion = bf16[128,2048]{1,0:T(8,128)(2,1)S(1)} fusion(bf16[2048,2048]{1,0:T(8,128)(2,1)S(1)} %copy-done, bf16[64,2048]{1,0:T(8,128)(2,1)S(1)} %get-tuple-element.14, bf16[64,2048]{1,0:T(8,128)(2,1)S(1)} %get-tuple-element.13), kind=kOutput, calls=%fused_computation | convolution fusion | flops 1075052544 | bytes 9437184 | tf_op jit(solution)/shard_map/dot_general | solution.py:64
  64.4 1.8 %collective-permute-start.22 = (bf16[128,2048]{1,0:T(8,128)(2,1)S(1)}, bf16[128,2048]{1,0:T(8,128)(2,1)S(1)}, u32[]{:S(2)}, u32[]{:S(2)}) collective-permute-start(bf16[128,2048]{1,0:T(8,128)(2,1)S(1)} %convolution_convert_fusion), channel_id=1, source_target_pairs={{0,1},{1,0},{2,3},{3,2},{4,5},{5,4},{6,7},{7,6},{8,11},{9,10},{10,... | collective-permute-start | bytes 1572872 | tf_op jit(solution)/shard_map/ppermute | solution.py:18
  66.2 2.9 %fusion.21 = f32[128,2048]{1,0:T(8,128)S(1)} fusion(bf16[2048,2048]{1,0:T(8,128)(2,1)S(1)} %copy-done, bf16[64,2048]{1,0:T(8,128)(2,1)S(1)} %get-tuple-element.15, bf16[64,2048]{1,0:T(8,128)(2,1)S(1)} %get-tuple-element.16), kind=kOutput, calls=%fused_computation.46 | convolution fusion | flops 1074790400 | bytes 9961472 | tf_op jit(solution)/shard_map/dot_general | solution.py:64
  69.1 2.9 %convolution_convert_fusion.1 = bf16[128,2048]{1,0:T(8,128)(2,1)S(1)} fusion(bf16[2048,2048]{1,0:T(8,128)(2,1)S(1)} %copy-done, bf16[64,2048]{1,0:T(8,128)(2,1)S(1)} %get-tuple-element.23, bf16[64,2048]{1,0:T(8,128)(2,1)S(1)} %get-tuple-element.24), kind=kOutput, calls=%fused_computation.1 | convolution fusion | flops 1075052544 | bytes 9437184 | tf_op jit(solution)/shard_map/dot_general | solution.py:64
  72.0 0.6 collective-permute-start.19
  72.6 2.9 %fusion.14 = f32[128,2048]{1,0:T(8,128)S(1)} fusion(bf16[2048,2048]{1,0:T(8,128)(2,1)S(1)} %copy-done, bf16[64,2048]{1,0:T(8,128)(2,1)S(1)} %get-tuple-element.22, bf16[64,2048]{1,0:T(8,128)(2,1)S(1)} %get-tuple-element.21), kind=kOutput, calls=%fused_computation.38 | convolution fusion | flops 1074790400 | bytes 9961472 | tf_op jit(solution)/shard_map/dot_general | solution.py:64
  75.5 0.1 convert_add_fusion.3
  75.6 2.8 %collective-permute-start.7 = (bf16[64,2048]{1,0:T(8,128)(2,1)S(1)}, bf16[64,2048]{1,0:T(8,128)(2,1)S(1)}, u32[]{:S(2)}, u32[]{:S(2)}) collective-permute-start(bf16[64,2048]{1,0:T(8,128)(2,1)S(1)} %slice.147), channel_id=1, source_target_pairs={{0,3},{1,2},{2,1},{3,0},{4,7},{5,6},{6,5},{7,4},{8,9},{9,8},{10,11... | collective-permute-start | bytes 786440 | tf_op jit(solution)/shard_map/ppermute | solution.py:18
  78.5 0.1 convert_add_fusion.2
  78.6 0.6 collective-permute-start.16
  79.2 0.1 convert_add_fusion
  79.4 2.8 %collective-permute-start.23 = (bf16[64,2048]{1,0:T(8,128)(2,1)S(1)}, bf16[64,2048]{1,0:T(8,128)(2,1)S(1)}, u32[]{:S(2)}, u32[]{:S(2)}) collective-permute-start(bf16[64,2048]{1,0:T(8,128)(2,1)S(1)} %slice.144), channel_id=1, source_target_pairs={{0,3},{1,2},{2,1},{3,0},{4,7},{5,6},{6,5},{7,4},{8,9},{9,8},{10,11... | collective-permute-start | bytes 786440 | tf_op jit(solution)/shard_map/ppermute | solution.py:18
  82.2 0.1 collective-permute-done.19
  82.3 0.1 convert_add_fusion.1
  82.4 1.5 %collective-permute-start.20 = (bf16[64,2048]{1,0:T(8,128)(2,1)S(1)}, bf16[64,2048]{1,0:T(8,128)(2,1)S(1)}, u32[]{:S(2)}, u32[]{:S(2)}) collective-permute-start(bf16[64,2048]{1,0:T(8,128)(2,1)S(1)} %slice.145), channel_id=1, source_target_pairs={{0,3},{1,2},{2,1},{3,0},{4,7},{5,6},{6,5},{7,4},{8,9},{9,8},{10,11... | collective-permute-start | bytes 786440 | tf_op jit(solution)/shard_map/ppermute | solution.py:18
  84.0 2.2 %collective-permute-done.7 = bf16[64,2048]{1,0:T(8,128)(2,1)S(1)} collective-permute-done((bf16[64,2048]{1,0:T(8,128)(2,1)S(1)}, bf16[64,2048]{1,0:T(8,128)(2,1)S(1)}, u32[]{:S(2)}, u32[]{:S(2)}) %collective-permute-start.7) | collective-permute-done | bytes 262176 | tf_op jit(solution)/shard_map/ppermute | solution.py:18
  86.2 3.0 %collective-permute-done.16 = bf16[64,2048]{1,0:T(8,128)(2,1)S(1)} collective-permute-done((bf16[64,2048]{1,0:T(8,128)(2,1)S(1)}, bf16[64,2048]{1,0:T(8,128)(2,1)S(1)}, u32[]{:S(2)}, u32[]{:S(2)}) %collective-permute-start.16) | collective-permute-done | bytes 262176 | tf_op jit(solution)/shard_map/ppermute | solution.py:18
  89.2 0.1 select_convert_fusion.1
  89.3 1.4 %collective-permute-start.17 = (bf16[64,2048]{1,0:T(8,128)(2,1)S(1)}, bf16[64,2048]{1,0:T(8,128)(2,1)S(1)}, u32[]{:S(2)}, u32[]{:S(2)}) collective-permute-start(bf16[64,2048]{1,0:T(8,128)(2,1)S(1)} %select_convert_fusion.1), channel_id=1, source_target_pairs={{0,4},{1,5},{2,6},{3,7},{4,0},{5,1},{6,2},{7,3},{8,12},{9,13},{10,... | collective-permute-start | bytes 786440 | tf_op jit(solution)/shard_map/ppermute | solution.py:18
  90.7 1.3 %collective-permute-done.23 = bf16[64,2048]{1,0:T(8,128)(2,1)S(1)} collective-permute-done((bf16[64,2048]{1,0:T(8,128)(2,1)S(1)}, bf16[64,2048]{1,0:T(8,128)(2,1)S(1)}, u32[]{:S(2)}, u32[]{:S(2)}) %collective-permute-start.23) | collective-permute-done | bytes 262176 | tf_op jit(solution)/shard_map/ppermute | solution.py:18
  92.0 2.8 %collective-permute-done.20 = bf16[64,2048]{1,0:T(8,128)(2,1)S(1)} collective-permute-done((bf16[64,2048]{1,0:T(8,128)(2,1)S(1)}, bf16[64,2048]{1,0:T(8,128)(2,1)S(1)}, u32[]{:S(2)}, u32[]{:S(2)}) %collective-permute-start.20) | collective-permute-done | bytes 262176 | tf_op jit(solution)/shard_map/ppermute | solution.py:18
  94.8 0.1 select_convert_fusion
  94.9 1.4 %collective-permute-start.24 = (bf16[64,2048]{1,0:T(8,128)(2,1)S(1)}, bf16[64,2048]{1,0:T(8,128)(2,1)S(1)}, u32[]{:S(2)}, u32[]{:S(2)}) collective-permute-start(bf16[64,2048]{1,0:T(8,128)(2,1)S(1)} %select_convert_fusion), channel_id=1, source_target_pairs={{0,4},{1,5},{2,6},{3,7},{4,0},{5,1},{6,2},{7,3},{8,12},{9,13},{10,... | collective-permute-start | bytes 786440 | tf_op jit(solution)/shard_map/ppermute | solution.py:18
  96.3 0.1 convert_add_fusion.5
  96.5 5.0 %collective-permute-done.24 = bf16[64,2048]{1,0:T(8,128)(2,1)S(1)} collective-permute-done((bf16[64,2048]{1,0:T(8,128)(2,1)S(1)}, bf16[64,2048]{1,0:T(8,128)(2,1)S(1)}, u32[]{:S(2)}, u32[]{:S(2)}) %collective-permute-start.24) | collective-permute-done | bytes 262176 | tf_op jit(solution)/shard_map/ppermute | solution.py:18
  101.4 0.1 convert_add_fusion.4
  101.5 1.1 %maximum_select_fusion = f32[128,2048]{1,0:T(8,128)} fusion(f32[64,2048]{1,0:T(8,128)S(1)} %convert_add_fusion.4, f32[64,2048]{1,0:T(8,128)S(1)} %convert_add_fusion.5, pred[]{:T(512)S(6)} %eq.187), kind=kLoop, calls=%fused_computation.10 | loop fusion | flops 786432 | bytes 2097153 | tf_op jit(solution)/shard_map/jit(_where)/select_n | solution.py:140
  (39 shorter events, 0.7 us)
Async XLA Ops:
  5.1 6.8 %collective-permute-start.8 = (bf16[32,2048]{1,0:T(8,128)(2,1)S(1)}, bf16[32,2048]{1,0:T(8,128)(2,1)S(1)}, u32[]{:S(2)}, u32[]{:S(2)}) collective-permute-start(bf16[32,2048]{1,0:T(8,128)(2,1)S(1)} %pad_maximum_fusion.6), channel_id=1, source_target_pairs={{0,128},{1,129},{2,130},{3,131},{4,132},{5,133},{6,134},{7,135},{8... | collective-permute-start | bytes 393224 | tf_op jit(solution)/shard_map/ppermute | solution.py:18
  7.2 4.7 %collective-permute-start = (bf16[32,2048]{1,0:T(8,128)(2,1)S(1)}, bf16[32,2048]{1,0:T(8,128)(2,1)S(1)}, u32[]{:S(2)}, u32[]{:S(2)}) collective-permute-start(bf16[32,2048]{1,0:T(8,128)(2,1)S(1)} %pad_maximum_fusion.6), channel_id=1, source_target_pairs={{0,8},{1,9},{2,10},{3,11},{4,12},{5,13},{6,14},{7,15},{8,0},{9,1},... | collective-permute-start | bytes 393224 | tf_op jit(solution)/shard_map/ppermute | solution.py:18
  11.9 2.1 %collective-permute-start.9 = (bf16[32,2048]{1,0:T(8,128)(2,1)S(1)}, bf16[32,2048]{1,0:T(8,128)(2,1)S(1)}, u32[]{:S(2)}, u32[]{:S(2)}) collective-permute-start(bf16[32,2048]{1,0:T(8,128)(2,1)S(1)} %collective-permute-done.8), channel_id=1, source_target_pairs={{0,8},{1,9},{2,10},{3,11},{4,12},{5,13},{6,14},{7,15},{8,0},{9,1},... | collective-permute-start | bytes 393224 | tf_op jit(solution)/shard_map/ppermute | solution.py:18
  11.9 10.3 %collective-permute-start.1 = (bf16[64,2048]{1,0:T(8,128)(2,1)S(1)}, bf16[64,2048]{1,0:T(8,128)(2,1)S(1)}, u32[]{:S(2)}, u32[]{:S(2)}) collective-permute-start(bf16[64,2048]{1,0:T(8,128)(2,1)S(1)} %maximum_select_fusion.1), channel_id=1, source_target_pairs={{0,16},{1,17},{2,18},{3,19},{4,20},{5,21},{6,22},{7,23},{8,120},{9... | collective-permute-start | bytes 786440 | tf_op jit(solution)/shard_map/ppermute | solution.py:18
  14.0 11.0 %collective-permute-start.10 = (bf16[64,2048]{1,0:T(8,128)(2,1)S(1)}, bf16[64,2048]{1,0:T(8,128)(2,1)S(1)}, u32[]{:S(2)}, u32[]{:S(2)}) collective-permute-start(bf16[64,2048]{1,0:T(8,128)(2,1)S(1)} %maximum_select_fusion.3), channel_id=1, source_target_pairs={{0,16},{1,17},{2,18},{3,19},{4,20},{5,21},{6,22},{7,23},{8,120},{9... | collective-permute-start | bytes 786440 | tf_op jit(solution)/shard_map/ppermute | solution.py:18
  22.2 7.6 %collective-permute-start.2 = (bf16[64,2048]{1,0:T(8,128)(2,1)S(1)}, bf16[64,2048]{1,0:T(8,128)(2,1)S(1)}, u32[]{:S(2)}, u32[]{:S(2)}) collective-permute-start(bf16[64,2048]{1,0:T(8,128)(2,1)S(1)} %collective-permute-done.1), channel_id=1, source_target_pairs={{0,16},{1,17},{2,18},{3,19},{4,20},{5,21},{6,22},{7,23},{8,120},{9... | collective-permute-start | bytes 786440 | tf_op jit(solution)/shard_map/ppermute | solution.py:18
  22.2 24.8 %copy-start = (bf16[2048,2048]{1,0:T(8,128)(2,1)S(1)}, bf16[2048,2048]{1,0:T(8,128)(2,1)}, u32[]{:S(2)}) copy-start(bf16[2048,2048]{1,0:T(8,128)(2,1)} %param.3) | copy-start | bytes 25165828
  25.0 7.6 %collective-permute-start.11 = (bf16[64,2048]{1,0:T(8,128)(2,1)S(1)}, bf16[64,2048]{1,0:T(8,128)(2,1)S(1)}, u32[]{:S(2)}, u32[]{:S(2)}) collective-permute-start(bf16[64,2048]{1,0:T(8,128)(2,1)S(1)} %collective-permute-done.10), channel_id=1, source_target_pairs={{0,16},{1,17},{2,18},{3,19},{4,20},{5,21},{6,22},{7,23},{8,120},{9... | collective-permute-start | bytes 786440 | tf_op jit(solution)/shard_map/ppermute | solution.py:18
  29.8 7.6 %collective-permute-start.3 = (bf16[64,2048]{1,0:T(8,128)(2,1)S(1)}, bf16[64,2048]{1,0:T(8,128)(2,1)S(1)}, u32[]{:S(2)}, u32[]{:S(2)}) collective-permute-start(bf16[64,2048]{1,0:T(8,128)(2,1)S(1)} %collective-permute-done.2), channel_id=1, source_target_pairs={{0,16},{1,17},{2,18},{3,19},{4,20},{5,21},{6,22},{7,23},{8,120},{9... | collective-permute-start | bytes 786440 | tf_op jit(solution)/shard_map/ppermute | solution.py:18
  32.6 7.6 %collective-permute-start.12 = (bf16[64,2048]{1,0:T(8,128)(2,1)S(1)}, bf16[64,2048]{1,0:T(8,128)(2,1)S(1)}, u32[]{:S(2)}, u32[]{:S(2)}) collective-permute-start(bf16[64,2048]{1,0:T(8,128)(2,1)S(1)} %collective-permute-done.11), channel_id=1, source_target_pairs={{0,16},{1,17},{2,18},{3,19},{4,20},{5,21},{6,22},{7,23},{8,120},{9... | collective-permute-start | bytes 786440 | tf_op jit(solution)/shard_map/ppermute | solution.py:18
  37.4 6.3 %collective-permute-start.4 = (bf16[32,2048]{1,0:T(8,128)(2,1)S(1)}, bf16[32,2048]{1,0:T(8,128)(2,1)S(1)}, u32[]{:S(2)}, u32[]{:S(2)}) collective-permute-start(bf16[32,2048]{1,0:T(8,128)(2,1)S(1)} %constant_dynamic-slice_fusion.17), channel_id=1, source_target_pairs={{0,16},{1,17},{2,18},{3,19},{4,20},{5,21},{6,22},{7,23},{8,120},{9... | collective-permute-start | bytes 393224 | tf_op jit(solution)/shard_map/ppermute | solution.py:18
  37.6 16.9 %collective-permute-start.18 = (bf16[128,2048]{1,0:T(8,128)(2,1)S(1)}, bf16[128,2048]{1,0:T(8,128)(2,1)S(1)}, u32[]{:S(2)}, u32[]{:S(2)}) collective-permute-start(bf16[128,2048]{1,0:T(8,128)(2,1)S(1)} %pad_maximum_fusion.2), channel_id=1, source_target_pairs={{0,8},{1,9},{2,10},{3,11},{4,12},{5,13},{6,14},{7,15},{8,0},{9,1},... | collective-permute-start | bytes 1572872 | tf_op jit(solution)/shard_map/ppermute | solution.py:18
  40.2 6.3 %collective-permute-start.13 = (bf16[32,2048]{1,0:T(8,128)(2,1)S(1)}, bf16[32,2048]{1,0:T(8,128)(2,1)S(1)}, u32[]{:S(2)}, u32[]{:S(2)}) collective-permute-start(bf16[32,2048]{1,0:T(8,128)(2,1)S(1)} %constant_dynamic-slice_fusion.12), channel_id=1, source_target_pairs={{0,16},{1,17},{2,18},{3,19},{4,20},{5,21},{6,22},{7,23},{8,120},{9... | collective-permute-start | bytes 393224 | tf_op jit(solution)/shard_map/ppermute | solution.py:18
  43.7 3.1 %collective-permute-start.5 = (bf16[96,2048]{1,0:T(8,128)(2,1)S(1)}, bf16[96,2048]{1,0:T(8,128)(2,1)S(1)}, u32[]{:S(2)}, u32[]{:S(2)}) collective-permute-start(bf16[96,2048]{1,0:T(8,128)(2,1)S(1)} %pad_maximum_fusion.4), channel_id=1, source_target_pairs={{0,8},{1,9},{2,10},{3,11},{4,12},{5,13},{6,14},{7,15},{8,0},{9,1},... | collective-permute-start | bytes 1179656 | tf_op jit(solution)/shard_map/ppermute | solution.py:18
  43.9 17.3 %collective-permute-start.21 = (bf16[128,2048]{1,0:T(8,128)(2,1)S(1)}, bf16[128,2048]{1,0:T(8,128)(2,1)S(1)}, u32[]{:S(2)}, u32[]{:S(2)}) collective-permute-start(bf16[128,2048]{1,0:T(8,128)(2,1)S(1)} %pad_maximum_fusion.3), channel_id=1, source_target_pairs={{0,8},{1,9},{2,10},{3,11},{4,12},{5,13},{6,14},{7,15},{8,0},{9,1},... | collective-permute-start | bytes 1572872 | tf_op jit(solution)/shard_map/ppermute | solution.py:18
  46.5 8.0 %collective-permute-start.14 = (bf16[96,2048]{1,0:T(8,128)(2,1)S(1)}, bf16[96,2048]{1,0:T(8,128)(2,1)S(1)}, u32[]{:S(2)}, u32[]{:S(2)}) collective-permute-start(bf16[96,2048]{1,0:T(8,128)(2,1)S(1)} %pad_maximum_fusion.5), channel_id=1, source_target_pairs={{0,8},{1,9},{2,10},{3,11},{4,12},{5,13},{6,14},{7,15},{8,0},{9,1},... | collective-permute-start | bytes 1179656 | tf_op jit(solution)/shard_map/ppermute | solution.py:18
  50.0 25.5 %collective-permute-start.6 = (bf16[128,2048]{1,0:T(8,128)(2,1)S(1)}, bf16[128,2048]{1,0:T(8,128)(2,1)S(1)}, u32[]{:S(2)}, u32[]{:S(2)}) collective-permute-start(bf16[128,2048]{1,0:T(8,128)(2,1)S(1)} %convolution_convert_fusion.3), channel_id=1, source_target_pairs={{0,1},{1,0},{2,3},{3,2},{4,5},{5,4},{6,7},{7,6},{8,11},{9,10},{10,... | collective-permute-start | bytes 1572872 | tf_op jit(solution)/shard_map/ppermute | solution.py:18
  57.7 20.8 %collective-permute-start.15 = (bf16[128,2048]{1,0:T(8,128)(2,1)S(1)}, bf16[128,2048]{1,0:T(8,128)(2,1)S(1)}, u32[]{:S(2)}, u32[]{:S(2)}) collective-permute-start(bf16[128,2048]{1,0:T(8,128)(2,1)S(1)} %convolution_convert_fusion.2), channel_id=1, source_target_pairs={{0,1},{1,0},{2,3},{3,2},{4,5},{5,4},{6,7},{7,6},{8,11},{9,10},{10,... | collective-permute-start | bytes 1572872 | tf_op jit(solution)/shard_map/ppermute | solution.py:18
  64.4 14.8 %collective-permute-start.22 = (bf16[128,2048]{1,0:T(8,128)(2,1)S(1)}, bf16[128,2048]{1,0:T(8,128)(2,1)S(1)}, u32[]{:S(2)}, u32[]{:S(2)}) collective-permute-start(bf16[128,2048]{1,0:T(8,128)(2,1)S(1)} %convolution_convert_fusion), channel_id=1, source_target_pairs={{0,1},{1,0},{2,3},{3,2},{4,5},{5,4},{6,7},{7,6},{8,11},{9,10},{10,... | collective-permute-start | bytes 1572872 | tf_op jit(solution)/shard_map/ppermute | solution.py:18
  72.0 10.3 %collective-permute-start.19 = (bf16[128,2048]{1,0:T(8,128)(2,1)S(1)}, bf16[128,2048]{1,0:T(8,128)(2,1)S(1)}, u32[]{:S(2)}, u32[]{:S(2)}) collective-permute-start(bf16[128,2048]{1,0:T(8,128)(2,1)S(1)} %convolution_convert_fusion.1), channel_id=1, source_target_pairs={{0,1},{1,0},{2,3},{3,2},{4,5},{5,4},{6,7},{7,6},{8,11},{9,10},{10,... | collective-permute-start | bytes 1572872 | tf_op jit(solution)/shard_map/ppermute | solution.py:18
  75.6 10.5 %collective-permute-start.7 = (bf16[64,2048]{1,0:T(8,128)(2,1)S(1)}, bf16[64,2048]{1,0:T(8,128)(2,1)S(1)}, u32[]{:S(2)}, u32[]{:S(2)}) collective-permute-start(bf16[64,2048]{1,0:T(8,128)(2,1)S(1)} %slice.147), channel_id=1, source_target_pairs={{0,3},{1,2},{2,1},{3,0},{4,7},{5,6},{6,5},{7,4},{8,9},{9,8},{10,11... | collective-permute-start | bytes 786440 | tf_op jit(solution)/shard_map/ppermute | solution.py:18
  78.6 10.6 %collective-permute-start.16 = (bf16[64,2048]{1,0:T(8,128)(2,1)S(1)}, bf16[64,2048]{1,0:T(8,128)(2,1)S(1)}, u32[]{:S(2)}, u32[]{:S(2)}) collective-permute-start(bf16[64,2048]{1,0:T(8,128)(2,1)S(1)} %slice.146), channel_id=1, source_target_pairs={{0,3},{1,2},{2,1},{3,0},{4,7},{5,6},{6,5},{7,4},{8,9},{9,8},{10,11... | collective-permute-start | bytes 786440 | tf_op jit(solution)/shard_map/ppermute | solution.py:18
  79.4 12.7 %collective-permute-start.23 = (bf16[64,2048]{1,0:T(8,128)(2,1)S(1)}, bf16[64,2048]{1,0:T(8,128)(2,1)S(1)}, u32[]{:S(2)}, u32[]{:S(2)}) collective-permute-start(bf16[64,2048]{1,0:T(8,128)(2,1)S(1)} %slice.144), channel_id=1, source_target_pairs={{0,3},{1,2},{2,1},{3,0},{4,7},{5,6},{6,5},{7,4},{8,9},{9,8},{10,11... | collective-permute-start | bytes 786440 | tf_op jit(solution)/shard_map/ppermute | solution.py:18
  82.4 12.4 %collective-permute-start.20 = (bf16[64,2048]{1,0:T(8,128)(2,1)S(1)}, bf16[64,2048]{1,0:T(8,128)(2,1)S(1)}, u32[]{:S(2)}, u32[]{:S(2)}) collective-permute-start(bf16[64,2048]{1,0:T(8,128)(2,1)S(1)} %slice.145), channel_id=1, source_target_pairs={{0,3},{1,2},{2,1},{3,0},{4,7},{5,6},{6,5},{7,4},{8,9},{9,8},{10,11... | collective-permute-start | bytes 786440 | tf_op jit(solution)/shard_map/ppermute | solution.py:18
  89.3 7.0 %collective-permute-start.17 = (bf16[64,2048]{1,0:T(8,128)(2,1)S(1)}, bf16[64,2048]{1,0:T(8,128)(2,1)S(1)}, u32[]{:S(2)}, u32[]{:S(2)}) collective-permute-start(bf16[64,2048]{1,0:T(8,128)(2,1)S(1)} %select_convert_fusion.1), channel_id=1, source_target_pairs={{0,4},{1,5},{2,6},{3,7},{4,0},{5,1},{6,2},{7,3},{8,12},{9,13},{10,... | collective-permute-start | bytes 786440 | tf_op jit(solution)/shard_map/ppermute | solution.py:18
  94.9 6.5 %collective-permute-start.24 = (bf16[64,2048]{1,0:T(8,128)(2,1)S(1)}, bf16[64,2048]{1,0:T(8,128)(2,1)S(1)}, u32[]{:S(2)}, u32[]{:S(2)}) collective-permute-start(bf16[64,2048]{1,0:T(8,128)(2,1)S(1)} %select_convert_fusion), channel_id=1, source_target_pairs={{0,4},{1,5},{2,6},{3,7},{4,0},{5,1},{6,2},{7,3},{8,12},{9,13},{10,... | collective-permute-start | bytes 786440 | tf_op jit(solution)/shard_map/ppermute | solution.py:18

commit v2 on v1

v2 whole, which is shorter than its diff:
```python
import itertools

import jax
import jax.numpy as jnp
from jax import lax
from jax.sharding import Mesh, PartitionSpec as P

NAMES = ("h", "z", "c", "l", "x")
SIZES = (2, 8, 2, 2, 4)


def move(value, target):
    pairs = []
    for place in itertools.product(*map(range, SIZES)):
        to = target(*place)
        if to is not None:
            pairs.append((flat(place), flat(to)))
    return lax.ppermute(value, NAMES, pairs)


def flat(place):
    index = 0
    for at, size in zip(place, SIZES, strict=True):
        index = index * size + at % size
    return index


def other_core(value):
    return move(value, lambda h, z, c, l, x: (h, z, 1 - c, l, x))


def other_half(value):
    return move(value, lambda h, z, c, l, x: (1 - h, z, c, l, x))


def other_run(value):
    return move(value, lambda h, z, c, l, x: (h, z, c, 1 - l, x))


def along_z_twice(value):
    return move(value, lambda h, z, c, l, x: (h, z + (2 if c == 0 else -2), c, l, x))


def along_z(value):
    return move(value, lambda h, z, c, l, x: (h, z + (1 if c == 0 else -1), c, l, x))


def first_x(value):
    return move(value, lambda h, z, c, l, x: (h, z, c, l, x ^ (1 if c == 0 else 3)))


def second_x(value):
    return move(value, lambda h, z, c, l, x: (h, z, c, l, x ^ (3 if c == 0 else 1)))


def prepare(rows, blocks):
    count = rows.shape[0]
    split = rows.reshape(count, blocks.shape[0], blocks.shape[1])
    mixed = jnp.einsum("rbi,bij->rbj", split, blocks, preferred_element_type=jnp.float32)
    return mixed.reshape(count, -1).astype(jnp.bfloat16)


def score_rows(ready, train_grads):
    return lax.dot_general(
        ready, train_grads, (((1,), (1,)), ((), ())), preferred_element_type=jnp.float32
    ).astype(jnp.bfloat16)


def both_cores(c, mine, theirs):
    return jnp.where(
        c == 0, jnp.concatenate([mine, theirs]), jnp.concatenate([theirs, mine])
    )


def together(*values):
    return lax.optimization_barrier(values)


def on_device(train_grads, query_grads, precond):
    h, z, c, l, x = (lax.axis_index(name) for name in NAMES)
    m1 = jnp.where(c == 0, 1, 3)
    m2 = jnp.where(c == 0, 3, 1)

    mine = prepare(query_grads, precond)
    theirs = other_core(mine)
    plane = both_cores(c, mine, theirs)
    rows = plane.shape[0]
    part = rows // 2
    own_rows = lambda held: lax.dynamic_slice_in_dim(held, c * part, part)

    def scores(place, cuts, *blocks):
        held = jnp.concatenate(blocks)
        size = rows // cuts
        picked = [
            lax.dynamic_slice_in_dim(held, place(owner) * rows + cut * size, size)
            for cut in range(cuts)
            for owner in (x ^ m1, x ^ 2, x, x ^ m2)
        ]
        return score_rows(jnp.concatenate(picked), train_grads)

    def odd_place(owner):
        step = (2 * owner + 1 - z % 2 - z) % 8
        near = (step == 1) | (step == 7)
        above = step < 4
        own = above == (c == 1)
        return jnp.where(own, 0, 1) + jnp.where(near, 0, 2)

    def even_place(owner):
        step = (2 * owner + z % 2 - z) % 8
        own = (step == 2) == (c == 1)
        return jnp.where(step == 0, 0, jnp.where(step == 4, 3, jnp.where(own, 1, 2)))

    mine, plane = together(mine, plane)
    across, o1 = together(other_half(mine), along_z(plane))
    o2 = along_z(o1)
    a0 = both_cores(c, across, other_core(across))
    a1 = along_z(a0)
    a2 = along_z_twice(a0)
    o3 = along_z(o2)
    a3 = along_z(a2)
    a4 = along_z_twice(own_rows(a2))
    o4 = along_z(own_rows(o3))
    t1, t2, t3 = map(other_core, (o1, o2, o3))
    odd = scores(odd_place, 1, o1, t1, o3, t3)
    odd_come, odd = first_x(odd[: 2 * rows]), odd[2 * rows :]
    a3, a4, o4, odd = together(a3, a4, o4, odd)
    t4 = other_core(o4)
    even = scores(even_place, 2, plane, o2, t2, both_cores(c, o4, t4))
    u1, u2, u3, u4 = map(other_core, (a1, a2, a3, a4))
    odd_across = scores(odd_place, 1, a1, u1, a3, u3)
    even_across = scores(even_place, 2, a0, a2, u2, both_cores(c, a4, u4))

    wide = lambda value: value.astype(jnp.float32)

    def pass_on(total, sizes):
        parts, at = [], 0
        for size in sizes:
            parts.append((total[at : at + size], total[at + size : at + 2 * size]))
            at += 2 * size
        come = second_x(jnp.concatenate([sent for _, sent in parts]).astype(jnp.bfloat16))
        sums, at = [], 0
        for (kept, _), size in zip(parts, sizes, strict=True):
            sums.append(kept + wide(come[at : at + size]))
            at += size
        return sums

    def over_runs(own, across):
        sent = jnp.where(l == h, across, own).astype(jnp.bfloat16)
        kept = jnp.where(l == h, own, across)
        return wide(kept) + wide(other_run(sent))

    half = 2 * rows
    (odd,) = pass_on(wide(odd) + wide(odd_come), [rows])
    second = over_runs(even[half:], even_across[half:])
    second_come = first_x(second[:rows].astype(jnp.bfloat16))
    come = first_x(odd_across[:half])
    (odd_across,) = pass_on(wide(odd_across[half:]) + wide(come), [rows])
    come = first_x(jnp.concatenate([even[:rows], even_across[:rows]]))
    kept = jnp.concatenate([even[rows:half], even_across[rows:half]])
    even, even_across = pass_on(wide(kept) + wide(come), [part, part])
    (second,) = pass_on(second[rows:] + wide(second_come), [part])

    odd = over_runs(odd, odd_across)
    even = jnp.concatenate([over_runs(even, even_across), second])
    return jnp.where(z % 2 == 0, jnp.concatenate([even, odd]), jnp.concatenate([odd, even]))


def solution(mesh):
    wide = Mesh(mesh.devices.reshape(SIZES), NAMES)
    ex, lb = NAMES[:3], NAMES[3:]
    placed = (P(ex, lb), P(ex, lb), P(lb, None, None))
    return jax.shard_map(
        on_device, mesh=wide, in_specs=placed, out_specs=P(lb, ex), check_vma=False
    )
```

time: 103 us -> 93.5 us (0.908)
  matrix products: 28.1 us -> 14.7 us
  local copies, waits for them, and re-layouts: 0.78 us -> 2.69 us
  waiting for transfers between devices: 48.4 us -> 49.5 us
    dot_general x8 -> x4, matrix products: 23 us -> 13.3 us  [score_rows(): lax.dot_general(ready, train_grads, (((1,), (1,)), ((), ())), preferred_e...]
    dot_general x4 -> x1, matrix products: 5.02 us -> 1.33 us  [prepare(): jnp.einsum('rbi,bij->rbj', split, blocks, preferred_element_type=jnp.floa...]
    unnamed x6 -> x26, local copies, waits for them, and re-layouts: 0.08 us -> 1.98 us
    ppermute x25 -> x30, waiting for transfers between devices: 48.4 us -> 49.5 us  [move(): return lax.ppermute(value, NAMES, pairs)]
    ppermute x25 -> x30, starting transfers between devices: 22.5 us -> 23.3 us  [move(): return lax.ppermute(value, NAMES, pairs)]
  transfers between devices with their start and end apart: 25 -> 30, of which waited for: 15 -> 16; matrix products, arithmetic and copies ran while one was open for 24% -> 17% of each run, Pallas kernels for 0% -> 0%
where the time goes in v2:
time: 93.5 us; the launch traced here: 93.4 us
  waiting for transfers between devices  49.5 us (53%)
  starting transfers between devices  23.3 us (25%)
  matrix products  14.7 us (16%)
  local copies, waits for them, and re-layouts  2.69 us (3%)
  other arithmetic  2.64 us (3%)
    ppermute x30, waiting for transfers between devices, move(): return lax.ppermute(value, NAMES, pairs)  49.5 us
    ppermute x30, starting transfers between devices, move(): return lax.ppermute(value, NAMES, pairs)  23.3 us
    dot_general x4, matrix products, score_rows(): lax.dot_general(ready, train_grads, (((1,), (1,)), ((), ())), preferred_e...  13.3 us
    unnamed x26, local copies, waits for them, and re-layouts  1.98 us
  transfers between devices with their start and end apart: 30, of which 16 were waited for; matrix products, arithmetic and copies ran while one was open for 17% of the time, Pallas kernels for 0%

profile of v2, /device:TPU:16, one launch (start us, length us, event | category | flops | bytes accessed | tf_op | source)
XLA Modules:
  0.0 93.4 jit_solution(10952300950684282237)
XLA Ops:
  0.0 1.6 %copy-done = bf16[4,512,512]{2,1,0:T(8,128)(2,1)S(1)} copy-done((bf16[4,512,512]{2,1,0:T(8,128)(2,1)S(1)}, bf16[4,512,512]{2,1,0:T(8,128)(2,1)}, u32[]{:S(2)}) %copy-start) | copy-done | bytes 2097176
  1.6 1.3 %fusion = bf16[4,4,8,512]{3,2,1,0:T(8,128)(2,1)S(1)} fusion(bf16[4,512,512]{2,1,0:T(8,128)(2,1)S(1)} %copy-done, bf16[4,4,8,512]{3,2,1,0:T(8,128)(2,1)} %bitcast.18), kind=kOutput, calls=%fused_computation.5 | convolution fusion | flops 67174400 | bytes 2359296 | tf_op jit(solution)/shard_map/rbi,bij->rbj/dot_general | solution.py:59
  3.0 0.1 collective-permute-start
  3.1 1.3 %collective-permute-done = bf16[32,2048]{1,0:T(8,128)(2,1)S(1)} collective-permute-done((bf16[32,2048]{1,0:T(8,128)(2,1)S(1)}, bf16[32,2048]{1,0:T(8,128)(2,1)S(1)}, u32[]{:S(2)}, u32[]{:S(2)}) %collective-permute-start) | collective-permute-done | bytes 131104 | tf_op jit(solution)/shard_map/ppermute | solution.py:18
  4.4 2.0 %collective-permute-start.2 = (bf16[64,2048]{1,0:T(8,128)(2,1)S(1)}, bf16[64,2048]{1,0:T(8,128)(2,1)S(1)}, u32[]{:S(2)}, u32[]{:S(2)}) collective-permute-start(bf16[64,2048]{1,0:T(8,128)(2,1)S(1)} %maximum_select_fusion.1), channel_id=1, source_target_pairs={{0,16},{1,17},{2,18},{3,19},{4,20},{5,21},{6,22},{7,23},{8,120},{9... | collective-permute-start | bytes 786440 | tf_op jit(solution)/shard_map/ppermute | solution.py:18
  6.4 0.3 collective-permute-start.1
  6.8 6.1 %collective-permute-done.1 = bf16[32,2048]{1,0:T(8,128)(2,1)S(1)} collective-permute-done((bf16[32,2048]{1,0:T(8,128)(2,1)S(1)}, bf16[32,2048]{1,0:T(8,128)(2,1)S(1)}, u32[]{:S(2)}, u32[]{:S(2)}) %collective-permute-start.1) | collective-permute-done | bytes 131104 | tf_op jit(solution)/shard_map/ppermute | solution.py:18
  12.9 1.8 %collective-permute-done.2 = bf16[64,2048]{1,0:T(8,128)(2,1)S(1)} collective-permute-done((bf16[64,2048]{1,0:T(8,128)(2,1)S(1)}, bf16[64,2048]{1,0:T(8,128)(2,1)S(1)}, u32[]{:S(2)}, u32[]{:S(2)}) %collective-permute-start.2) | collective-permute-done | bytes 262176 | tf_op jit(solution)/shard_map/ppermute | solution.py:18
  14.7 0.8 collective-permute-start.5
  15.6 1.0 %collective-permute-done.5 = bf16[32,2048]{1,0:T(8,128)(2,1)S(1)} collective-permute-done((bf16[32,2048]{1,0:T(8,128)(2,1)S(1)}, bf16[32,2048]{1,0:T(8,128)(2,1)S(1)}, u32[]{:S(2)}, u32[]{:S(2)}) %collective-permute-start.5) | collective-permute-done | bytes 131104 | tf_op jit(solution)/shard_map/ppermute | solution.py:18
  16.6 3.3 %collective-permute-start.6 = (bf16[64,2048]{1,0:T(8,128)(2,1)S(1)}, bf16[64,2048]{1,0:T(8,128)(2,1)S(1)}, u32[]{:S(2)}, u32[]{:S(2)}) collective-permute-start(bf16[64,2048]{1,0:T(8,128)(2,1)S(1)} %maximum_select_fusion.2), channel_id=1, source_target_pairs={{0,32},{1,33},{2,34},{3,35},{4,36},{5,37},{6,38},{7,39},{8,104},{9... | collective-permute-start | bytes 786440 | tf_op jit(solution)/shard_map/ppermute | solution.py:18
  20.0 1.2 %collective-permute-start.24 = (bf16[64,2048]{1,0:T(8,128)(2,1)S(1)}, bf16[64,2048]{1,0:T(8,128)(2,1)S(1)}, u32[]{:S(2)}, u32[]{:S(2)}) collective-permute-start(bf16[64,2048]{1,0:T(8,128)(2,1)S(1)} %maximum_select_fusion.2), channel_id=1, source_target_pairs={{0,16},{1,17},{2,18},{3,19},{4,20},{5,21},{6,22},{7,23},{8,120},{9... | collective-permute-start | bytes 786440 | tf_op jit(solution)/shard_map/ppermute | solution.py:18
  21.2 2.0 %collective-permute-done.3 = bf16[64,2048]{1,0:T(8,128)(2,1)S(1)} collective-permute-done((bf16[64,2048]{1,0:T(8,128)(2,1)S(1)}, bf16[64,2048]{1,0:T(8,128)(2,1)S(1)}, u32[]{:S(2)}, u32[]{:S(2)}) %collective-permute-start.3) | collective-permute-done | bytes 262176 | tf_op jit(solution)/shard_map/ppermute | solution.py:18
  23.2 2.0 %collective-permute-start.4 = (bf16[64,2048]{1,0:T(8,128)(2,1)S(1)}, bf16[64,2048]{1,0:T(8,128)(2,1)S(1)}, u32[]{:S(2)}, u32[]{:S(2)}) collective-permute-start(bf16[64,2048]{1,0:T(8,128)(2,1)S(1)} %collective-permute-done.3), channel_id=1, source_target_pairs={{0,8},{1,9},{2,10},{3,11},{4,12},{5,13},{6,14},{7,15},{8,0},{9,1},... | collective-permute-start | bytes 786440 | tf_op jit(solution)/shard_map/ppermute | solution.py:18
  25.2 5.0 %collective-permute-done.6 = bf16[64,2048]{1,0:T(8,128)(2,1)S(1)} collective-permute-done((bf16[64,2048]{1,0:T(8,128)(2,1)S(1)}, bf16[64,2048]{1,0:T(8,128)(2,1)S(1)}, u32[]{:S(2)}, u32[]{:S(2)}) %collective-permute-start.6) | collective-permute-done | bytes 262176 | tf_op jit(solution)/shard_map/ppermute | solution.py:18
  30.2 0.1 collective-permute-start.8
  30.3 1.1 %collective-permute-start.7 = (bf16[64,2048]{1,0:T(8,128)(2,1)S(1)}, bf16[64,2048]{1,0:T(8,128)(2,1)S(1)}, u32[]{:S(2)}, u32[]{:S(2)}) collective-permute-start(bf16[64,2048]{1,0:T(8,128)(2,1)S(1)} %collective-permute-done.6), channel_id=1, source_target_pairs={{0,16},{1,17},{2,18},{3,19},{4,20},{5,21},{6,22},{7,23},{8,120},{9... | collective-permute-start | bytes 786440 | tf_op jit(solution)/shard_map/ppermute | solution.py:18
  31.4 0.2 collective-permute-done.24
  31.6 2.8 %collective-permute-done.9 = bf16[64,2048]{1,0:T(8,128)(2,1)S(1)} collective-permute-done((bf16[64,2048]{1,0:T(8,128)(2,1)S(1)}, bf16[64,2048]{1,0:T(8,128)(2,1)S(1)}, u32[]{:S(2)}, u32[]{:S(2)}) %collective-permute-start.9) | collective-permute-done | bytes 262176 | tf_op jit(solution)/shard_map/ppermute | solution.py:18
  34.5 0.6 collective-permute-start.14
  35.1 0.9 collective-permute-done.12
  35.9 0.7 collective-permute-start.10
  36.6 0.1 constant_dynamic-slice_fusion.7
  36.8 0.0 slice-start.1
  36.8 5.9 %convolution_convert_fusion.3 = bf16[256,2048]{1,0:T(8,128)(2,1)S(1)} fusion(bf16[2048,2048]{1,0:T(8,128)(2,1)} %param.3, bf16[64,2048]{1,0:T(8,128)(2,1)S(1)} %get-tuple-element.34, bf16[64,2048]{1,0:T(8,128)(2,1)S(1)} %get-tuple-element.35, bf16[64,2048]{1,0:T(8,128)(2,1)S(1)} %get-tuple-element.36, bf16[64,2048]{1,0:T(8,128)(2,1)S(1)} %get-tuple-element.33), kind=kOutput, calls=%fused_computation.3 | convolution fusion | flops 2152202240 | bytes 10485760 | tf_op jit(solution)/shard_map/dot_general | solution.py:64
  42.7 0.1 fusion.22
  42.8 1.6 %collective-permute-start.22 = (bf16[128,2048]{1,0:T(8,128)(2,1)S(1)}, bf16[128,2048]{1,0:T(8,128)(2,1)S(1)}, u32[]{:S(2)}, u32[]{:S(2)}) collective-permute-start(bf16[128,2048]{1,0:T(8,128)(2,1)S(1)} %get-tuple-element.32), channel_id=1, source_target_pairs={{0,1},{1,0},{2,3},{3,2},{4,5},{5,4},{6,7},{7,6},{8,11},{9,10},{10,... | collective-permute-start | bytes 1572872 | tf_op jit(solution)/shard_map/ppermute | solution.py:18
  44.4 2.4 %collective-permute-start.26 = (bf16[64,2048]{1,0:T(8,128)(2,1)S(1)}, bf16[64,2048]{1,0:T(8,128)(2,1)S(1)}, u32[]{:S(2)}, u32[]{:S(2)}) collective-permute-start(bf16[64,2048]{1,0:T(8,128)(2,1)S(1)} %collective-permute-done.7), channel_id=1, source_target_pairs={{0,8},{1,9},{2,10},{3,11},{4,12},{5,13},{6,14},{7,15},{8,0},{9,1},... | collective-permute-start | bytes 786440 | tf_op jit(solution)/shard_map/ppermute | solution.py:18
  46.8 0.1 collective-permute-start.15
  46.9 1.2 %collective-permute-done.15 = bf16[32,2048]{1,0:T(8,128)(2,1)S(1)} collective-permute-done((bf16[32,2048]{1,0:T(8,128)(2,1)S(1)}, bf16[32,2048]{1,0:T(8,128)(2,1)S(1)}, u32[]{:S(2)}, u32[]{:S(2)}) %collective-permute-start.15) | collective-permute-done | bytes 131104 | tf_op jit(solution)/shard_map/ppermute | solution.py:18
  48.1 0.4 collective-permute-start.13
  48.5 0.1 pad_maximum_fusion.1
  48.9 2.5 %convolution_convert_fusion.1 = bf16[256,2048]{1,0:T(8,128)(2,1)S(1)} fusion(bf16[256,2048]{1,0:T(8,128)(2,1)S(1)} %dynamic-slice_dynamic-update-slice_fusion, bf16[2048,2048]{1,0:T(8,128)(2,1)S(1)} %bitcast.20), kind=kOutput, calls=%fused_computation.1 | convolution fusion | flops 2148007936 | bytes 10485760 | tf_op jit(solution)/shard_map/dot_general | solution.py:64
  51.5 0.1 pad_maximum_fusion
  51.8 2.5 %convolution_convert_fusion.2 = bf16[256,2048]{1,0:T(8,128)(2,1)S(1)} fusion(bf16[256,2048]{1,0:T(8,128)(2,1)S(1)} %dynamic-slice_dynamic-update-slice_fusion.8, bf16[2048,2048]{1,0:T(8,128)(2,1)S(1)} %bitcast.20), kind=kOutput, calls=%fused_computation.2 | convolution fusion | flops 2148007936 | bytes 10485760 | tf_op jit(solution)/shard_map/dot_general | solution.py:64
  54.3 0.1 fusion.20
  54.4 0.1 broadcast_select_fusion
  54.5 1.4 %collective-permute-start.19 = (bf16[128,2048]{1,0:T(8,128)(2,1)S(1)}, bf16[128,2048]{1,0:T(8,128)(2,1)S(1)}, u32[]{:S(2)}, u32[]{:S(2)}) collective-permute-start(bf16[128,2048]{1,0:T(8,128)(2,1)S(1)} %broadcast_select_fusion), channel_id=1, source_target_pairs={{0,4},{1,5},{2,6},{3,7},{4,0},{5,1},{6,2},{7,3},{8,12},{9,13},{10,... | collective-permute-start | bytes 1572872 | tf_op jit(solution)/shard_map/ppermute | solution.py:18
  55.9 0.5 collective-permute-start.16
  56.5 0.1 constant_dynamic-slice_fusion.3
  56.6 2.4 %convolution_convert_fusion = bf16[256,2048]{1,0:T(8,128)(2,1)S(1)} fusion(bf16[2048,2048]{1,0:T(8,128)(2,1)S(1)} %bitcast.20, bf16[64,2048]{1,0:T(8,128)(2,1)S(1)} %get-tuple-element.28, bf16[64,2048]{1,0:T(8,128)(2,1)S(1)} %get-tuple-element.29, bf16[64,2048]{1,0:T(8,128)(2,1)S(1)} %get-tuple-element.30, bf16[64,2048]{1,0:T(8,128)(2,1)S(1)} %get-tuple-element.27), kind=kOutput, calls=%fused_computation | convolution fusion | flops 2152202240 | bytes 10485760 | tf_op jit(solution)/shard_map/dot_general | solution.py:64
  59.1 1.9 %collective-permute-start.27 = (bf16[128,2048]{1,0:T(8,128)(2,1)S(1)}, bf16[128,2048]{1,0:T(8,128)(2,1)S(1)}, u32[]{:S(2)}, u32[]{:S(2)}) collective-permute-start(bf16[128,2048]{1,0:T(8,128)(2,1)S(1)} %slice.123), channel_id=1, source_target_pairs={{0,1},{1,0},{2,3},{3,2},{4,5},{5,4},{6,7},{7,6},{8,11},{9,10},{10,... | collective-permute-start | bytes 1572872 | tf_op jit(solution)/shard_map/ppermute | solution.py:18
  60.9 0.1 convert_add_fusion.1
  61.1 0.6 collective-permute-start.23
  61.7 6.8 %collective-permute-done.19 = bf16[128,2048]{1,0:T(8,128)(2,1)S(1)} collective-permute-done((bf16[128,2048]{1,0:T(8,128)(2,1)S(1)}, bf16[128,2048]{1,0:T(8,128)(2,1)S(1)}, u32[]{:S(2)}, u32[]{:S(2)}) %collective-permute-start.19) | collective-permute-done | bytes 524320 | tf_op jit(solution)/shard_map/ppermute | solution.py:18
  68.5 0.2 convert_add_fusion.2
  68.8 0.3 collective-permute-start.20
  69.1 0.2 fusion.19
  69.3 1.2 %collective-permute-start.17 = (bf16[64,2048]{1,0:T(8,128)(2,1)S(1)}, bf16[64,2048]{1,0:T(8,128)(2,1)S(1)}, u32[]{:S(2)}, u32[]{:S(2)}) collective-permute-start(bf16[64,2048]{1,0:T(8,128)(2,1)S(1)} %pad_maximum_fusion.3), channel_id=1, source_target_pairs={{0,3},{1,2},{2,1},{3,0},{4,7},{5,6},{6,5},{7,4},{8,9},{9,8},{10,11... | collective-permute-start | bytes 786440 | tf_op jit(solution)/shard_map/ppermute | solution.py:18
  70.5 5.7 %collective-permute-done.27 = bf16[128,2048]{1,0:T(8,128)(2,1)S(1)} collective-permute-done((bf16[128,2048]{1,0:T(8,128)(2,1)S(1)}, bf16[128,2048]{1,0:T(8,128)(2,1)S(1)}, u32[]{:S(2)}, u32[]{:S(2)}) %collective-permute-start.27) | collective-permute-done | bytes 524320 | tf_op jit(solution)/shard_map/ppermute | solution.py:18
  76.3 0.1 convert_add_fusion
  76.4 0.1 collective-permute-start.28
  76.5 5.3 %collective-permute-done.20 = bf16[64,2048]{1,0:T(8,128)(2,1)S(1)} collective-permute-done((bf16[64,2048]{1,0:T(8,128)(2,1)S(1)}, bf16[64,2048]{1,0:T(8,128)(2,1)S(1)}, u32[]{:S(2)}, u32[]{:S(2)}) %collective-permute-start.20) | collective-permute-done | bytes 262176 | tf_op jit(solution)/shard_map/ppermute | solution.py:18
  82.0 0.1 collective-permute-start.21
  82.1 0.1 select_convert_fusion.1
  82.1 0.3 collective-permute-start.18
  82.4 1.7 %collective-permute-done.28 = bf16[64,2048]{1,0:T(8,128)(2,1)S(1)} collective-permute-done((bf16[64,2048]{1,0:T(8,128)(2,1)S(1)}, bf16[64,2048]{1,0:T(8,128)(2,1)S(1)}, u32[]{:S(2)}, u32[]{:S(2)}) %collective-permute-start.28) | collective-permute-done | bytes 262176 | tf_op jit(solution)/shard_map/ppermute | solution.py:18
  84.1 0.1 select_convert_fusion
  84.2 0.3 collective-permute-start.29
  84.5 4.0 %collective-permute-done.18 = bf16[32,2048]{1,0:T(8,128)(2,1)S(1)} collective-permute-done((bf16[32,2048]{1,0:T(8,128)(2,1)S(1)}, bf16[32,2048]{1,0:T(8,128)(2,1)S(1)}, u32[]{:S(2)}, u32[]{:S(2)}) %collective-permute-start.18) | collective-permute-done | bytes 131104 | tf_op jit(solution)/shard_map/ppermute | solution.py:18
  88.5 0.1 convert_add_fusion.5
  88.7 3.5 %collective-permute-done.29 = bf16[64,2048]{1,0:T(8,128)(2,1)S(1)} collective-permute-done((bf16[64,2048]{1,0:T(8,128)(2,1)S(1)}, bf16[64,2048]{1,0:T(8,128)(2,1)S(1)}, u32[]{:S(2)}, u32[]{:S(2)}) %collective-permute-start.29) | collective-permute-done | bytes 262176 | tf_op jit(solution)/shard_map/ppermute | solution.py:18
  92.2 0.1 convert_add_fusion.4
  92.3 1.1 %maximum_select_fusion = f32[128,2048]{1,0:T(8,128)} fusion(f32[64,2048]{1,0:T(8,128)S(1)} %convert_add_fusion.4, f32[32,2048]{1,0:T(8,128)S(1)} %slice_add_fusion.3, f32[32,2048]{1,0:T(8,128)S(1)} %convert_add_fusion.5, pred[]{:T(512)S(6)} %eq.114), kind=kLoop, calls=%fused_computation.22 | loop fusion | flops 1310720 | bytes 2097153 | tf_op jit(solution)/shard_map/jit(_where)/select_n | solution.py:165
  (65 shorter events, 1.0 us)
Async XLA Ops:
  0.0 1.6 %copy-start = (bf16[4,512,512]{2,1,0:T(8,128)(2,1)S(1)}, bf16[4,512,512]{2,1,0:T(8,128)(2,1)}, u32[]{:S(2)}) copy-start(bf16[4,512,512]{2,1,0:T(8,128)(2,1)} %param.5) | copy-start | bytes 6291460
  3.0 1.4 %collective-permute-start = (bf16[32,2048]{1,0:T(8,128)(2,1)S(1)}, bf16[32,2048]{1,0:T(8,128)(2,1)S(1)}, u32[]{:S(2)}, u32[]{:S(2)}) collective-permute-start(bf16[32,2048]{1,0:T(8,128)(2,1)S(1)} %bitcast.15), channel_id=1, source_target_pairs={{0,8},{1,9},{2,10},{3,11},{4,12},{5,13},{6,14},{7,15},{8,0},{9,1},... | collective-permute-start | bytes 393224 | tf_op jit(solution)/shard_map/ppermute | solution.py:18
  4.4 10.3 %collective-permute-start.2 = (bf16[64,2048]{1,0:T(8,128)(2,1)S(1)}, bf16[64,2048]{1,0:T(8,128)(2,1)S(1)}, u32[]{:S(2)}, u32[]{:S(2)}) collective-permute-start(bf16[64,2048]{1,0:T(8,128)(2,1)S(1)} %maximum_select_fusion.1), channel_id=1, source_target_pairs={{0,16},{1,17},{2,18},{3,19},{4,20},{5,21},{6,22},{7,23},{8,120},{9... | collective-permute-start | bytes 786440 | tf_op jit(solution)/shard_map/ppermute | solution.py:18
  6.4 6.5 %collective-permute-start.1 = (bf16[32,2048]{1,0:T(8,128)(2,1)S(1)}, bf16[32,2048]{1,0:T(8,128)(2,1)S(1)}, u32[]{:S(2)}, u32[]{:S(2)}) collective-permute-start(bf16[32,2048]{1,0:T(8,128)(2,1)S(1)} %bitcast.17), channel_id=1, source_target_pairs={{0,128},{1,129},{2,130},{3,131},{4,132},{5,133},{6,134},{7,135},{8... | collective-permute-start | bytes 393224 | tf_op jit(solution)/shard_map/ppermute | solution.py:18
  14.7 1.8 %collective-permute-start.5 = (bf16[32,2048]{1,0:T(8,128)(2,1)S(1)}, bf16[32,2048]{1,0:T(8,128)(2,1)S(1)}, u32[]{:S(2)}, u32[]{:S(2)}) collective-permute-start(bf16[32,2048]{1,0:T(8,128)(2,1)S(1)} %collective-permute-done.1), channel_id=1, source_target_pairs={{0,8},{1,9},{2,10},{3,11},{4,12},{5,13},{6,14},{7,15},{8,0},{9,1},... | collective-permute-start | bytes 393224 | tf_op jit(solution)/shard_map/ppermute | solution.py:18
  15.6 9.6 %collective-permute-start.11 = (bf16[64,2048]{1,0:T(8,128)(2,1)S(1)}, bf16[64,2048]{1,0:T(8,128)(2,1)S(1)}, u32[]{:S(2)}, u32[]{:S(2)}) collective-permute-start(bf16[64,2048]{1,0:T(8,128)(2,1)S(1)} %collective-permute-done.2), channel_id=1, source_target_pairs={{0,8},{1,9},{2,10},{3,11},{4,12},{5,13},{6,14},{7,15},{8,0},{9,1},... | collective-permute-start | bytes 786440 | tf_op jit(solution)/shard_map/ppermute | solution.py:18
  15.6 7.6 %collective-permute-start.3 = (bf16[64,2048]{1,0:T(8,128)(2,1)S(1)}, bf16[64,2048]{1,0:T(8,128)(2,1)S(1)}, u32[]{:S(2)}, u32[]{:S(2)}) collective-permute-start(bf16[64,2048]{1,0:T(8,128)(2,1)S(1)} %collective-permute-done.2), channel_id=1, source_target_pairs={{0,16},{1,17},{2,18},{3,19},{4,20},{5,21},{6,22},{7,23},{8,120},{9... | collective-permute-start | bytes 786440 | tf_op jit(solution)/shard_map/ppermute | solution.py:18
  16.6 13.6 %collective-permute-start.6 = (bf16[64,2048]{1,0:T(8,128)(2,1)S(1)}, bf16[64,2048]{1,0:T(8,128)(2,1)S(1)}, u32[]{:S(2)}, u32[]{:S(2)}) collective-permute-start(bf16[64,2048]{1,0:T(8,128)(2,1)S(1)} %maximum_select_fusion.2), channel_id=1, source_target_pairs={{0,32},{1,33},{2,34},{3,35},{4,36},{5,37},{6,38},{7,39},{8,104},{9... | collective-permute-start | bytes 786440 | tf_op jit(solution)/shard_map/ppermute | solution.py:18
  20.0 11.6 %collective-permute-start.24 = (bf16[64,2048]{1,0:T(8,128)(2,1)S(1)}, bf16[64,2048]{1,0:T(8,128)(2,1)S(1)}, u32[]{:S(2)}, u32[]{:S(2)}) collective-permute-start(bf16[64,2048]{1,0:T(8,128)(2,1)S(1)} %maximum_select_fusion.2), channel_id=1, source_target_pairs={{0,16},{1,17},{2,18},{3,19},{4,20},{5,21},{6,22},{7,23},{8,120},{9... | collective-permute-start | bytes 786440 | tf_op jit(solution)/shard_map/ppermute | solution.py:18
  23.2 11.2 %collective-permute-start.9 = (bf16[64,2048]{1,0:T(8,128)(2,1)S(1)}, bf16[64,2048]{1,0:T(8,128)(2,1)S(1)}, u32[]{:S(2)}, u32[]{:S(2)}) collective-permute-start(bf16[64,2048]{1,0:T(8,128)(2,1)S(1)} %collective-permute-done.3), channel_id=1, source_target_pairs={{0,16},{1,17},{2,18},{3,19},{4,20},{5,21},{6,22},{7,23},{8,120},{9... | collective-permute-start | bytes 786440 | tf_op jit(solution)/shard_map/ppermute | solution.py:18
  23.2 28.3 %collective-permute-start.4 = (bf16[64,2048]{1,0:T(8,128)(2,1)S(1)}, bf16[64,2048]{1,0:T(8,128)(2,1)S(1)}, u32[]{:S(2)}, u32[]{:S(2)}) collective-permute-start(bf16[64,2048]{1,0:T(8,128)(2,1)S(1)} %collective-permute-done.3), channel_id=1, source_target_pairs={{0,8},{1,9},{2,10},{3,11},{4,12},{5,13},{6,14},{7,15},{8,0},{9,1},... | collective-permute-start | bytes 786440 | tf_op jit(solution)/shard_map/ppermute | solution.py:18
  30.2 12.6 %collective-permute-start.8 = (bf16[32,2048]{1,0:T(8,128)(2,1)S(1)}, bf16[32,2048]{1,0:T(8,128)(2,1)S(1)}, u32[]{:S(2)}, u32[]{:S(2)}) collective-permute-start(bf16[32,2048]{1,0:T(8,128)(2,1)S(1)} %constant_dynamic-slice_fusion.9), channel_id=1, source_target_pairs={{0,32},{1,33},{2,34},{3,35},{4,36},{5,37},{6,38},{7,39},{8,104},{9... | collective-permute-start | bytes 393224 | tf_op jit(solution)/shard_map/ppermute | solution.py:18
  30.3 14.1 %collective-permute-start.7 = (bf16[64,2048]{1,0:T(8,128)(2,1)S(1)}, bf16[64,2048]{1,0:T(8,128)(2,1)S(1)}, u32[]{:S(2)}, u32[]{:S(2)}) collective-permute-start(bf16[64,2048]{1,0:T(8,128)(2,1)S(1)} %collective-permute-done.6), channel_id=1, source_target_pairs={{0,16},{1,17},{2,18},{3,19},{4,20},{5,21},{6,22},{7,23},{8,120},{9... | collective-permute-start | bytes 786440 | tf_op jit(solution)/shard_map/ppermute | solution.py:18
  31.6 2.9 %collective-permute-start.25 = (bf16[64,2048]{1,0:T(8,128)(2,1)S(1)}, bf16[64,2048]{1,0:T(8,128)(2,1)S(1)}, u32[]{:S(2)}, u32[]{:S(2)}) collective-permute-start(bf16[64,2048]{1,0:T(8,128)(2,1)S(1)} %collective-permute-done.24), channel_id=1, source_target_pairs={{0,8},{1,9},{2,10},{3,11},{4,12},{5,13},{6,14},{7,15},{8,0},{9,1},... | collective-permute-start | bytes 786440 | tf_op jit(solution)/shard_map/ppermute | solution.py:18
  34.4 1.5 %collective-permute-start.12 = (bf16[64,2048]{1,0:T(8,128)(2,1)S(1)}, bf16[64,2048]{1,0:T(8,128)(2,1)S(1)}, u32[]{:S(2)}, u32[]{:S(2)}) collective-permute-start(bf16[64,2048]{1,0:T(8,128)(2,1)S(1)} %collective-permute-done.9), channel_id=1, source_target_pairs={{0,8},{1,9},{2,10},{3,11},{4,12},{5,13},{6,14},{7,15},{8,0},{9,1},... | collective-permute-start | bytes 786440 | tf_op jit(solution)/shard_map/ppermute | solution.py:18
  34.5 14.1 %collective-permute-start.14 = (bf16[64,2048]{1,0:T(8,128)(2,1)S(1)}, bf16[64,2048]{1,0:T(8,128)(2,1)S(1)}, u32[]{:S(2)}, u32[]{:S(2)}) collective-permute-start(bf16[64,2048]{1,0:T(8,128)(2,1)S(1)} %collective-permute-done.6), channel_id=1, source_target_pairs={{0,8},{1,9},{2,10},{3,11},{4,12},{5,13},{6,14},{7,15},{8,0},{9,1},... | collective-permute-start | bytes 786440 | tf_op jit(solution)/shard_map/ppermute | solution.py:18
  35.9 8.4 %collective-permute-start.10 = (bf16[32,2048]{1,0:T(8,128)(2,1)S(1)}, bf16[32,2048]{1,0:T(8,128)(2,1)S(1)}, u32[]{:S(2)}, u32[]{:S(2)}) collective-permute-start(bf16[32,2048]{1,0:T(8,128)(2,1)S(1)} %constant_dynamic-slice_fusion.8), channel_id=1, source_target_pairs={{0,16},{1,17},{2,18},{3,19},{4,20},{5,21},{6,22},{7,23},{8,120},{9... | collective-permute-start | bytes 393224 | tf_op jit(solution)/shard_map/ppermute | solution.py:18
  36.6 12.2 %slice-start = ((s8[8388608]{0:T(1024)(128)(4,1)}), s8[4194304]{0:T(1024)(128)(4,1)S(1)}, s32[]{:S(2)}) async-start(s8[8388608]{0:T(1024)(128)(4,1)} %bitcast.19), calls=%async_computation | async-start | bytes 8388608
  36.8 12.1 %slice-start.1 = ((s8[8388608]{0:T(1024)(128)(4,1)}), s8[4194304]{0:T(1024)(128)(4,1)S(1)}, s32[]{:S(2)}) async-start(s8[8388608]{0:T(1024)(128)(4,1)} %bitcast.19), calls=%async_computation.1 | async-start | bytes 8388608
  42.8 18.2 %collective-permute-start.22 = (bf16[128,2048]{1,0:T(8,128)(2,1)S(1)}, bf16[128,2048]{1,0:T(8,128)(2,1)S(1)}, u32[]{:S(2)}, u32[]{:S(2)}) collective-permute-start(bf16[128,2048]{1,0:T(8,128)(2,1)S(1)} %get-tuple-element.32), channel_id=1, source_target_pairs={{0,1},{1,0},{2,3},{3,2},{4,5},{5,4},{6,7},{7,6},{8,11},{9,10},{10,... | collective-permute-start | bytes 1572872 | tf_op jit(solution)/shard_map/ppermute | solution.py:18
  44.4 12.1 %collective-permute-start.26 = (bf16[64,2048]{1,0:T(8,128)(2,1)S(1)}, bf16[64,2048]{1,0:T(8,128)(2,1)S(1)}, u32[]{:S(2)}, u32[]{:S(2)}) collective-permute-start(bf16[64,2048]{1,0:T(8,128)(2,1)S(1)} %collective-permute-done.7), channel_id=1, source_target_pairs={{0,8},{1,9},{2,10},{3,11},{4,12},{5,13},{6,14},{7,15},{8,0},{9,1},... | collective-permute-start | bytes 786440 | tf_op jit(solution)/shard_map/ppermute | solution.py:18
  46.8 1.3 %collective-permute-start.15 = (bf16[32,2048]{1,0:T(8,128)(2,1)S(1)}, bf16[32,2048]{1,0:T(8,128)(2,1)S(1)}, u32[]{:S(2)}, u32[]{:S(2)}) collective-permute-start(bf16[32,2048]{1,0:T(8,128)(2,1)S(1)} %collective-permute-done.8), channel_id=1, source_target_pairs={{0,8},{1,9},{2,10},{3,11},{4,12},{5,13},{6,14},{7,15},{8,0},{9,1},... | collective-permute-start | bytes 393224 | tf_op jit(solution)/shard_map/ppermute | solution.py:18
  48.1 3.3 %collective-permute-start.13 = (bf16[32,2048]{1,0:T(8,128)(2,1)S(1)}, bf16[32,2048]{1,0:T(8,128)(2,1)S(1)}, u32[]{:S(2)}, u32[]{:S(2)}) collective-permute-start(bf16[32,2048]{1,0:T(8,128)(2,1)S(1)} %collective-permute-done.10), channel_id=1, source_target_pairs={{0,8},{1,9},{2,10},{3,11},{4,12},{5,13},{6,14},{7,15},{8,0},{9,1},... | collective-permute-start | bytes 393224 | tf_op jit(solution)/shard_map/ppermute | solution.py:18
  54.5 14.1 %collective-permute-start.19 = (bf16[128,2048]{1,0:T(8,128)(2,1)S(1)}, bf16[128,2048]{1,0:T(8,128)(2,1)S(1)}, u32[]{:S(2)}, u32[]{:S(2)}) collective-permute-start(bf16[128,2048]{1,0:T(8,128)(2,1)S(1)} %broadcast_select_fusion), channel_id=1, source_target_pairs={{0,4},{1,5},{2,6},{3,7},{4,0},{5,1},{6,2},{7,3},{8,12},{9,13},{10,... | collective-permute-start | bytes 1572872 | tf_op jit(solution)/shard_map/ppermute | solution.py:18
  55.9 13.2 %collective-permute-start.16 = (bf16[128,2048]{1,0:T(8,128)(2,1)S(1)}, bf16[128,2048]{1,0:T(8,128)(2,1)S(1)}, u32[]{:S(2)}, u32[]{:S(2)}) collective-permute-start(bf16[128,2048]{1,0:T(8,128)(2,1)S(1)} %pad_maximum_fusion.2), channel_id=1, source_target_pairs={{0,1},{1,0},{2,3},{3,2},{4,5},{5,4},{6,7},{7,6},{8,11},{9,10},{10,... | collective-permute-start | bytes 1572872 | tf_op jit(solution)/shard_map/ppermute | solution.py:18
  59.1 17.2 %collective-permute-start.27 = (bf16[128,2048]{1,0:T(8,128)(2,1)S(1)}, bf16[128,2048]{1,0:T(8,128)(2,1)S(1)}, u32[]{:S(2)}, u32[]{:S(2)}) collective-permute-start(bf16[128,2048]{1,0:T(8,128)(2,1)S(1)} %slice.123), channel_id=1, source_target_pairs={{0,1},{1,0},{2,3},{3,2},{4,5},{5,4},{6,7},{7,6},{8,11},{9,10},{10,... | collective-permute-start | bytes 1572872 | tf_op jit(solution)/shard_map/ppermute | solution.py:18
  61.1 21.3 %collective-permute-start.23 = (bf16[64,2048]{1,0:T(8,128)(2,1)S(1)}, bf16[64,2048]{1,0:T(8,128)(2,1)S(1)}, u32[]{:S(2)}, u32[]{:S(2)}) collective-permute-start(bf16[64,2048]{1,0:T(8,128)(2,1)S(1)} %slice.162), channel_id=1, source_target_pairs={{0,3},{1,2},{2,1},{3,0},{4,7},{5,6},{6,5},{7,4},{8,9},{9,8},{10,11... | collective-permute-start | bytes 786440 | tf_op jit(solution)/shard_map/ppermute | solution.py:18
  68.8 13.1 %collective-permute-start.20 = (bf16[64,2048]{1,0:T(8,128)(2,1)S(1)}, bf16[64,2048]{1,0:T(8,128)(2,1)S(1)}, u32[]{:S(2)}, u32[]{:S(2)}) collective-permute-start(bf16[64,2048]{1,0:T(8,128)(2,1)S(1)} %slice.163), channel_id=1, source_target_pairs={{0,1},{1,0},{2,3},{3,2},{4,5},{5,4},{6,7},{7,6},{8,11},{9,10},{10,... | collective-permute-start | bytes 786440 | tf_op jit(solution)/shard_map/ppermute | solution.py:18
  69.3 12.8 %collective-permute-start.17 = (bf16[64,2048]{1,0:T(8,128)(2,1)S(1)}, bf16[64,2048]{1,0:T(8,128)(2,1)S(1)}, u32[]{:S(2)}, u32[]{:S(2)}) collective-permute-start(bf16[64,2048]{1,0:T(8,128)(2,1)S(1)} %pad_maximum_fusion.3), channel_id=1, source_target_pairs={{0,3},{1,2},{2,1},{3,0},{4,7},{5,6},{6,5},{7,4},{8,9},{9,8},{10,11... | collective-permute-start | bytes 786440 | tf_op jit(solution)/shard_map/ppermute | solution.py:18
  76.4 7.7 %collective-permute-start.28 = (bf16[64,2048]{1,0:T(8,128)(2,1)S(1)}, bf16[64,2048]{1,0:T(8,128)(2,1)S(1)}, u32[]{:S(2)}, u32[]{:S(2)}) collective-permute-start(bf16[64,2048]{1,0:T(8,128)(2,1)S(1)} %slice.161), channel_id=1, source_target_pairs={{0,3},{1,2},{2,1},{3,0},{4,7},{5,6},{6,5},{7,4},{8,9},{9,8},{10,11... | collective-permute-start | bytes 786440 | tf_op jit(solution)/shard_map/ppermute | solution.py:18
  82.0 6.7 %collective-permute-start.21 = (bf16[32,2048]{1,0:T(8,128)(2,1)S(1)}, bf16[32,2048]{1,0:T(8,128)(2,1)S(1)}, u32[]{:S(2)}, u32[]{:S(2)}) collective-permute-start(bf16[32,2048]{1,0:T(8,128)(2,1)S(1)} %slice.164), channel_id=1, source_target_pairs={{0,3},{1,2},{2,1},{3,0},{4,7},{5,6},{6,5},{7,4},{8,9},{9,8},{10,11... | collective-permute-start | bytes 393224 | tf_op jit(solution)/shard_map/ppermute | solution.py:18
  82.1 6.4 %collective-permute-start.18 = (bf16[32,2048]{1,0:T(8,128)(2,1)S(1)}, bf16[32,2048]{1,0:T(8,128)(2,1)S(1)}, u32[]{:S(2)}, u32[]{:S(2)}) collective-permute-start(bf16[32,2048]{1,0:T(8,128)(2,1)S(1)} %select_convert_fusion.1), channel_id=1, source_target_pairs={{0,4},{1,5},{2,6},{3,7},{4,0},{5,1},{6,2},{7,3},{8,12},{9,13},{10,... | collective-permute-start | bytes 393224 | tf_op jit(solution)/shard_map/ppermute | solution.py:18
  84.2 7.9 %collective-permute-start.29 = (bf16[64,2048]{1,0:T(8,128)(2,1)S(1)}, bf16[64,2048]{1,0:T(8,128)(2,1)S(1)}, u32[]{:S(2)}, u32[]{:S(2)}) collective-permute-start(bf16[64,2048]{1,0:T(8,128)(2,1)S(1)} %select_convert_fusion), channel_id=1, source_target_pairs={{0,4},{1,5},{2,6},{3,7},{4,0},{5,1},{6,2},{7,3},{8,12},{9,13},{10,... | collective-permute-start | bytes 786440 | tf_op jit(solution)/shard_map/ppermute | solution.py:18

commit v3 on v2

--- a/solution.py
+++ b/solution.py
@@ -88,15 +88,19 @@
     part = rows // 2
     own_rows = lambda held: lax.dynamic_slice_in_dim(held, c * part, part)
 
-    def scores(place, cuts, *blocks):
+    def picked(place, cuts, *blocks):
         held = jnp.concatenate(blocks)
         size = rows // cuts
-        picked = [
-            lax.dynamic_slice_in_dim(held, place(owner) * rows + cut * size, size)
-            for cut in range(cuts)
-            for owner in (x ^ m1, x ^ 2, x, x ^ m2)
-        ]
-        return score_rows(jnp.concatenate(picked), train_grads)
+        return jnp.concatenate(
+            [
+                lax.dynamic_slice_in_dim(held, place(owner) * rows + cut * size, size)
+                for cut in range(cuts)
+                for owner in (x ^ m1, x ^ 2, x, x ^ m2)
+            ]
+        )
+
+    def scores(ready):
+        return score_rows(ready, train_grads)
 
     def odd_place(owner):
         step = (2 * owner + 1 - z % 2 - z) % 8
@@ -114,21 +118,26 @@
     across, o1 = together(other_half(mine), along_z(plane))
     o2 = along_z(o1)
     a0 = both_cores(c, across, other_core(across))
+    t1, t2 = other_core(o1), other_core(o2)
+    known = scores(jnp.concatenate([plane, o2, t2]))
+    known = [known[:rows], known[rows : 2 * rows], known[2 * rows :]]
     a1 = along_z(a0)
-    a2 = along_z_twice(a0)
+    a2, known[1] = together(along_z_twice(a0), known[1])
     o3 = along_z(o2)
     a3 = along_z(a2)
     a4 = along_z_twice(own_rows(a2))
     o4 = along_z(own_rows(o3))
-    t1, t2, t3 = map(other_core, (o1, o2, o3))
-    odd = scores(odd_place, 1, o1, t1, o3, t3)
+    t3 = other_core(o3)
+    odd = scores(picked(odd_place, 1, o1, t1, o3, t3))
     odd_come, odd = first_x(odd[: 2 * rows]), odd[2 * rows :]
     a3, a4, o4, odd = together(a3, a4, o4, odd)
     t4 = other_core(o4)
-    even = scores(even_place, 2, plane, o2, t2, both_cores(c, o4, t4))
     u1, u2, u3, u4 = map(other_core, (a1, a2, a3, a4))
-    odd_across = scores(odd_place, 1, a1, u1, a3, u3)
-    even_across = scores(even_place, 2, a0, a2, u2, both_cores(c, a4, u4))
+    odd_across = scores(picked(odd_place, 1, a1, u1, a3, u3))
+    u4, odd_across_kept = together(u4, odd_across[2 * rows :])
+    ready = picked(even_place, 2, a0, a2, u2, both_cores(c, a4, u4))
+    even_across = scores(jnp.concatenate([ready, both_cores(c, o4, t4)]))
+    even = picked(even_place, 2, *known, even_across[4 * rows :])
 
     wide = lambda value: value.astype(jnp.float32)
 
@@ -151,10 +160,10 @@
 
     half = 2 * rows
     (odd,) = pass_on(wide(odd) + wide(odd_come), [rows])
-    second = over_runs(even[half:], even_across[half:])
+    second = over_runs(even[half:], even_across[half : 2 * half])
     second_come = first_x(second[:rows].astype(jnp.bfloat16))
     come = first_x(odd_across[:half])
-    (odd_across,) = pass_on(wide(odd_across[half:]) + wide(come), [rows])
+    (odd_across,) = pass_on(wide(odd_across_kept) + wide(come), [rows])
     come = first_x(jnp.concatenate([even[:rows], even_across[:rows]]))
     kept = jnp.concatenate([even[rows:half], even_across[rows:half]])
     even, even_across = pass_on(wide(kept) + wide(come), [part, part])

time: 93.5 us -> 89.8 us (0.960)
  waiting for transfers between devices: 49.5 us -> 32.7 us
  starting transfers between devices: 23.3 us -> 35.6 us
    ppermute x30, waiting for transfers between devices: 49.5 us -> 32.7 us  [move(): return lax.ppermute(value, NAMES, pairs)]
    ppermute x30, starting transfers between devices: 23.3 us -> 35.6 us  [move(): return lax.ppermute(value, NAMES, pairs)]
    unnamed x26 -> x20, local copies, waits for them, and re-layouts: 1.98 us -> 1.86 us
  transfers between devices with their start and end apart: 30 -> 30, of which waited for: 16 -> 14; matrix products, arithmetic and copies ran while one was open for 17% -> 19% of each run, Pallas kernels for 0% -> 0%
where the time goes in v3:
time: 89.8 us; the launch traced here: 89.7 us
  starting transfers between devices  35.6 us (40%)
  waiting for transfers between devices  32.7 us (36%)
  matrix products  15.5 us (17%)
  local copies, waits for them, and re-layouts  2.72 us (3%)
  other arithmetic  2.7 us (3%)
    ppermute x30, starting transfers between devices, move(): return lax.ppermute(value, NAMES, pairs)  35.6 us
    ppermute x30, waiting for transfers between devices, move(): return lax.ppermute(value, NAMES, pairs)  32.7 us
    dot_general x4, matrix products, score_rows(): lax.dot_general(ready, train_grads, (((1,), (1,)), ((), ())), preferred_e...  14.1 us
    unnamed x20, local copies, waits for them, and re-layouts  1.86 us
  transfers between devices with their start and end apart: 30, of which 14 were waited for; matrix products, arithmetic and copies ran while one was open for 19% of the time, Pallas kernels for 0%

profile of v3, /device:TPU:16, one launch (start us, length us, event | category | flops | bytes accessed | tf_op | source)
XLA Modules:
  0.0 89.7 jit_solution(14439421069620041950)
XLA Ops:
  0.0 1.6 %copy-done = bf16[4,512,512]{2,1,0:T(8,128)(2,1)S(1)} copy-done((bf16[4,512,512]{2,1,0:T(8,128)(2,1)S(1)}, bf16[4,512,512]{2,1,0:T(8,128)(2,1)}, u32[]{:S(2)}) %copy-start) | copy-done | bytes 2097176
  1.6 1.3 %fusion = bf16[4,4,8,512]{3,2,1,0:T(8,128)(2,1)S(1)} fusion(bf16[4,512,512]{2,1,0:T(8,128)(2,1)S(1)} %copy-done, bf16[4,4,8,512]{3,2,1,0:T(8,128)(2,1)} %bitcast.17), kind=kOutput, calls=%fused_computation.5 | convolution fusion | flops 67174400 | bytes 2359296 | tf_op jit(solution)/shard_map/rbi,bij->rbj/dot_general | solution.py:59
  3.0 0.1 collective-permute-start
  3.1 1.3 %collective-permute-done = bf16[32,2048]{1,0:T(8,128)(2,1)S(1)} collective-permute-done((bf16[32,2048]{1,0:T(8,128)(2,1)S(1)}, bf16[32,2048]{1,0:T(8,128)(2,1)S(1)}, u32[]{:S(2)}, u32[]{:S(2)}) %collective-permute-start) | collective-permute-done | bytes 131104 | tf_op jit(solution)/shard_map/ppermute | solution.py:18
  4.4 2.0 %collective-permute-start.2 = (bf16[64,2048]{1,0:T(8,128)(2,1)S(1)}, bf16[64,2048]{1,0:T(8,128)(2,1)S(1)}, u32[]{:S(2)}, u32[]{:S(2)}) collective-permute-start(bf16[64,2048]{1,0:T(8,128)(2,1)S(1)} %maximum_select_fusion.1), channel_id=1, source_target_pairs={{0,16},{1,17},{2,18},{3,19},{4,20},{5,21},{6,22},{7,23},{8,120},{9... | collective-permute-start | bytes 786440 | tf_op jit(solution)/shard_map/ppermute | solution.py:18
  6.4 0.3 collective-permute-start.1
  6.8 6.1 %collective-permute-done.1 = bf16[32,2048]{1,0:T(8,128)(2,1)S(1)} collective-permute-done((bf16[32,2048]{1,0:T(8,128)(2,1)S(1)}, bf16[32,2048]{1,0:T(8,128)(2,1)S(1)}, u32[]{:S(2)}, u32[]{:S(2)}) %collective-permute-start.1) | collective-permute-done | bytes 131104 | tf_op jit(solution)/shard_map/ppermute | solution.py:18
  12.9 1.8 %collective-permute-done.2 = bf16[64,2048]{1,0:T(8,128)(2,1)S(1)} collective-permute-done((bf16[64,2048]{1,0:T(8,128)(2,1)S(1)}, bf16[64,2048]{1,0:T(8,128)(2,1)S(1)}, u32[]{:S(2)}, u32[]{:S(2)}) %collective-permute-start.2) | collective-permute-done | bytes 262176 | tf_op jit(solution)/shard_map/ppermute | solution.py:18
  14.7 0.8 collective-permute-start.5
  15.6 1.0 %collective-permute-done.5 = bf16[32,2048]{1,0:T(8,128)(2,1)S(1)} collective-permute-done((bf16[32,2048]{1,0:T(8,128)(2,1)S(1)}, bf16[32,2048]{1,0:T(8,128)(2,1)S(1)}, u32[]{:S(2)}, u32[]{:S(2)}) %collective-permute-start.5) | collective-permute-done | bytes 131104 | tf_op jit(solution)/shard_map/ppermute | solution.py:18
  16.6 0.8 collective-permute-start.15
  17.4 3.7 %collective-permute-start.6 = (bf16[64,2048]{1,0:T(8,128)(2,1)S(1)}, bf16[64,2048]{1,0:T(8,128)(2,1)S(1)}, u32[]{:S(2)}, u32[]{:S(2)}) collective-permute-start(bf16[64,2048]{1,0:T(8,128)(2,1)S(1)} %maximum_select_fusion.2), channel_id=1, source_target_pairs={{0,32},{1,33},{2,34},{3,35},{4,36},{5,37},{6,38},{7,39},{8,104},{9... | collective-permute-start | bytes 786440 | tf_op jit(solution)/shard_map/ppermute | solution.py:18
  21.2 2.0 %collective-permute-done.3 = bf16[64,2048]{1,0:T(8,128)(2,1)S(1)} collective-permute-done((bf16[64,2048]{1,0:T(8,128)(2,1)S(1)}, bf16[64,2048]{1,0:T(8,128)(2,1)S(1)}, u32[]{:S(2)}, u32[]{:S(2)}) %collective-permute-start.3) | collective-permute-done | bytes 262176 | tf_op jit(solution)/shard_map/ppermute | solution.py:18
  23.2 1.7 %collective-permute-start.4 = (bf16[64,2048]{1,0:T(8,128)(2,1)S(1)}, bf16[64,2048]{1,0:T(8,128)(2,1)S(1)}, u32[]{:S(2)}, u32[]{:S(2)}) collective-permute-start(bf16[64,2048]{1,0:T(8,128)(2,1)S(1)} %collective-permute-done.3), channel_id=1, source_target_pairs={{0,8},{1,9},{2,10},{3,11},{4,12},{5,13},{6,14},{7,15},{8,0},{9,1},... | collective-permute-start | bytes 786440 | tf_op jit(solution)/shard_map/ppermute | solution.py:18
  24.9 1.1 %collective-permute-done.15 = bf16[64,2048]{1,0:T(8,128)(2,1)S(1)} collective-permute-done((bf16[64,2048]{1,0:T(8,128)(2,1)S(1)}, bf16[64,2048]{1,0:T(8,128)(2,1)S(1)}, u32[]{:S(2)}, u32[]{:S(2)}) %collective-permute-start.15) | collective-permute-done | bytes 262176 | tf_op jit(solution)/shard_map/ppermute | solution.py:18
  26.0 0.8 collective-permute-start.16
  26.8 6.4 %convolution_convert_fusion.3 = bf16[192,2048]{1,0:T(8,128)(2,1)S(1)} fusion(bf16[2048,2048]{1,0:T(8,128)(2,1)} %param.3, bf16[64,2048]{1,0:T(8,128)(2,1)S(1)} %collective-permute-done.4, bf16[64,2048]{1,0:T(8,128)(2,1)S(1)} %collective-permute-done.3, bf16[64,2048]{1,0:T(8,128)(2,1)S(1)} %maximum_select_fusion.1), kind=kOutput, calls=%fused_computation.3 | convolution fusion | flops 1613365248 | bytes 9961472 | tf_op jit(solution)/shard_map/dot_general | solution.py:64
  33.2 0.1 fusion.30
  33.3 0.5 collective-permute-start.8
  33.8 0.9 %collective-permute-start.7 = (bf16[64,2048]{1,0:T(8,128)(2,1)S(1)}, bf16[64,2048]{1,0:T(8,128)(2,1)S(1)}, u32[]{:S(2)}, u32[]{:S(2)}) collective-permute-start(bf16[64,2048]{1,0:T(8,128)(2,1)S(1)} %collective-permute-done.6), channel_id=1, source_target_pairs={{0,8},{1,9},{2,10},{3,11},{4,12},{5,13},{6,14},{7,15},{8,0},{9,1},... | collective-permute-start | bytes 786440 | tf_op jit(solution)/shard_map/ppermute | solution.py:18
  34.8 3.7 %collective-permute-start.9 = (bf16[32,2048]{1,0:T(8,128)(2,1)S(1)}, bf16[32,2048]{1,0:T(8,128)(2,1)S(1)}, u32[]{:S(2)}, u32[]{:S(2)}) collective-permute-start(bf16[32,2048]{1,0:T(8,128)(2,1)S(1)} %constant_dynamic-slice_fusion.17), channel_id=1, source_target_pairs={{0,32},{1,33},{2,34},{3,35},{4,36},{5,37},{6,38},{7,39},{8,104},{9... | collective-permute-start | bytes 393224 | tf_op jit(solution)/shard_map/ppermute | solution.py:18
  38.5 1.5 %collective-permute-done.13 = bf16[64,2048]{1,0:T(8,128)(2,1)S(1)} collective-permute-done((bf16[64,2048]{1,0:T(8,128)(2,1)S(1)}, bf16[64,2048]{1,0:T(8,128)(2,1)S(1)}, u32[]{:S(2)}, u32[]{:S(2)}) %collective-permute-start.13) | collective-permute-done | bytes 262176 | tf_op jit(solution)/shard_map/ppermute | solution.py:18
  40.0 0.1 collective-permute-start.11
  40.1 0.1 constant_dynamic-slice_fusion.15
  40.3 2.4 %convolution_convert_fusion.2 = bf16[256,2048]{1,0:T(8,128)(2,1)S(1)} fusion(bf16[2048,2048]{1,0:T(8,128)(2,1)S(1)} %bitcast.19, bf16[64,2048]{1,0:T(8,128)(2,1)S(1)} %get-tuple-element.51, bf16[64,2048]{1,0:T(8,128)(2,1)S(1)} %get-tuple-element.52, bf16[64,2048]{1,0:T(8,128)(2,1)S(1)} %get-tuple-element.53, bf16[64,2048]{1,0:T(8,128)(2,1)S(1)} %get-tuple-element.50), kind=kOutput, calls=%fused_computation.2 | convolution fusion | flops 2152202240 | bytes 10485760 | tf_op jit(solution)/shard_map/dot_general | solution.py:64
  42.7 0.1 fusion.29
  42.8 0.2 collective-permute-done.9
  43.0 3.1 %collective-permute-done.11 = bf16[32,2048]{1,0:T(8,128)(2,1)S(1)} collective-permute-done((bf16[32,2048]{1,0:T(8,128)(2,1)S(1)}, bf16[32,2048]{1,0:T(8,128)(2,1)S(1)}, u32[]{:S(2)}, u32[]{:S(2)}) %collective-permute-start.11) | collective-permute-done | bytes 131104 | tf_op jit(solution)/shard_map/ppermute | solution.py:18
  46.2 1.6 %collective-permute-start.25 = (bf16[128,2048]{1,0:T(8,128)(2,1)S(1)}, bf16[128,2048]{1,0:T(8,128)(2,1)S(1)}, u32[]{:S(2)}, u32[]{:S(2)}) collective-permute-start(bf16[128,2048]{1,0:T(8,128)(2,1)S(1)} %get-tuple-element.49), channel_id=1, source_target_pairs={{0,1},{1,0},{2,3},{3,2},{4,5},{5,4},{6,7},{7,6},{8,11},{9,10},{10,... | collective-permute-start | bytes 1572872 | tf_op jit(solution)/shard_map/ppermute | solution.py:18
  47.8 1.5 %collective-permute-start.14 = (bf16[32,2048]{1,0:T(8,128)(2,1)S(1)}, bf16[32,2048]{1,0:T(8,128)(2,1)S(1)}, u32[]{:S(2)}, u32[]{:S(2)}) collective-permute-start(bf16[32,2048]{1,0:T(8,128)(2,1)S(1)} %collective-permute-done.9), channel_id=1, source_target_pairs={{0,8},{1,9},{2,10},{3,11},{4,12},{5,13},{6,14},{7,15},{8,0},{9,1},... | collective-permute-start | bytes 393224 | tf_op jit(solution)/shard_map/ppermute | solution.py:18
  49.3 0.1 constant_dynamic-slice_fusion.11
  49.4 2.4 %convolution_convert_fusion.1 = bf16[256,2048]{1,0:T(8,128)(2,1)S(1)} fusion(bf16[2048,2048]{1,0:T(8,128)(2,1)S(1)} %bitcast.19, bf16[64,2048]{1,0:T(8,128)(2,1)S(1)} %get-tuple-element.45, bf16[64,2048]{1,0:T(8,128)(2,1)S(1)} %get-tuple-element.46, bf16[64,2048]{1,0:T(8,128)(2,1)S(1)} %get-tuple-element.47, bf16[64,2048]{1,0:T(8,128)(2,1)S(1)} %get-tuple-element.44), kind=kOutput, calls=%fused_computation.1 | convolution fusion | flops 2152202240 | bytes 10485760 | tf_op jit(solution)/shard_map/dot_general | solution.py:64
  51.8 0.1 fusion.28
  51.9 0.3 collective-permute-start.27
  52.3 0.1 pad_maximum_fusion
  52.7 2.9 %convolution_convert_fusion = bf16[320,2048]{1,0:T(8,128)(2,1)S(1)} fusion(bf16[320,2048]{1,0:T(8,128)(2,1)S(1)} %fusion.20, bf16[2048,2048]{1,0:T(8,128)(2,1)S(1)} %bitcast.19), kind=kOutput, calls=%fused_computation | convolution fusion | flops 2685009920 | bytes 11010048 | tf_op jit(solution)/shard_map/dot_general | solution.py:64
  55.6 0.1 fusion.27
  55.7 0.1 pad_maximum_fusion.1
  55.8 0.1 constant_dynamic-slice_fusion.7
  55.9 0.1 broadcast_select_fusion
  56.0 1.6 %collective-permute-start.22 = (bf16[128,2048]{1,0:T(8,128)(2,1)S(1)}, bf16[128,2048]{1,0:T(8,128)(2,1)S(1)}, u32[]{:S(2)}, u32[]{:S(2)}) collective-permute-start(bf16[128,2048]{1,0:T(8,128)(2,1)S(1)} %broadcast_select_fusion), channel_id=1, source_target_pairs={{0,4},{1,5},{2,6},{3,7},{4,0},{5,1},{6,2},{7,3},{8,12},{9,13},{10,... | collective-permute-start | bytes 1572872 | tf_op jit(solution)/shard_map/ppermute | solution.py:18
  57.6 1.9 %collective-permute-start.19 = (bf16[128,2048]{1,0:T(8,128)(2,1)S(1)}, bf16[128,2048]{1,0:T(8,128)(2,1)S(1)}, u32[]{:S(2)}, u32[]{:S(2)}) collective-permute-start(bf16[128,2048]{1,0:T(8,128)(2,1)S(1)} %pad_maximum_fusion.2), channel_id=1, source_target_pairs={{0,1},{1,0},{2,3},{3,2},{4,5},{5,4},{6,7},{7,6},{8,11},{9,10},{10,... | collective-permute-start | bytes 1572872 | tf_op jit(solution)/shard_map/ppermute | solution.py:18
  59.5 0.1 convert_add_fusion.1
  59.7 1.2 %collective-permute-start.26 = (bf16[64,2048]{1,0:T(8,128)(2,1)S(1)}, bf16[64,2048]{1,0:T(8,128)(2,1)S(1)}, u32[]{:S(2)}, u32[]{:S(2)}) collective-permute-start(bf16[64,2048]{1,0:T(8,128)(2,1)S(1)} %slice.170), channel_id=1, source_target_pairs={{0,3},{1,2},{2,1},{3,0},{4,7},{5,6},{6,5},{7,4},{8,9},{9,8},{10,11... | collective-permute-start | bytes 786440 | tf_op jit(solution)/shard_map/ppermute | solution.py:18
  60.9 0.3 collective-permute-done.27
  61.2 0.1 convert_add_fusion
  61.4 2.7 %collective-permute-start.28 = (bf16[64,2048]{1,0:T(8,128)(2,1)S(1)}, bf16[64,2048]{1,0:T(8,128)(2,1)S(1)}, u32[]{:S(2)}, u32[]{:S(2)}) collective-permute-start(bf16[64,2048]{1,0:T(8,128)(2,1)S(1)} %slice.169), channel_id=1, source_target_pairs={{0,3},{1,2},{2,1},{3,0},{4,7},{5,6},{6,5},{7,4},{8,9},{9,8},{10,11... | collective-permute-start | bytes 786440 | tf_op jit(solution)/shard_map/ppermute | solution.py:18
  64.1 6.8 %collective-permute-done.22 = bf16[128,2048]{1,0:T(8,128)(2,1)S(1)} collective-permute-done((bf16[128,2048]{1,0:T(8,128)(2,1)S(1)}, bf16[128,2048]{1,0:T(8,128)(2,1)S(1)}, u32[]{:S(2)}, u32[]{:S(2)}) %collective-permute-start.22) | collective-permute-done | bytes 524320 | tf_op jit(solution)/shard_map/ppermute | solution.py:18
  70.9 0.2 convert_add_fusion.2
  71.2 0.5 collective-permute-start.23
  71.7 0.1 fusion.26
  71.9 3.2 %collective-permute-start.20 = (bf16[64,2048]{1,0:T(8,128)(2,1)S(1)}, bf16[64,2048]{1,0:T(8,128)(2,1)S(1)}, u32[]{:S(2)}, u32[]{:S(2)}) collective-permute-start(bf16[64,2048]{1,0:T(8,128)(2,1)S(1)} %pad_maximum_fusion.4), channel_id=1, source_target_pairs={{0,3},{1,2},{2,1},{3,0},{4,7},{5,6},{6,5},{7,4},{8,9},{9,8},{10,11... | collective-permute-start | bytes 786440 | tf_op jit(solution)/shard_map/ppermute | solution.py:18
  75.1 0.1 select_convert_fusion
  75.2 1.6 %collective-permute-start.29 = (bf16[64,2048]{1,0:T(8,128)(2,1)S(1)}, bf16[64,2048]{1,0:T(8,128)(2,1)S(1)}, u32[]{:S(2)}, u32[]{:S(2)}) collective-permute-start(bf16[64,2048]{1,0:T(8,128)(2,1)S(1)} %select_convert_fusion), channel_id=1, source_target_pairs={{0,4},{1,5},{2,6},{3,7},{4,0},{5,1},{6,2},{7,3},{8,12},{9,13},{10,... | collective-permute-start | bytes 786440 | tf_op jit(solution)/shard_map/ppermute | solution.py:18
  76.9 3.7 %collective-permute-done.20 = bf16[64,2048]{1,0:T(8,128)(2,1)S(1)} collective-permute-done((bf16[64,2048]{1,0:T(8,128)(2,1)S(1)}, bf16[64,2048]{1,0:T(8,128)(2,1)S(1)}, u32[]{:S(2)}, u32[]{:S(2)}) %collective-permute-start.20) | collective-permute-done | bytes 262176 | tf_op jit(solution)/shard_map/ppermute | solution.py:18
  80.6 0.1 select_convert_fusion.1
  80.7 1.4 %collective-permute-start.21 = (bf16[32,2048]{1,0:T(8,128)(2,1)S(1)}, bf16[32,2048]{1,0:T(8,128)(2,1)S(1)}, u32[]{:S(2)}, u32[]{:S(2)}) collective-permute-start(bf16[32,2048]{1,0:T(8,128)(2,1)S(1)} %select_convert_fusion.1), channel_id=1, source_target_pairs={{0,4},{1,5},{2,6},{3,7},{4,0},{5,1},{6,2},{7,3},{8,12},{9,13},{10,... | collective-permute-start | bytes 393224 | tf_op jit(solution)/shard_map/ppermute | solution.py:18
  82.0 0.1 slice_add_fusion.2
  82.1 2.6 %collective-permute-start.24 = (bf16[32,2048]{1,0:T(8,128)(2,1)S(1)}, bf16[32,2048]{1,0:T(8,128)(2,1)S(1)}, u32[]{:S(2)}, u32[]{:S(2)}) collective-permute-start(bf16[32,2048]{1,0:T(8,128)(2,1)S(1)} %slice.172), channel_id=1, source_target_pairs={{0,3},{1,2},{2,1},{3,0},{4,7},{5,6},{6,5},{7,4},{8,9},{9,8},{10,11... | collective-permute-start | bytes 393224 | tf_op jit(solution)/shard_map/ppermute | solution.py:18
  84.7 1.4 %collective-permute-done.21 = bf16[32,2048]{1,0:T(8,128)(2,1)S(1)} collective-permute-done((bf16[32,2048]{1,0:T(8,128)(2,1)S(1)}, bf16[32,2048]{1,0:T(8,128)(2,1)S(1)}, u32[]{:S(2)}, u32[]{:S(2)}) %collective-permute-start.21) | collective-permute-done | bytes 131104 | tf_op jit(solution)/shard_map/ppermute | solution.py:18
  86.1 0.1 convert_add_fusion.5
  86.2 2.2 %collective-permute-done.24 = bf16[32,2048]{1,0:T(8,128)(2,1)S(1)} collective-permute-done((bf16[32,2048]{1,0:T(8,128)(2,1)S(1)}, bf16[32,2048]{1,0:T(8,128)(2,1)S(1)}, u32[]{:S(2)}, u32[]{:S(2)}) %collective-permute-start.24) | collective-permute-done | bytes 131104 | tf_op jit(solution)/shard_map/ppermute | solution.py:18
  88.4 0.2 convert_add_fusion.4
  88.6 1.1 %maximum_select_fusion = f32[128,2048]{1,0:T(8,128)} fusion(f32[64,2048]{1,0:T(8,128)S(1)} %convert_add_fusion.4, f32[32,2048]{1,0:T(8,128)S(1)} %slice_add_fusion.3, f32[32,2048]{1,0:T(8,128)S(1)} %convert_add_fusion.5, pred[]{:T(512)S(6)} %eq.114), kind=kLoop, calls=%fused_computation.22 | loop fusion | flops 1310720 | bytes 2097153 | tf_op jit(solution)/shard_map/jit(_where)/select_n | solution.py:174
  (59 shorter events, 0.8 us)
Async XLA Ops:
  0.0 1.6 %copy-start = (bf16[4,512,512]{2,1,0:T(8,128)(2,1)S(1)}, bf16[4,512,512]{2,1,0:T(8,128)(2,1)}, u32[]{:S(2)}) copy-start(bf16[4,512,512]{2,1,0:T(8,128)(2,1)} %param.5) | copy-start | bytes 6291460
  3.0 1.4 %collective-permute-start = (bf16[32,2048]{1,0:T(8,128)(2,1)S(1)}, bf16[32,2048]{1,0:T(8,128)(2,1)S(1)}, u32[]{:S(2)}, u32[]{:S(2)}) collective-permute-start(bf16[32,2048]{1,0:T(8,128)(2,1)S(1)} %bitcast.14), channel_id=1, source_target_pairs={{0,8},{1,9},{2,10},{3,11},{4,12},{5,13},{6,14},{7,15},{8,0},{9,1},... | collective-permute-start | bytes 393224 | tf_op jit(solution)/shard_map/ppermute | solution.py:18
  4.4 10.3 %collective-permute-start.2 = (bf16[64,2048]{1,0:T(8,128)(2,1)S(1)}, bf16[64,2048]{1,0:T(8,128)(2,1)S(1)}, u32[]{:S(2)}, u32[]{:S(2)}) collective-permute-start(bf16[64,2048]{1,0:T(8,128)(2,1)S(1)} %maximum_select_fusion.1), channel_id=1, source_target_pairs={{0,16},{1,17},{2,18},{3,19},{4,20},{5,21},{6,22},{7,23},{8,120},{9... | collective-permute-start | bytes 786440 | tf_op jit(solution)/shard_map/ppermute | solution.py:18
  6.4 6.5 %collective-permute-start.1 = (bf16[32,2048]{1,0:T(8,128)(2,1)S(1)}, bf16[32,2048]{1,0:T(8,128)(2,1)S(1)}, u32[]{:S(2)}, u32[]{:S(2)}) collective-permute-start(bf16[32,2048]{1,0:T(8,128)(2,1)S(1)} %bitcast.16), channel_id=1, source_target_pairs={{0,128},{1,129},{2,130},{3,131},{4,132},{5,133},{6,134},{7,135},{8... | collective-permute-start | bytes 393224 | tf_op jit(solution)/shard_map/ppermute | solution.py:18
  14.7 1.8 %collective-permute-start.5 = (bf16[32,2048]{1,0:T(8,128)(2,1)S(1)}, bf16[32,2048]{1,0:T(8,128)(2,1)S(1)}, u32[]{:S(2)}, u32[]{:S(2)}) collective-permute-start(bf16[32,2048]{1,0:T(8,128)(2,1)S(1)} %collective-permute-done.1), channel_id=1, source_target_pairs={{0,8},{1,9},{2,10},{3,11},{4,12},{5,13},{6,14},{7,15},{8,0},{9,1},... | collective-permute-start | bytes 393224 | tf_op jit(solution)/shard_map/ppermute | solution.py:18
  15.6 9.3 %collective-permute-start.12 = (bf16[64,2048]{1,0:T(8,128)(2,1)S(1)}, bf16[64,2048]{1,0:T(8,128)(2,1)S(1)}, u32[]{:S(2)}, u32[]{:S(2)}) collective-permute-start(bf16[64,2048]{1,0:T(8,128)(2,1)S(1)} %collective-permute-done.2), channel_id=1, source_target_pairs={{0,8},{1,9},{2,10},{3,11},{4,12},{5,13},{6,14},{7,15},{8,0},{9,1},... | collective-permute-start | bytes 786440 | tf_op jit(solution)/shard_map/ppermute | solution.py:18
  15.6 7.6 %collective-permute-start.3 = (bf16[64,2048]{1,0:T(8,128)(2,1)S(1)}, bf16[64,2048]{1,0:T(8,128)(2,1)S(1)}, u32[]{:S(2)}, u32[]{:S(2)}) collective-permute-start(bf16[64,2048]{1,0:T(8,128)(2,1)S(1)} %collective-permute-done.2), channel_id=1, source_target_pairs={{0,16},{1,17},{2,18},{3,19},{4,20},{5,21},{6,22},{7,23},{8,120},{9... | collective-permute-start | bytes 786440 | tf_op jit(solution)/shard_map/ppermute | solution.py:18
  16.6 9.4 %collective-permute-start.15 = (bf16[64,2048]{1,0:T(8,128)(2,1)S(1)}, bf16[64,2048]{1,0:T(8,128)(2,1)S(1)}, u32[]{:S(2)}, u32[]{:S(2)}) collective-permute-start(bf16[64,2048]{1,0:T(8,128)(2,1)S(1)} %maximum_select_fusion.2), channel_id=1, source_target_pairs={{0,16},{1,17},{2,18},{3,19},{4,20},{5,21},{6,22},{7,23},{8,120},{9... | collective-permute-start | bytes 786440 | tf_op jit(solution)/shard_map/ppermute | solution.py:18
  17.4 15.9 %collective-permute-start.6 = (bf16[64,2048]{1,0:T(8,128)(2,1)S(1)}, bf16[64,2048]{1,0:T(8,128)(2,1)S(1)}, u32[]{:S(2)}, u32[]{:S(2)}) collective-permute-start(bf16[64,2048]{1,0:T(8,128)(2,1)S(1)} %maximum_select_fusion.2), channel_id=1, source_target_pairs={{0,32},{1,33},{2,34},{3,35},{4,36},{5,37},{6,38},{7,39},{8,104},{9... | collective-permute-start | bytes 786440 | tf_op jit(solution)/shard_map/ppermute | solution.py:18
  23.2 15.3 %collective-permute-start.10 = (bf16[64,2048]{1,0:T(8,128)(2,1)S(1)}, bf16[64,2048]{1,0:T(8,128)(2,1)S(1)}, u32[]{:S(2)}, u32[]{:S(2)}) collective-permute-start(bf16[64,2048]{1,0:T(8,128)(2,1)S(1)} %collective-permute-done.3), channel_id=1, source_target_pairs={{0,16},{1,17},{2,18},{3,19},{4,20},{5,21},{6,22},{7,23},{8,120},{9... | collective-permute-start | bytes 786440 | tf_op jit(solution)/shard_map/ppermute | solution.py:18
  23.2 3.6 %collective-permute-start.4 = (bf16[64,2048]{1,0:T(8,128)(2,1)S(1)}, bf16[64,2048]{1,0:T(8,128)(2,1)S(1)}, u32[]{:S(2)}, u32[]{:S(2)}) collective-permute-start(bf16[64,2048]{1,0:T(8,128)(2,1)S(1)} %collective-permute-done.3), channel_id=1, source_target_pairs={{0,8},{1,9},{2,10},{3,11},{4,12},{5,13},{6,14},{7,15},{8,0},{9,1},... | collective-permute-start | bytes 786440 | tf_op jit(solution)/shard_map/ppermute | solution.py:18
  26.0 20.2 %collective-permute-start.16 = (bf16[64,2048]{1,0:T(8,128)(2,1)S(1)}, bf16[64,2048]{1,0:T(8,128)(2,1)S(1)}, u32[]{:S(2)}, u32[]{:S(2)}) collective-permute-start(bf16[64,2048]{1,0:T(8,128)(2,1)S(1)} %collective-permute-done.15), channel_id=1, source_target_pairs={{0,8},{1,9},{2,10},{3,11},{4,12},{5,13},{6,14},{7,15},{8,0},{9,1},... | collective-permute-start | bytes 786440 | tf_op jit(solution)/shard_map/ppermute | solution.py:18
  26.7 13.5 %slice-start = ((s8[8388608]{0:T(1024)(128)(4,1)}), s8[4194304]{0:T(1024)(128)(4,1)S(1)}, s32[]{:S(2)}) async-start(s8[8388608]{0:T(1024)(128)(4,1)} %bitcast.18), calls=%async_computation | async-start | bytes 8388608
  26.8 13.5 %slice-start.1 = ((s8[8388608]{0:T(1024)(128)(4,1)}), s8[4194304]{0:T(1024)(128)(4,1)S(1)}, s32[]{:S(2)}) async-start(s8[8388608]{0:T(1024)(128)(4,1)} %bitcast.18), calls=%async_computation.1 | async-start | bytes 8388608
  33.3 12.8 %collective-permute-start.8 = (bf16[64,2048]{1,0:T(8,128)(2,1)S(1)}, bf16[64,2048]{1,0:T(8,128)(2,1)S(1)}, u32[]{:S(2)}, u32[]{:S(2)}) collective-permute-start(bf16[64,2048]{1,0:T(8,128)(2,1)S(1)} %collective-permute-done.6), channel_id=1, source_target_pairs={{0,16},{1,17},{2,18},{3,19},{4,20},{5,21},{6,22},{7,23},{8,120},{9... | collective-permute-start | bytes 786440 | tf_op jit(solution)/shard_map/ppermute | solution.py:18
  33.8 18.5 %collective-permute-start.7 = (bf16[64,2048]{1,0:T(8,128)(2,1)S(1)}, bf16[64,2048]{1,0:T(8,128)(2,1)S(1)}, u32[]{:S(2)}, u32[]{:S(2)}) collective-permute-start(bf16[64,2048]{1,0:T(8,128)(2,1)S(1)} %collective-permute-done.6), channel_id=1, source_target_pairs={{0,8},{1,9},{2,10},{3,11},{4,12},{5,13},{6,14},{7,15},{8,0},{9,1},... | collective-permute-start | bytes 786440 | tf_op jit(solution)/shard_map/ppermute | solution.py:18
  34.8 8.3 %collective-permute-start.9 = (bf16[32,2048]{1,0:T(8,128)(2,1)S(1)}, bf16[32,2048]{1,0:T(8,128)(2,1)S(1)}, u32[]{:S(2)}, u32[]{:S(2)}) collective-permute-start(bf16[32,2048]{1,0:T(8,128)(2,1)S(1)} %constant_dynamic-slice_fusion.17), channel_id=1, source_target_pairs={{0,32},{1,33},{2,34},{3,35},{4,36},{5,37},{6,38},{7,39},{8,104},{9... | collective-permute-start | bytes 393224 | tf_op jit(solution)/shard_map/ppermute | solution.py:18
  38.4 1.5 %collective-permute-start.13 = (bf16[64,2048]{1,0:T(8,128)(2,1)S(1)}, bf16[64,2048]{1,0:T(8,128)(2,1)S(1)}, u32[]{:S(2)}, u32[]{:S(2)}) collective-permute-start(bf16[64,2048]{1,0:T(8,128)(2,1)S(1)} %collective-permute-done.10), channel_id=1, source_target_pairs={{0,8},{1,9},{2,10},{3,11},{4,12},{5,13},{6,14},{7,15},{8,0},{9,1},... | collective-permute-start | bytes 786440 | tf_op jit(solution)/shard_map/ppermute | solution.py:18
  40.0 6.2 %collective-permute-start.11 = (bf16[32,2048]{1,0:T(8,128)(2,1)S(1)}, bf16[32,2048]{1,0:T(8,128)(2,1)S(1)}, u32[]{:S(2)}, u32[]{:S(2)}) collective-permute-start(bf16[32,2048]{1,0:T(8,128)(2,1)S(1)} %constant_dynamic-slice_fusion.16), channel_id=1, source_target_pairs={{0,16},{1,17},{2,18},{3,19},{4,20},{5,21},{6,22},{7,23},{8,120},{9... | collective-permute-start | bytes 393224 | tf_op jit(solution)/shard_map/ppermute | solution.py:18
  46.2 3.1 %collective-permute-start.17 = (bf16[64,2048]{1,0:T(8,128)(2,1)S(1)}, bf16[64,2048]{1,0:T(8,128)(2,1)S(1)}, u32[]{:S(2)}, u32[]{:S(2)}) collective-permute-start(bf16[64,2048]{1,0:T(8,128)(2,1)S(1)} %collective-permute-done.8), channel_id=1, source_target_pairs={{0,8},{1,9},{2,10},{3,11},{4,12},{5,13},{6,14},{7,15},{8,0},{9,1},... | collective-permute-start | bytes 786440 | tf_op jit(solution)/shard_map/ppermute | solution.py:18
  46.2 13.3 %collective-permute-start.25 = (bf16[128,2048]{1,0:T(8,128)(2,1)S(1)}, bf16[128,2048]{1,0:T(8,128)(2,1)S(1)}, u32[]{:S(2)}, u32[]{:S(2)}) collective-permute-start(bf16[128,2048]{1,0:T(8,128)(2,1)S(1)} %get-tuple-element.49), channel_id=1, source_target_pairs={{0,1},{1,0},{2,3},{3,2},{4,5},{5,4},{6,7},{7,6},{8,11},{9,10},{10,... | collective-permute-start | bytes 1572872 | tf_op jit(solution)/shard_map/ppermute | solution.py:18
  47.8 4.5 %collective-permute-start.14 = (bf16[32,2048]{1,0:T(8,128)(2,1)S(1)}, bf16[32,2048]{1,0:T(8,128)(2,1)S(1)}, u32[]{:S(2)}, u32[]{:S(2)}) collective-permute-start(bf16[32,2048]{1,0:T(8,128)(2,1)S(1)} %collective-permute-done.9), channel_id=1, source_target_pairs={{0,8},{1,9},{2,10},{3,11},{4,12},{5,13},{6,14},{7,15},{8,0},{9,1},... | collective-permute-start | bytes 393224 | tf_op jit(solution)/shard_map/ppermute | solution.py:18
  49.3 3.4 %collective-permute-start.18 = (bf16[32,2048]{1,0:T(8,128)(2,1)S(1)}, bf16[32,2048]{1,0:T(8,128)(2,1)S(1)}, u32[]{:S(2)}, u32[]{:S(2)}) collective-permute-start(bf16[32,2048]{1,0:T(8,128)(2,1)S(1)} %collective-permute-done.11), channel_id=1, source_target_pairs={{0,8},{1,9},{2,10},{3,11},{4,12},{5,13},{6,14},{7,15},{8,0},{9,1},... | collective-permute-start | bytes 393224 | tf_op jit(solution)/shard_map/ppermute | solution.py:18
  51.9 9.3 %collective-permute-start.27 = (bf16[128,2048]{1,0:T(8,128)(2,1)S(1)}, bf16[128,2048]{1,0:T(8,128)(2,1)S(1)}, u32[]{:S(2)}, u32[]{:S(2)}) collective-permute-start(bf16[128,2048]{1,0:T(8,128)(2,1)S(1)} %get-tuple-element.43), channel_id=1, source_target_pairs={{0,1},{1,0},{2,3},{3,2},{4,5},{5,4},{6,7},{7,6},{8,11},{9,10},{10,... | collective-permute-start | bytes 1572872 | tf_op jit(solution)/shard_map/ppermute | solution.py:18
  56.0 14.9 %collective-permute-start.22 = (bf16[128,2048]{1,0:T(8,128)(2,1)S(1)}, bf16[128,2048]{1,0:T(8,128)(2,1)S(1)}, u32[]{:S(2)}, u32[]{:S(2)}) collective-permute-start(bf16[128,2048]{1,0:T(8,128)(2,1)S(1)} %broadcast_select_fusion), channel_id=1, source_target_pairs={{0,4},{1,5},{2,6},{3,7},{4,0},{5,1},{6,2},{7,3},{8,12},{9,13},{10,... | collective-permute-start | bytes 1572872 | tf_op jit(solution)/shard_map/ppermute | solution.py:18
  57.6 14.1 %collective-permute-start.19 = (bf16[128,2048]{1,0:T(8,128)(2,1)S(1)}, bf16[128,2048]{1,0:T(8,128)(2,1)S(1)}, u32[]{:S(2)}, u32[]{:S(2)}) collective-permute-start(bf16[128,2048]{1,0:T(8,128)(2,1)S(1)} %pad_maximum_fusion.2), channel_id=1, source_target_pairs={{0,1},{1,0},{2,3},{3,2},{4,5},{5,4},{6,7},{7,6},{8,11},{9,10},{10,... | collective-permute-start | bytes 1572872 | tf_op jit(solution)/shard_map/ppermute | solution.py:18
  59.7 15.4 %collective-permute-start.26 = (bf16[64,2048]{1,0:T(8,128)(2,1)S(1)}, bf16[64,2048]{1,0:T(8,128)(2,1)S(1)}, u32[]{:S(2)}, u32[]{:S(2)}) collective-permute-start(bf16[64,2048]{1,0:T(8,128)(2,1)S(1)} %slice.170), channel_id=1, source_target_pairs={{0,3},{1,2},{2,1},{3,0},{4,7},{5,6},{6,5},{7,4},{8,9},{9,8},{10,11... | collective-permute-start | bytes 786440 | tf_op jit(solution)/shard_map/ppermute | solution.py:18
  61.4 13.7 %collective-permute-start.28 = (bf16[64,2048]{1,0:T(8,128)(2,1)S(1)}, bf16[64,2048]{1,0:T(8,128)(2,1)S(1)}, u32[]{:S(2)}, u32[]{:S(2)}) collective-permute-start(bf16[64,2048]{1,0:T(8,128)(2,1)S(1)} %slice.169), channel_id=1, source_target_pairs={{0,3},{1,2},{2,1},{3,0},{4,7},{5,6},{6,5},{7,4},{8,9},{9,8},{10,11... | collective-permute-start | bytes 786440 | tf_op jit(solution)/shard_map/ppermute | solution.py:18
  71.2 10.9 %collective-permute-start.23 = (bf16[64,2048]{1,0:T(8,128)(2,1)S(1)}, bf16[64,2048]{1,0:T(8,128)(2,1)S(1)}, u32[]{:S(2)}, u32[]{:S(2)}) collective-permute-start(bf16[64,2048]{1,0:T(8,128)(2,1)S(1)} %slice.171), channel_id=1, source_target_pairs={{0,1},{1,0},{2,3},{3,2},{4,5},{5,4},{6,7},{7,6},{8,11},{9,10},{10,... | collective-permute-start | bytes 786440 | tf_op jit(solution)/shard_map/ppermute | solution.py:18
  71.9 8.7 %collective-permute-start.20 = (bf16[64,2048]{1,0:T(8,128)(2,1)S(1)}, bf16[64,2048]{1,0:T(8,128)(2,1)S(1)}, u32[]{:S(2)}, u32[]{:S(2)}) collective-permute-start(bf16[64,2048]{1,0:T(8,128)(2,1)S(1)} %pad_maximum_fusion.4), channel_id=1, source_target_pairs={{0,3},{1,2},{2,1},{3,0},{4,7},{5,6},{6,5},{7,4},{8,9},{9,8},{10,11... | collective-permute-start | bytes 786440 | tf_op jit(solution)/shard_map/ppermute | solution.py:18
  75.2 13.2 %collective-permute-start.29 = (bf16[64,2048]{1,0:T(8,128)(2,1)S(1)}, bf16[64,2048]{1,0:T(8,128)(2,1)S(1)}, u32[]{:S(2)}, u32[]{:S(2)}) collective-permute-start(bf16[64,2048]{1,0:T(8,128)(2,1)S(1)} %select_convert_fusion), channel_id=1, source_target_pairs={{0,4},{1,5},{2,6},{3,7},{4,0},{5,1},{6,2},{7,3},{8,12},{9,13},{10,... | collective-permute-start | bytes 786440 | tf_op jit(solution)/shard_map/ppermute | solution.py:18
  80.7 5.4 %collective-permute-start.21 = (bf16[32,2048]{1,0:T(8,128)(2,1)S(1)}, bf16[32,2048]{1,0:T(8,128)(2,1)S(1)}, u32[]{:S(2)}, u32[]{:S(2)}) collective-permute-start(bf16[32,2048]{1,0:T(8,128)(2,1)S(1)} %select_convert_fusion.1), channel_id=1, source_target_pairs={{0,4},{1,5},{2,6},{3,7},{4,0},{5,1},{6,2},{7,3},{8,12},{9,13},{10,... | collective-permute-start | bytes 393224 | tf_op jit(solution)/shard_map/ppermute | solution.py:18
  82.1 6.3 %collective-permute-start.24 = (bf16[32,2048]{1,0:T(8,128)(2,1)S(1)}, bf16[32,2048]{1,0:T(8,128)(2,1)S(1)}, u32[]{:S(2)}, u32[]{:S(2)}) collective-permute-start(bf16[32,2048]{1,0:T(8,128)(2,1)S(1)} %slice.172), channel_id=1, source_target_pairs={{0,3},{1,2},{2,1},{3,0},{4,7},{5,6},{6,5},{7,4},{8,9},{9,8},{10,11... | collective-permute-start | bytes 393224 | tf_op jit(solution)/shard_map/ppermute | solution.py:18

commit v4 on v3

--- a/solution.py
+++ b/solution.py
@@ -115,18 +115,20 @@
         return jnp.where(step == 0, 0, jnp.where(step == 4, 3, jnp.where(own, 1, 2)))
 
     mine, plane = together(mine, plane)
-    across, o1 = together(other_half(mine), along_z(plane))
+    across = other_half(mine)
+    theirs = other_core(across)
+    across, o1 = together(across, along_z(plane))
     o2 = along_z(o1)
-    a0 = both_cores(c, across, other_core(across))
+    a0 = both_cores(c, across, theirs)
     t1, t2 = other_core(o1), other_core(o2)
     known = scores(jnp.concatenate([plane, o2, t2]))
     known = [known[:rows], known[rows : 2 * rows], known[2 * rows :]]
-    a1 = along_z(a0)
+    a1, known[0] = together(along_z(a0), known[0])
     a2, known[1] = together(along_z_twice(a0), known[1])
     o3 = along_z(o2)
     a3 = along_z(a2)
     a4 = along_z_twice(own_rows(a2))
-    o4 = along_z(own_rows(o3))
+    o4 = along_z_twice(own_rows(o2))
     t3 = other_core(o3)
     odd = scores(picked(odd_place, 1, o1, t1, o3, t3))
     odd_come, odd = first_x(odd[: 2 * rows]), odd[2 * rows :]

time: 89.8 us -> 89.6 us (level)
  starting transfers between devices: 35.6 us -> 31.7 us
  waiting for transfers between devices: 32.7 us -> 36.5 us
    ppermute x30, starting transfers between devices: 35.6 us -> 31.7 us  [move(): return lax.ppermute(value, NAMES, pairs)]
    ppermute x30, waiting for transfers between devices: 32.7 us -> 36.5 us  [move(): return lax.ppermute(value, NAMES, pairs)]
  transfers between devices with their start and end apart: 30 -> 30, of which waited for: 14 -> 12; matrix products, arithmetic and copies ran while one was open for 19% -> 19% of each run, Pallas kernels for 0% -> 0%
where the time goes in v4:
time: 89.6 us; the launch traced here: 89.5 us
  waiting for transfers between devices  36.5 us (41%)
  starting transfers between devices  31.7 us (35%)
  matrix products  15.4 us (17%)
  local copies, waits for them, and re-layouts  2.71 us (3%)
  other arithmetic  2.65 us (3%)
    ppermute x30, waiting for transfers between devices, move(): return lax.ppermute(value, NAMES, pairs)  36.5 us
    ppermute x30, starting transfers between devices, move(): return lax.ppermute(value, NAMES, pairs)  31.7 us
    dot_general x4, matrix products, score_rows(): lax.dot_general(ready, train_grads, (((1,), (1,)), ((), ())), preferred_e...  14.1 us
    unnamed x20, local copies, waits for them, and re-layouts  1.86 us
  transfers between devices with their start and end apart: 30, of which 12 were waited for; matrix products, arithmetic and copies ran while one was open for 19% of the time, Pallas kernels for 0%

profile of v4, /device:TPU:16, one launch (start us, length us, event | category | flops | bytes accessed | tf_op | source)
XLA Modules:
  0.0 89.5 jit_solution(778412796462306077)
XLA Ops:
  0.0 1.6 %copy-done = bf16[4,512,512]{2,1,0:T(8,128)(2,1)S(1)} copy-done((bf16[4,512,512]{2,1,0:T(8,128)(2,1)S(1)}, bf16[4,512,512]{2,1,0:T(8,128)(2,1)}, u32[]{:S(2)}) %copy-start) | copy-done | bytes 2097176
  1.6 1.3 %fusion = bf16[4,4,8,512]{3,2,1,0:T(8,128)(2,1)S(1)} fusion(bf16[4,512,512]{2,1,0:T(8,128)(2,1)S(1)} %copy-done, bf16[4,4,8,512]{3,2,1,0:T(8,128)(2,1)} %bitcast.17), kind=kOutput, calls=%fused_computation.5 | convolution fusion | flops 67174400 | bytes 2359296 | tf_op jit(solution)/shard_map/rbi,bij->rbj/dot_general | solution.py:59
  3.0 0.1 collective-permute-start
  3.1 1.3 %collective-permute-done = bf16[32,2048]{1,0:T(8,128)(2,1)S(1)} collective-permute-done((bf16[32,2048]{1,0:T(8,128)(2,1)S(1)}, bf16[32,2048]{1,0:T(8,128)(2,1)S(1)}, u32[]{:S(2)}, u32[]{:S(2)}) %collective-permute-start) | collective-permute-done | bytes 131104 | tf_op jit(solution)/shard_map/ppermute | solution.py:18
  4.4 2.0 %collective-permute-start.2 = (bf16[64,2048]{1,0:T(8,128)(2,1)S(1)}, bf16[64,2048]{1,0:T(8,128)(2,1)S(1)}, u32[]{:S(2)}, u32[]{:S(2)}) collective-permute-start(bf16[64,2048]{1,0:T(8,128)(2,1)S(1)} %maximum_select_fusion.1), channel_id=1, source_target_pairs={{0,16},{1,17},{2,18},{3,19},{4,20},{5,21},{6,22},{7,23},{8,120},{9... | collective-permute-start | bytes 786440 | tf_op jit(solution)/shard_map/ppermute | solution.py:18
  6.4 0.3 collective-permute-start.1
  6.8 6.1 %collective-permute-done.1 = bf16[32,2048]{1,0:T(8,128)(2,1)S(1)} collective-permute-done((bf16[32,2048]{1,0:T(8,128)(2,1)S(1)}, bf16[32,2048]{1,0:T(8,128)(2,1)S(1)}, u32[]{:S(2)}, u32[]{:S(2)}) %collective-permute-start.1) | collective-permute-done | bytes 131104 | tf_op jit(solution)/shard_map/ppermute | solution.py:18
  12.9 2.7 %collective-permute-start.3 = (bf16[32,2048]{1,0:T(8,128)(2,1)S(1)}, bf16[32,2048]{1,0:T(8,128)(2,1)S(1)}, u32[]{:S(2)}, u32[]{:S(2)}) collective-permute-start(bf16[32,2048]{1,0:T(8,128)(2,1)S(1)} %collective-permute-done.1), channel_id=1, source_target_pairs={{0,8},{1,9},{2,10},{3,11},{4,12},{5,13},{6,14},{7,15},{8,0},{9,1},... | collective-permute-start | bytes 393224 | tf_op jit(solution)/shard_map/ppermute | solution.py:18
  15.6 2.9 %collective-permute-start.12 = (bf16[64,2048]{1,0:T(8,128)(2,1)S(1)}, bf16[64,2048]{1,0:T(8,128)(2,1)S(1)}, u32[]{:S(2)}, u32[]{:S(2)}) collective-permute-start(bf16[64,2048]{1,0:T(8,128)(2,1)S(1)} %collective-permute-done.2), channel_id=1, source_target_pairs={{0,8},{1,9},{2,10},{3,11},{4,12},{5,13},{6,14},{7,15},{8,0},{9,1},... | collective-permute-start | bytes 786440 | tf_op jit(solution)/shard_map/ppermute | solution.py:18
  18.6 1.0 %collective-permute-start.7 = (bf16[64,2048]{1,0:T(8,128)(2,1)S(1)}, bf16[64,2048]{1,0:T(8,128)(2,1)S(1)}, u32[]{:S(2)}, u32[]{:S(2)}) collective-permute-start(bf16[64,2048]{1,0:T(8,128)(2,1)S(1)} %maximum_select_fusion.2), channel_id=1, source_target_pairs={{0,32},{1,33},{2,34},{3,35},{4,36},{5,37},{6,38},{7,39},{8,104},{9... | collective-permute-start | bytes 786440 | tf_op jit(solution)/shard_map/ppermute | solution.py:18
  19.6 1.2 %collective-permute-start.4 = (bf16[64,2048]{1,0:T(8,128)(2,1)S(1)}, bf16[64,2048]{1,0:T(8,128)(2,1)S(1)}, u32[]{:S(2)}, u32[]{:S(2)}) collective-permute-start(bf16[64,2048]{1,0:T(8,128)(2,1)S(1)} %maximum_select_fusion.2), channel_id=1, source_target_pairs={{0,16},{1,17},{2,18},{3,19},{4,20},{5,21},{6,22},{7,23},{8,120},{9... | collective-permute-start | bytes 786440 | tf_op jit(solution)/shard_map/ppermute | solution.py:18
  20.8 2.4 %collective-permute-done.5 = bf16[64,2048]{1,0:T(8,128)(2,1)S(1)} collective-permute-done((bf16[64,2048]{1,0:T(8,128)(2,1)S(1)}, bf16[64,2048]{1,0:T(8,128)(2,1)S(1)}, u32[]{:S(2)}, u32[]{:S(2)}) %collective-permute-start.5) | collective-permute-done | bytes 262176 | tf_op jit(solution)/shard_map/ppermute | solution.py:18
  23.2 0.5 collective-permute-start.11
  23.7 3.5 %collective-permute-start.13 = (bf16[64,2048]{1,0:T(8,128)(2,1)S(1)}, bf16[64,2048]{1,0:T(8,128)(2,1)S(1)}, u32[]{:S(2)}, u32[]{:S(2)}) collective-permute-start(bf16[64,2048]{1,0:T(8,128)(2,1)S(1)} %collective-permute-done.5), channel_id=1, source_target_pairs={{0,16},{1,17},{2,18},{3,19},{4,20},{5,21},{6,22},{7,23},{8,120},{9... | collective-permute-start | bytes 786440 | tf_op jit(solution)/shard_map/ppermute | solution.py:18
  27.3 0.0 slice-start.1
  27.3 6.4 %convolution_convert_fusion.3 = bf16[192,2048]{1,0:T(8,128)(2,1)S(1)} fusion(bf16[2048,2048]{1,0:T(8,128)(2,1)} %param.3, bf16[64,2048]{1,0:T(8,128)(2,1)S(1)} %collective-permute-done.6, bf16[64,2048]{1,0:T(8,128)(2,1)S(1)} %collective-permute-done.5, bf16[64,2048]{1,0:T(8,128)(2,1)S(1)} %maximum_select_fusion.1), kind=kOutput, calls=%fused_computation.3 | convolution fusion | flops 1613365248 | bytes 9961472 | tf_op jit(solution)/shard_map/dot_general | solution.py:64
  33.7 0.1 fusion.30
  33.8 0.9 %collective-permute-start.9 = (bf16[64,2048]{1,0:T(8,128)(2,1)S(1)}, bf16[64,2048]{1,0:T(8,128)(2,1)S(1)}, u32[]{:S(2)}, u32[]{:S(2)}) collective-permute-start(bf16[64,2048]{1,0:T(8,128)(2,1)S(1)} %collective-permute-done.7), channel_id=1, source_target_pairs={{0,16},{1,17},{2,18},{3,19},{4,20},{5,21},{6,22},{7,23},{8,120},{9... | collective-permute-start | bytes 786440 | tf_op jit(solution)/shard_map/ppermute | solution.py:18
  34.8 2.4 %collective-permute-done.13 = bf16[64,2048]{1,0:T(8,128)(2,1)S(1)} collective-permute-done((bf16[64,2048]{1,0:T(8,128)(2,1)S(1)}, bf16[64,2048]{1,0:T(8,128)(2,1)S(1)}, u32[]{:S(2)}, u32[]{:S(2)}) %collective-permute-start.13) | collective-permute-done | bytes 262176 | tf_op jit(solution)/shard_map/ppermute | solution.py:18
  37.2 0.6 collective-permute-start.16
  37.8 0.3 collective-permute-start.8
  38.1 0.6 collective-permute-done.14
  38.7 0.7 collective-permute-start.10
  39.5 0.1 constant_dynamic-slice_fusion.15
  39.6 2.4 %convolution_convert_fusion.2 = bf16[256,2048]{1,0:T(8,128)(2,1)S(1)} fusion(bf16[2048,2048]{1,0:T(8,128)(2,1)S(1)} %bitcast.19, bf16[64,2048]{1,0:T(8,128)(2,1)S(1)} %get-tuple-element.55, bf16[64,2048]{1,0:T(8,128)(2,1)S(1)} %get-tuple-element.56, bf16[64,2048]{1,0:T(8,128)(2,1)S(1)} %get-tuple-element.57, bf16[64,2048]{1,0:T(8,128)(2,1)S(1)} %get-tuple-element.54), kind=kOutput, calls=%fused_computation.2 | convolution fusion | flops 2152202240 | bytes 10485760 | tf_op jit(solution)/shard_map/dot_general | solution.py:64
  42.0 0.1 fusion.29
  42.1 1.6 %collective-permute-start.25 = (bf16[128,2048]{1,0:T(8,128)(2,1)S(1)}, bf16[128,2048]{1,0:T(8,128)(2,1)S(1)}, u32[]{:S(2)}, u32[]{:S(2)}) collective-permute-start(bf16[128,2048]{1,0:T(8,128)(2,1)S(1)} %get-tuple-element.53), channel_id=1, source_target_pairs={{0,1},{1,0},{2,3},{3,2},{4,5},{5,4},{6,7},{7,6},{8,11},{9,10},{10,... | collective-permute-start | bytes 1572872 | tf_op jit(solution)/shard_map/ppermute | solution.py:18
  43.7 2.3 %collective-permute-done.10 = bf16[32,2048]{1,0:T(8,128)(2,1)S(1)} collective-permute-done((bf16[32,2048]{1,0:T(8,128)(2,1)S(1)}, bf16[32,2048]{1,0:T(8,128)(2,1)S(1)}, u32[]{:S(2)}, u32[]{:S(2)}) %collective-permute-start.10) | collective-permute-done | bytes 131104 | tf_op jit(solution)/shard_map/ppermute | solution.py:18
  46.0 0.5 collective-permute-start.15
  46.5 0.0 collective-permute-start.18
  46.6 1.0 %collective-permute-done.17 = bf16[64,2048]{1,0:T(8,128)(2,1)S(1)} collective-permute-done((bf16[64,2048]{1,0:T(8,128)(2,1)S(1)}, bf16[64,2048]{1,0:T(8,128)(2,1)S(1)}, u32[]{:S(2)}, u32[]{:S(2)}) %collective-permute-start.17) | collective-permute-done | bytes 262176 | tf_op jit(solution)/shard_map/ppermute | solution.py:18
  47.6 0.1 constant_dynamic-slice_fusion.11
  47.7 2.4 %convolution_convert_fusion.1 = bf16[256,2048]{1,0:T(8,128)(2,1)S(1)} fusion(bf16[2048,2048]{1,0:T(8,128)(2,1)S(1)} %bitcast.19, bf16[64,2048]{1,0:T(8,128)(2,1)S(1)} %get-tuple-element.49, bf16[64,2048]{1,0:T(8,128)(2,1)S(1)} %get-tuple-element.50, bf16[64,2048]{1,0:T(8,128)(2,1)S(1)} %get-tuple-element.51, bf16[64,2048]{1,0:T(8,128)(2,1)S(1)} %get-tuple-element.48), kind=kOutput, calls=%fused_computation.1 | convolution fusion | flops 2152202240 | bytes 10485760 | tf_op jit(solution)/shard_map/dot_general | solution.py:64
  50.1 0.1 fusion.28
  50.2 1.6 %collective-permute-start.27 = (bf16[128,2048]{1,0:T(8,128)(2,1)S(1)}, bf16[128,2048]{1,0:T(8,128)(2,1)S(1)}, u32[]{:S(2)}, u32[]{:S(2)}) collective-permute-start(bf16[128,2048]{1,0:T(8,128)(2,1)S(1)} %get-tuple-element.47), channel_id=1, source_target_pairs={{0,1},{1,0},{2,3},{3,2},{4,5},{5,4},{6,7},{7,6},{8,11},{9,10},{10,... | collective-permute-start | bytes 1572872 | tf_op jit(solution)/shard_map/ppermute | solution.py:18
  51.8 0.1 pad_maximum_fusion
  52.2 2.9 %convolution_convert_fusion = bf16[320,2048]{1,0:T(8,128)(2,1)S(1)} fusion(bf16[320,2048]{1,0:T(8,128)(2,1)S(1)} %fusion.20, bf16[2048,2048]{1,0:T(8,128)(2,1)S(1)} %bitcast.19), kind=kOutput, calls=%fused_computation | convolution fusion | flops 2685009920 | bytes 11010048 | tf_op jit(solution)/shard_map/dot_general | solution.py:64
  55.1 0.1 fusion.27
  55.2 0.1 pad_maximum_fusion.1
  55.3 0.1 constant_dynamic-slice_fusion.7
  55.4 0.1 broadcast_select_fusion
  55.5 1.6 %collective-permute-start.22 = (bf16[128,2048]{1,0:T(8,128)(2,1)S(1)}, bf16[128,2048]{1,0:T(8,128)(2,1)S(1)}, u32[]{:S(2)}, u32[]{:S(2)}) collective-permute-start(bf16[128,2048]{1,0:T(8,128)(2,1)S(1)} %broadcast_select_fusion), channel_id=1, source_target_pairs={{0,4},{1,5},{2,6},{3,7},{4,0},{5,1},{6,2},{7,3},{8,12},{9,13},{10,... | collective-permute-start | bytes 1572872 | tf_op jit(solution)/shard_map/ppermute | solution.py:18
  57.1 0.6 collective-permute-start.19
  57.8 0.1 convert_add_fusion.1
  57.9 2.8 %collective-permute-start.26 = (bf16[64,2048]{1,0:T(8,128)(2,1)S(1)}, bf16[64,2048]{1,0:T(8,128)(2,1)S(1)}, u32[]{:S(2)}, u32[]{:S(2)}) collective-permute-start(bf16[64,2048]{1,0:T(8,128)(2,1)S(1)} %slice.170), channel_id=1, source_target_pairs={{0,3},{1,2},{2,1},{3,0},{4,7},{5,6},{6,5},{7,4},{8,9},{9,8},{10,11... | collective-permute-start | bytes 786440 | tf_op jit(solution)/shard_map/ppermute | solution.py:18
  60.8 0.1 convert_add_fusion
  61.0 1.5 %collective-permute-start.28 = (bf16[64,2048]{1,0:T(8,128)(2,1)S(1)}, bf16[64,2048]{1,0:T(8,128)(2,1)S(1)}, u32[]{:S(2)}, u32[]{:S(2)}) collective-permute-start(bf16[64,2048]{1,0:T(8,128)(2,1)S(1)} %slice.169), channel_id=1, source_target_pairs={{0,3},{1,2},{2,1},{3,0},{4,7},{5,6},{6,5},{7,4},{8,9},{9,8},{10,11... | collective-permute-start | bytes 786440 | tf_op jit(solution)/shard_map/ppermute | solution.py:18
  62.5 8.0 %collective-permute-done.22 = bf16[128,2048]{1,0:T(8,128)(2,1)S(1)} collective-permute-done((bf16[128,2048]{1,0:T(8,128)(2,1)S(1)}, bf16[128,2048]{1,0:T(8,128)(2,1)S(1)}, u32[]{:S(2)}, u32[]{:S(2)}) %collective-permute-start.22) | collective-permute-done | bytes 524320 | tf_op jit(solution)/shard_map/ppermute | solution.py:18
  70.5 0.2 convert_add_fusion.2
  70.7 0.6 collective-permute-start.23
  71.3 0.4 collective-permute-done.19
  71.7 0.1 fusion.26
  71.9 1.5 %collective-permute-start.20 = (bf16[64,2048]{1,0:T(8,128)(2,1)S(1)}, bf16[64,2048]{1,0:T(8,128)(2,1)S(1)}, u32[]{:S(2)}, u32[]{:S(2)}) collective-permute-start(bf16[64,2048]{1,0:T(8,128)(2,1)S(1)} %pad_maximum_fusion.4), channel_id=1, source_target_pairs={{0,3},{1,2},{2,1},{3,0},{4,7},{5,6},{6,5},{7,4},{8,9},{9,8},{10,11... | collective-permute-start | bytes 786440 | tf_op jit(solution)/shard_map/ppermute | solution.py:18
  73.4 0.1 select_convert_fusion
  73.5 0.8 collective-permute-start.29
  74.4 6.1 %collective-permute-done.20 = bf16[64,2048]{1,0:T(8,128)(2,1)S(1)} collective-permute-done((bf16[64,2048]{1,0:T(8,128)(2,1)S(1)}, bf16[64,2048]{1,0:T(8,128)(2,1)S(1)}, u32[]{:S(2)}, u32[]{:S(2)}) %collective-permute-start.20) | collective-permute-done | bytes 262176 | tf_op jit(solution)/shard_map/ppermute | solution.py:18
  80.5 0.1 select_convert_fusion.1
  80.5 1.4 %collective-permute-start.21 = (bf16[32,2048]{1,0:T(8,128)(2,1)S(1)}, bf16[32,2048]{1,0:T(8,128)(2,1)S(1)}, u32[]{:S(2)}, u32[]{:S(2)}) collective-permute-start(bf16[32,2048]{1,0:T(8,128)(2,1)S(1)} %select_convert_fusion.1), channel_id=1, source_target_pairs={{0,4},{1,5},{2,6},{3,7},{4,0},{5,1},{6,2},{7,3},{8,12},{9,13},{10,... | collective-permute-start | bytes 393224 | tf_op jit(solution)/shard_map/ppermute | solution.py:18
  82.0 0.4 collective-permute-start.24
  82.4 3.3 %collective-permute-done.21 = bf16[32,2048]{1,0:T(8,128)(2,1)S(1)} collective-permute-done((bf16[32,2048]{1,0:T(8,128)(2,1)S(1)}, bf16[32,2048]{1,0:T(8,128)(2,1)S(1)}, u32[]{:S(2)}, u32[]{:S(2)}) %collective-permute-start.21) | collective-permute-done | bytes 131104 | tf_op jit(solution)/shard_map/ppermute | solution.py:18
  85.6 0.1 convert_add_fusion.5
  85.7 2.5 %collective-permute-done.24 = bf16[32,2048]{1,0:T(8,128)(2,1)S(1)} collective-permute-done((bf16[32,2048]{1,0:T(8,128)(2,1)S(1)}, bf16[32,2048]{1,0:T(8,128)(2,1)S(1)}, u32[]{:S(2)}, u32[]{:S(2)}) %collective-permute-start.24) | collective-permute-done | bytes 131104 | tf_op jit(solution)/shard_map/ppermute | solution.py:18
  88.3 0.1 convert_add_fusion.4
  88.5 1.1 %maximum_select_fusion = f32[128,2048]{1,0:T(8,128)} fusion(f32[64,2048]{1,0:T(8,128)S(1)} %convert_add_fusion.4, f32[32,2048]{1,0:T(8,128)S(1)} %slice_add_fusion.3, f32[32,2048]{1,0:T(8,128)S(1)} %convert_add_fusion.5, pred[]{:T(512)S(6)} %eq.114), kind=kLoop, calls=%fused_computation.22 | loop fusion | flops 1310720 | bytes 2097153 | tf_op jit(solution)/shard_map/jit(_where)/select_n | solution.py:176
  (59 shorter events, 0.9 us)
Async XLA Ops:
  0.0 1.6 %copy-start = (bf16[4,512,512]{2,1,0:T(8,128)(2,1)S(1)}, bf16[4,512,512]{2,1,0:T(8,128)(2,1)}, u32[]{:S(2)}) copy-start(bf16[4,512,512]{2,1,0:T(8,128)(2,1)} %param.5) | copy-start | bytes 6291460
  3.0 1.4 %collective-permute-start = (bf16[32,2048]{1,0:T(8,128)(2,1)S(1)}, bf16[32,2048]{1,0:T(8,128)(2,1)S(1)}, u32[]{:S(2)}, u32[]{:S(2)}) collective-permute-start(bf16[32,2048]{1,0:T(8,128)(2,1)S(1)} %bitcast.14), channel_id=1, source_target_pairs={{0,8},{1,9},{2,10},{3,11},{4,12},{5,13},{6,14},{7,15},{8,0},{9,1},... | collective-permute-start | bytes 393224 | tf_op jit(solution)/shard_map/ppermute | solution.py:18
  4.4 11.1 %collective-permute-start.2 = (bf16[64,2048]{1,0:T(8,128)(2,1)S(1)}, bf16[64,2048]{1,0:T(8,128)(2,1)S(1)}, u32[]{:S(2)}, u32[]{:S(2)}) collective-permute-start(bf16[64,2048]{1,0:T(8,128)(2,1)S(1)} %maximum_select_fusion.1), channel_id=1, source_target_pairs={{0,16},{1,17},{2,18},{3,19},{4,20},{5,21},{6,22},{7,23},{8,120},{9... | collective-permute-start | bytes 786440 | tf_op jit(solution)/shard_map/ppermute | solution.py:18
  6.4 6.5 %collective-permute-start.1 = (bf16[32,2048]{1,0:T(8,128)(2,1)S(1)}, bf16[32,2048]{1,0:T(8,128)(2,1)S(1)}, u32[]{:S(2)}, u32[]{:S(2)}) collective-permute-start(bf16[32,2048]{1,0:T(8,128)(2,1)S(1)} %bitcast.16), channel_id=1, source_target_pairs={{0,128},{1,129},{2,130},{3,131},{4,132},{5,133},{6,134},{7,135},{8... | collective-permute-start | bytes 393224 | tf_op jit(solution)/shard_map/ppermute | solution.py:18
  12.9 5.6 %collective-permute-start.3 = (bf16[32,2048]{1,0:T(8,128)(2,1)S(1)}, bf16[32,2048]{1,0:T(8,128)(2,1)S(1)}, u32[]{:S(2)}, u32[]{:S(2)}) collective-permute-start(bf16[32,2048]{1,0:T(8,128)(2,1)S(1)} %collective-permute-done.1), channel_id=1, source_target_pairs={{0,8},{1,9},{2,10},{3,11},{4,12},{5,13},{6,14},{7,15},{8,0},{9,1},... | collective-permute-start | bytes 393224 | tf_op jit(solution)/shard_map/ppermute | solution.py:18
  15.6 7.6 %collective-permute-start.5 = (bf16[64,2048]{1,0:T(8,128)(2,1)S(1)}, bf16[64,2048]{1,0:T(8,128)(2,1)S(1)}, u32[]{:S(2)}, u32[]{:S(2)}) collective-permute-start(bf16[64,2048]{1,0:T(8,128)(2,1)S(1)} %collective-permute-done.2), channel_id=1, source_target_pairs={{0,16},{1,17},{2,18},{3,19},{4,20},{5,21},{6,22},{7,23},{8,120},{9... | collective-permute-start | bytes 786440 | tf_op jit(solution)/shard_map/ppermute | solution.py:18
  15.6 8.1 %collective-permute-start.12 = (bf16[64,2048]{1,0:T(8,128)(2,1)S(1)}, bf16[64,2048]{1,0:T(8,128)(2,1)S(1)}, u32[]{:S(2)}, u32[]{:S(2)}) collective-permute-start(bf16[64,2048]{1,0:T(8,128)(2,1)S(1)} %collective-permute-done.2), channel_id=1, source_target_pairs={{0,8},{1,9},{2,10},{3,11},{4,12},{5,13},{6,14},{7,15},{8,0},{9,1},... | collective-permute-start | bytes 786440 | tf_op jit(solution)/shard_map/ppermute | solution.py:18
  18.6 15.3 %collective-permute-start.7 = (bf16[64,2048]{1,0:T(8,128)(2,1)S(1)}, bf16[64,2048]{1,0:T(8,128)(2,1)S(1)}, u32[]{:S(2)}, u32[]{:S(2)}) collective-permute-start(bf16[64,2048]{1,0:T(8,128)(2,1)S(1)} %maximum_select_fusion.2), channel_id=1, source_target_pairs={{0,32},{1,33},{2,34},{3,35},{4,36},{5,37},{6,38},{7,39},{8,104},{9... | collective-permute-start | bytes 786440 | tf_op jit(solution)/shard_map/ppermute | solution.py:18
  19.6 15.2 %collective-permute-start.4 = (bf16[64,2048]{1,0:T(8,128)(2,1)S(1)}, bf16[64,2048]{1,0:T(8,128)(2,1)S(1)}, u32[]{:S(2)}, u32[]{:S(2)}) collective-permute-start(bf16[64,2048]{1,0:T(8,128)(2,1)S(1)} %maximum_select_fusion.2), channel_id=1, source_target_pairs={{0,16},{1,17},{2,18},{3,19},{4,20},{5,21},{6,22},{7,23},{8,120},{9... | collective-permute-start | bytes 786440 | tf_op jit(solution)/shard_map/ppermute | solution.py:18
  23.2 4.1 %collective-permute-start.6 = (bf16[64,2048]{1,0:T(8,128)(2,1)S(1)}, bf16[64,2048]{1,0:T(8,128)(2,1)S(1)}, u32[]{:S(2)}, u32[]{:S(2)}) collective-permute-start(bf16[64,2048]{1,0:T(8,128)(2,1)S(1)} %collective-permute-done.5), channel_id=1, source_target_pairs={{0,8},{1,9},{2,10},{3,11},{4,12},{5,13},{6,14},{7,15},{8,0},{9,1},... | collective-permute-start | bytes 786440 | tf_op jit(solution)/shard_map/ppermute | solution.py:18
  23.2 18.9 %collective-permute-start.11 = (bf16[32,2048]{1,0:T(8,128)(2,1)S(1)}, bf16[32,2048]{1,0:T(8,128)(2,1)S(1)}, u32[]{:S(2)}, u32[]{:S(2)}) collective-permute-start(bf16[32,2048]{1,0:T(8,128)(2,1)S(1)} %constant_dynamic-slice_fusion.16), channel_id=1, source_target_pairs={{0,32},{1,33},{2,34},{3,35},{4,36},{5,37},{6,38},{7,39},{8,104},{9... | collective-permute-start | bytes 393224 | tf_op jit(solution)/shard_map/ppermute | solution.py:18
  23.7 13.5 %collective-permute-start.13 = (bf16[64,2048]{1,0:T(8,128)(2,1)S(1)}, bf16[64,2048]{1,0:T(8,128)(2,1)S(1)}, u32[]{:S(2)}, u32[]{:S(2)}) collective-permute-start(bf16[64,2048]{1,0:T(8,128)(2,1)S(1)} %collective-permute-done.5), channel_id=1, source_target_pairs={{0,16},{1,17},{2,18},{3,19},{4,20},{5,21},{6,22},{7,23},{8,120},{9... | collective-permute-start | bytes 786440 | tf_op jit(solution)/shard_map/ppermute | solution.py:18
  27.2 12.3 %slice-start = ((s8[8388608]{0:T(1024)(128)(4,1)}), s8[4194304]{0:T(1024)(128)(4,1)S(1)}, s32[]{:S(2)}) async-start(s8[8388608]{0:T(1024)(128)(4,1)} %bitcast.18), calls=%async_computation | async-start | bytes 8388608
  27.3 12.3 %slice-start.1 = ((s8[8388608]{0:T(1024)(128)(4,1)}), s8[4194304]{0:T(1024)(128)(4,1)S(1)}, s32[]{:S(2)}) async-start(s8[8388608]{0:T(1024)(128)(4,1)} %bitcast.18), calls=%async_computation.1 | async-start | bytes 8388608
  33.8 12.2 %collective-permute-start.9 = (bf16[64,2048]{1,0:T(8,128)(2,1)S(1)}, bf16[64,2048]{1,0:T(8,128)(2,1)S(1)}, u32[]{:S(2)}, u32[]{:S(2)}) collective-permute-start(bf16[64,2048]{1,0:T(8,128)(2,1)S(1)} %collective-permute-done.7), channel_id=1, source_target_pairs={{0,16},{1,17},{2,18},{3,19},{4,20},{5,21},{6,22},{7,23},{8,120},{9... | collective-permute-start | bytes 786440 | tf_op jit(solution)/shard_map/ppermute | solution.py:18
  37.2 1.5 %collective-permute-start.14 = (bf16[64,2048]{1,0:T(8,128)(2,1)S(1)}, bf16[64,2048]{1,0:T(8,128)(2,1)S(1)}, u32[]{:S(2)}, u32[]{:S(2)}) collective-permute-start(bf16[64,2048]{1,0:T(8,128)(2,1)S(1)} %collective-permute-done.13), channel_id=1, source_target_pairs={{0,8},{1,9},{2,10},{3,11},{4,12},{5,13},{6,14},{7,15},{8,0},{9,1},... | collective-permute-start | bytes 786440 | tf_op jit(solution)/shard_map/ppermute | solution.py:18
  37.2 9.3 %collective-permute-start.16 = (bf16[64,2048]{1,0:T(8,128)(2,1)S(1)}, bf16[64,2048]{1,0:T(8,128)(2,1)S(1)}, u32[]{:S(2)}, u32[]{:S(2)}) collective-permute-start(bf16[64,2048]{1,0:T(8,128)(2,1)S(1)} %collective-permute-done.4), channel_id=1, source_target_pairs={{0,8},{1,9},{2,10},{3,11},{4,12},{5,13},{6,14},{7,15},{8,0},{9,1},... | collective-permute-start | bytes 786440 | tf_op jit(solution)/shard_map/ppermute | solution.py:18
  37.8 14.0 %collective-permute-start.8 = (bf16[64,2048]{1,0:T(8,128)(2,1)S(1)}, bf16[64,2048]{1,0:T(8,128)(2,1)S(1)}, u32[]{:S(2)}, u32[]{:S(2)}) collective-permute-start(bf16[64,2048]{1,0:T(8,128)(2,1)S(1)} %collective-permute-done.7), channel_id=1, source_target_pairs={{0,8},{1,9},{2,10},{3,11},{4,12},{5,13},{6,14},{7,15},{8,0},{9,1},... | collective-permute-start | bytes 786440 | tf_op jit(solution)/shard_map/ppermute | solution.py:18
  38.7 7.3 %collective-permute-start.10 = (bf16[32,2048]{1,0:T(8,128)(2,1)S(1)}, bf16[32,2048]{1,0:T(8,128)(2,1)S(1)}, u32[]{:S(2)}, u32[]{:S(2)}) collective-permute-start(bf16[32,2048]{1,0:T(8,128)(2,1)S(1)} %constant_dynamic-slice_fusion.17), channel_id=1, source_target_pairs={{0,32},{1,33},{2,34},{3,35},{4,36},{5,37},{6,38},{7,39},{8,104},{9... | collective-permute-start | bytes 393224 | tf_op jit(solution)/shard_map/ppermute | solution.py:18
  42.1 15.6 %collective-permute-start.25 = (bf16[128,2048]{1,0:T(8,128)(2,1)S(1)}, bf16[128,2048]{1,0:T(8,128)(2,1)S(1)}, u32[]{:S(2)}, u32[]{:S(2)}) collective-permute-start(bf16[128,2048]{1,0:T(8,128)(2,1)S(1)} %get-tuple-element.53), channel_id=1, source_target_pairs={{0,1},{1,0},{2,3},{3,2},{4,5},{5,4},{6,7},{7,6},{8,11},{9,10},{10,... | collective-permute-start | bytes 1572872 | tf_op jit(solution)/shard_map/ppermute | solution.py:18
  46.0 1.5 %collective-permute-start.17 = (bf16[64,2048]{1,0:T(8,128)(2,1)S(1)}, bf16[64,2048]{1,0:T(8,128)(2,1)S(1)}, u32[]{:S(2)}, u32[]{:S(2)}) collective-permute-start(bf16[64,2048]{1,0:T(8,128)(2,1)S(1)} %collective-permute-done.9), channel_id=1, source_target_pairs={{0,8},{1,9},{2,10},{3,11},{4,12},{5,13},{6,14},{7,15},{8,0},{9,1},... | collective-permute-start | bytes 786440 | tf_op jit(solution)/shard_map/ppermute | solution.py:18
  46.0 5.7 %collective-permute-start.15 = (bf16[32,2048]{1,0:T(8,128)(2,1)S(1)}, bf16[32,2048]{1,0:T(8,128)(2,1)S(1)}, u32[]{:S(2)}, u32[]{:S(2)}) collective-permute-start(bf16[32,2048]{1,0:T(8,128)(2,1)S(1)} %collective-permute-done.10), channel_id=1, source_target_pairs={{0,8},{1,9},{2,10},{3,11},{4,12},{5,13},{6,14},{7,15},{8,0},{9,1},... | collective-permute-start | bytes 393224 | tf_op jit(solution)/shard_map/ppermute | solution.py:18
  46.5 5.6 %collective-permute-start.18 = (bf16[32,2048]{1,0:T(8,128)(2,1)S(1)}, bf16[32,2048]{1,0:T(8,128)(2,1)S(1)}, u32[]{:S(2)}, u32[]{:S(2)}) collective-permute-start(bf16[32,2048]{1,0:T(8,128)(2,1)S(1)} %collective-permute-done.11), channel_id=1, source_target_pairs={{0,8},{1,9},{2,10},{3,11},{4,12},{5,13},{6,14},{7,15},{8,0},{9,1},... | collective-permute-start | bytes 393224 | tf_op jit(solution)/shard_map/ppermute | solution.py:18
  50.2 10.6 %collective-permute-start.27 = (bf16[128,2048]{1,0:T(8,128)(2,1)S(1)}, bf16[128,2048]{1,0:T(8,128)(2,1)S(1)}, u32[]{:S(2)}, u32[]{:S(2)}) collective-permute-start(bf16[128,2048]{1,0:T(8,128)(2,1)S(1)} %get-tuple-element.47), channel_id=1, source_target_pairs={{0,1},{1,0},{2,3},{3,2},{4,5},{5,4},{6,7},{7,6},{8,11},{9,10},{10,... | collective-permute-start | bytes 1572872 | tf_op jit(solution)/shard_map/ppermute | solution.py:18
  55.5 15.0 %collective-permute-start.22 = (bf16[128,2048]{1,0:T(8,128)(2,1)S(1)}, bf16[128,2048]{1,0:T(8,128)(2,1)S(1)}, u32[]{:S(2)}, u32[]{:S(2)}) collective-permute-start(bf16[128,2048]{1,0:T(8,128)(2,1)S(1)} %broadcast_select_fusion), channel_id=1, source_target_pairs={{0,4},{1,5},{2,6},{3,7},{4,0},{5,1},{6,2},{7,3},{8,12},{9,13},{10,... | collective-permute-start | bytes 1572872 | tf_op jit(solution)/shard_map/ppermute | solution.py:18
  57.1 14.6 %collective-permute-start.19 = (bf16[128,2048]{1,0:T(8,128)(2,1)S(1)}, bf16[128,2048]{1,0:T(8,128)(2,1)S(1)}, u32[]{:S(2)}, u32[]{:S(2)}) collective-permute-start(bf16[128,2048]{1,0:T(8,128)(2,1)S(1)} %pad_maximum_fusion.2), channel_id=1, source_target_pairs={{0,1},{1,0},{2,3},{3,2},{4,5},{5,4},{6,7},{7,6},{8,11},{9,10},{10,... | collective-permute-start | bytes 1572872 | tf_op jit(solution)/shard_map/ppermute | solution.py:18
  57.9 15.5 %collective-permute-start.26 = (bf16[64,2048]{1,0:T(8,128)(2,1)S(1)}, bf16[64,2048]{1,0:T(8,128)(2,1)S(1)}, u32[]{:S(2)}, u32[]{:S(2)}) collective-permute-start(bf16[64,2048]{1,0:T(8,128)(2,1)S(1)} %slice.170), channel_id=1, source_target_pairs={{0,3},{1,2},{2,1},{3,0},{4,7},{5,6},{6,5},{7,4},{8,9},{9,8},{10,11... | collective-permute-start | bytes 786440 | tf_op jit(solution)/shard_map/ppermute | solution.py:18
  61.0 12.5 %collective-permute-start.28 = (bf16[64,2048]{1,0:T(8,128)(2,1)S(1)}, bf16[64,2048]{1,0:T(8,128)(2,1)S(1)}, u32[]{:S(2)}, u32[]{:S(2)}) collective-permute-start(bf16[64,2048]{1,0:T(8,128)(2,1)S(1)} %slice.169), channel_id=1, source_target_pairs={{0,3},{1,2},{2,1},{3,0},{4,7},{5,6},{6,5},{7,4},{8,9},{9,8},{10,11... | collective-permute-start | bytes 786440 | tf_op jit(solution)/shard_map/ppermute | solution.py:18
  70.7 11.2 %collective-permute-start.23 = (bf16[64,2048]{1,0:T(8,128)(2,1)S(1)}, bf16[64,2048]{1,0:T(8,128)(2,1)S(1)}, u32[]{:S(2)}, u32[]{:S(2)}) collective-permute-start(bf16[64,2048]{1,0:T(8,128)(2,1)S(1)} %slice.171), channel_id=1, source_target_pairs={{0,1},{1,0},{2,3},{3,2},{4,5},{5,4},{6,7},{7,6},{8,11},{9,10},{10,... | collective-permute-start | bytes 786440 | tf_op jit(solution)/shard_map/ppermute | solution.py:18
  71.9 8.6 %collective-permute-start.20 = (bf16[64,2048]{1,0:T(8,128)(2,1)S(1)}, bf16[64,2048]{1,0:T(8,128)(2,1)S(1)}, u32[]{:S(2)}, u32[]{:S(2)}) collective-permute-start(bf16[64,2048]{1,0:T(8,128)(2,1)S(1)} %pad_maximum_fusion.4), channel_id=1, source_target_pairs={{0,3},{1,2},{2,1},{3,0},{4,7},{5,6},{6,5},{7,4},{8,9},{9,8},{10,11... | collective-permute-start | bytes 786440 | tf_op jit(solution)/shard_map/ppermute | solution.py:18
  73.5 14.8 %collective-permute-start.29 = (bf16[64,2048]{1,0:T(8,128)(2,1)S(1)}, bf16[64,2048]{1,0:T(8,128)(2,1)S(1)}, u32[]{:S(2)}, u32[]{:S(2)}) collective-permute-start(bf16[64,2048]{1,0:T(8,128)(2,1)S(1)} %select_convert_fusion), channel_id=1, source_target_pairs={{0,4},{1,5},{2,6},{3,7},{4,0},{5,1},{6,2},{7,3},{8,12},{9,13},{10,... | collective-permute-start | bytes 786440 | tf_op jit(solution)/shard_map/ppermute | solution.py:18
  80.5 5.1 %collective-permute-start.21 = (bf16[32,2048]{1,0:T(8,128)(2,1)S(1)}, bf16[32,2048]{1,0:T(8,128)(2,1)S(1)}, u32[]{:S(2)}, u32[]{:S(2)}) collective-permute-start(bf16[32,2048]{1,0:T(8,128)(2,1)S(1)} %select_convert_fusion.1), channel_id=1, source_target_pairs={{0,4},{1,5},{2,6},{3,7},{4,0},{5,1},{6,2},{7,3},{8,12},{9,13},{10,... | collective-permute-start | bytes 393224 | tf_op jit(solution)/shard_map/ppermute | solution.py:18
  82.0 6.3 %collective-permute-start.24 = (bf16[32,2048]{1,0:T(8,128)(2,1)S(1)}, bf16[32,2048]{1,0:T(8,128)(2,1)S(1)}, u32[]{:S(2)}, u32[]{:S(2)}) collective-permute-start(bf16[32,2048]{1,0:T(8,128)(2,1)S(1)} %slice.172), channel_id=1, source_target_pairs={{0,3},{1,2},{2,1},{3,0},{4,7},{5,6},{6,5},{7,4},{8,9},{9,8},{10,11... | collective-permute-start | bytes 393224 | tf_op jit(solution)/shard_map/ppermute | solution.py:18

commit v5 on v4

--- a/solution.py
+++ b/solution.py
@@ -133,8 +133,9 @@
     odd = scores(picked(odd_place, 1, o1, t1, o3, t3))
     odd_come, odd = first_x(odd[: 2 * rows]), odd[2 * rows :]
     a3, a4, o4, odd = together(a3, a4, o4, odd)
-    t4 = other_core(o4)
-    u1, u2, u3, u4 = map(other_core, (a1, a2, a3, a4))
+    u1, u2, u3 = map(other_core, (a1, a2, a3))
+    swapped = other_core(jnp.concatenate([a4, o4]))
+    u4, t4 = swapped[:part], swapped[part:]
     odd_across = scores(picked(odd_place, 1, a1, u1, a3, u3))
     u4, odd_across_kept = together(u4, odd_across[2 * rows :])
     ready = picked(even_place, 2, a0, a2, u2, both_cores(c, a4, u4))

time: 89.6 us -> 89.5 us (level)
    ppermute x30 -> x29, waiting for transfers between devices: 36.5 us -> 36.2 us  [move(): return lax.ppermute(value, NAMES, pairs)]
    ppermute x30 -> x29, starting transfers between devices: 31.7 us -> 31.8 us  [move(): return lax.ppermute(value, NAMES, pairs)]
  transfers between devices with their start and end apart: 30 -> 29, of which waited for: 12 -> 12; matrix products, arithmetic and copies ran while one was open for 19% -> 19% of each run, Pallas kernels for 0% -> 0%
where the time goes in v5:
time: 89.5 us; the launch traced here: 89.4 us
  waiting for transfers between devices  36.2 us (40%)
  starting transfers between devices  31.8 us (36%)
  matrix products  15.4 us (17%)
  other arithmetic  2.73 us (3%)
  local copies, waits for them, and re-layouts  2.72 us (3%)
    ppermute x29, waiting for transfers between devices, move(): return lax.ppermute(value, NAMES, pairs)  36.2 us
    ppermute x29, starting transfers between devices, move(): return lax.ppermute(value, NAMES, pairs)  31.8 us
    dot_general x4, matrix products, score_rows(): lax.dot_general(ready, train_grads, (((1,), (1,)), ((), ())), preferred_e...  14.1 us
    unnamed x20, local copies, waits for them, and re-layouts  1.86 us
  transfers between devices with their start and end apart: 29, of which 12 were waited for; matrix products, arithmetic and copies ran while one was open for 19% of the time, Pallas kernels for 0%

profile of v5, /device:TPU:16, one launch (start us, length us, event | category | flops | bytes accessed | tf_op | source)
XLA Modules:
  0.0 89.4 jit_solution(12993427275443132740)
XLA Ops:
  0.0 1.6 %copy-done = bf16[4,512,512]{2,1,0:T(8,128)(2,1)S(1)} copy-done((bf16[4,512,512]{2,1,0:T(8,128)(2,1)S(1)}, bf16[4,512,512]{2,1,0:T(8,128)(2,1)}, u32[]{:S(2)}) %copy-start) | copy-done | bytes 2097176
  1.6 1.3 %fusion = bf16[4,4,8,512]{3,2,1,0:T(8,128)(2,1)S(1)} fusion(bf16[4,512,512]{2,1,0:T(8,128)(2,1)S(1)} %copy-done, bf16[4,4,8,512]{3,2,1,0:T(8,128)(2,1)} %bitcast.17), kind=kOutput, calls=%fused_computation.5 | convolution fusion | flops 67174400 | bytes 2359296 | tf_op jit(solution)/shard_map/rbi,bij->rbj/dot_general | solution.py:59
  3.0 0.1 collective-permute-start
  3.1 1.3 %collective-permute-done = bf16[32,2048]{1,0:T(8,128)(2,1)S(1)} collective-permute-done((bf16[32,2048]{1,0:T(8,128)(2,1)S(1)}, bf16[32,2048]{1,0:T(8,128)(2,1)S(1)}, u32[]{:S(2)}, u32[]{:S(2)}) %collective-permute-start) | collective-permute-done | bytes 131104 | tf_op jit(solution)/shard_map/ppermute | solution.py:18
  4.4 2.0 %collective-permute-start.2 = (bf16[64,2048]{1,0:T(8,128)(2,1)S(1)}, bf16[64,2048]{1,0:T(8,128)(2,1)S(1)}, u32[]{:S(2)}, u32[]{:S(2)}) collective-permute-start(bf16[64,2048]{1,0:T(8,128)(2,1)S(1)} %maximum_select_fusion.1), channel_id=1, source_target_pairs={{0,16},{1,17},{2,18},{3,19},{4,20},{5,21},{6,22},{7,23},{8,120},{9... | collective-permute-start | bytes 786440 | tf_op jit(solution)/shard_map/ppermute | solution.py:18
  6.4 0.3 collective-permute-start.1
  6.8 6.1 %collective-permute-done.1 = bf16[32,2048]{1,0:T(8,128)(2,1)S(1)} collective-permute-done((bf16[32,2048]{1,0:T(8,128)(2,1)S(1)}, bf16[32,2048]{1,0:T(8,128)(2,1)S(1)}, u32[]{:S(2)}, u32[]{:S(2)}) %collective-permute-start.1) | collective-permute-done | bytes 131104 | tf_op jit(solution)/shard_map/ppermute | solution.py:18
  12.9 2.7 %collective-permute-start.3 = (bf16[32,2048]{1,0:T(8,128)(2,1)S(1)}, bf16[32,2048]{1,0:T(8,128)(2,1)S(1)}, u32[]{:S(2)}, u32[]{:S(2)}) collective-permute-start(bf16[32,2048]{1,0:T(8,128)(2,1)S(1)} %collective-permute-done.1), channel_id=1, source_target_pairs={{0,8},{1,9},{2,10},{3,11},{4,12},{5,13},{6,14},{7,15},{8,0},{9,1},... | collective-permute-start | bytes 393224 | tf_op jit(solution)/shard_map/ppermute | solution.py:18
  15.6 0.0 collective-permute-done.2
  15.6 2.9 %collective-permute-start.12 = (bf16[64,2048]{1,0:T(8,128)(2,1)S(1)}, bf16[64,2048]{1,0:T(8,128)(2,1)S(1)}, u32[]{:S(2)}, u32[]{:S(2)}) collective-permute-start(bf16[64,2048]{1,0:T(8,128)(2,1)S(1)} %collective-permute-done.2), channel_id=1, source_target_pairs={{0,8},{1,9},{2,10},{3,11},{4,12},{5,13},{6,14},{7,15},{8,0},{9,1},... | collective-permute-start | bytes 786440 | tf_op jit(solution)/shard_map/ppermute | solution.py:18
  18.6 1.0 %collective-permute-start.7 = (bf16[64,2048]{1,0:T(8,128)(2,1)S(1)}, bf16[64,2048]{1,0:T(8,128)(2,1)S(1)}, u32[]{:S(2)}, u32[]{:S(2)}) collective-permute-start(bf16[64,2048]{1,0:T(8,128)(2,1)S(1)} %maximum_select_fusion.2), channel_id=1, source_target_pairs={{0,32},{1,33},{2,34},{3,35},{4,36},{5,37},{6,38},{7,39},{8,104},{9... | collective-permute-start | bytes 786440 | tf_op jit(solution)/shard_map/ppermute | solution.py:18
  19.6 1.2 %collective-permute-start.4 = (bf16[64,2048]{1,0:T(8,128)(2,1)S(1)}, bf16[64,2048]{1,0:T(8,128)(2,1)S(1)}, u32[]{:S(2)}, u32[]{:S(2)}) collective-permute-start(bf16[64,2048]{1,0:T(8,128)(2,1)S(1)} %maximum_select_fusion.2), channel_id=1, source_target_pairs={{0,16},{1,17},{2,18},{3,19},{4,20},{5,21},{6,22},{7,23},{8,120},{9... | collective-permute-start | bytes 786440 | tf_op jit(solution)/shard_map/ppermute | solution.py:18
  20.8 2.4 %collective-permute-done.5 = bf16[64,2048]{1,0:T(8,128)(2,1)S(1)} collective-permute-done((bf16[64,2048]{1,0:T(8,128)(2,1)S(1)}, bf16[64,2048]{1,0:T(8,128)(2,1)S(1)}, u32[]{:S(2)}, u32[]{:S(2)}) %collective-permute-start.5) | collective-permute-done | bytes 262176 | tf_op jit(solution)/shard_map/ppermute | solution.py:18
  23.2 0.5 collective-permute-start.11
  23.7 3.5 %collective-permute-start.13 = (bf16[64,2048]{1,0:T(8,128)(2,1)S(1)}, bf16[64,2048]{1,0:T(8,128)(2,1)S(1)}, u32[]{:S(2)}, u32[]{:S(2)}) collective-permute-start(bf16[64,2048]{1,0:T(8,128)(2,1)S(1)} %collective-permute-done.5), channel_id=1, source_target_pairs={{0,16},{1,17},{2,18},{3,19},{4,20},{5,21},{6,22},{7,23},{8,120},{9... | collective-permute-start | bytes 786440 | tf_op jit(solution)/shard_map/ppermute | solution.py:18
  27.3 0.0 slice-start.1
  27.3 6.4 %convolution_convert_fusion.3 = bf16[192,2048]{1,0:T(8,128)(2,1)S(1)} fusion(bf16[2048,2048]{1,0:T(8,128)(2,1)} %param.3, bf16[64,2048]{1,0:T(8,128)(2,1)S(1)} %collective-permute-done.6, bf16[64,2048]{1,0:T(8,128)(2,1)S(1)} %collective-permute-done.5, bf16[64,2048]{1,0:T(8,128)(2,1)S(1)} %maximum_select_fusion.1), kind=kOutput, calls=%fused_computation.3 | convolution fusion | flops 1613365248 | bytes 9961472 | tf_op jit(solution)/shard_map/dot_general | solution.py:64
  33.7 0.1 fusion.32
  33.8 0.9 %collective-permute-start.9 = (bf16[64,2048]{1,0:T(8,128)(2,1)S(1)}, bf16[64,2048]{1,0:T(8,128)(2,1)S(1)}, u32[]{:S(2)}, u32[]{:S(2)}) collective-permute-start(bf16[64,2048]{1,0:T(8,128)(2,1)S(1)} %collective-permute-done.7), channel_id=1, source_target_pairs={{0,16},{1,17},{2,18},{3,19},{4,20},{5,21},{6,22},{7,23},{8,120},{9... | collective-permute-start | bytes 786440 | tf_op jit(solution)/shard_map/ppermute | solution.py:18
  34.8 2.4 %collective-permute-done.13 = bf16[64,2048]{1,0:T(8,128)(2,1)S(1)} collective-permute-done((bf16[64,2048]{1,0:T(8,128)(2,1)S(1)}, bf16[64,2048]{1,0:T(8,128)(2,1)S(1)}, u32[]{:S(2)}, u32[]{:S(2)}) %collective-permute-start.13) | collective-permute-done | bytes 262176 | tf_op jit(solution)/shard_map/ppermute | solution.py:18
  37.2 0.6 collective-permute-start.16
  37.8 0.3 collective-permute-start.8
  38.1 0.6 collective-permute-done.14
  38.7 0.7 collective-permute-start.10
  39.5 0.1 constant_dynamic-slice_fusion.15
  39.6 2.4 %convolution_convert_fusion.2 = bf16[256,2048]{1,0:T(8,128)(2,1)S(1)} fusion(bf16[2048,2048]{1,0:T(8,128)(2,1)S(1)} %bitcast.19, bf16[64,2048]{1,0:T(8,128)(2,1)S(1)} %get-tuple-element.55, bf16[64,2048]{1,0:T(8,128)(2,1)S(1)} %get-tuple-element.56, bf16[64,2048]{1,0:T(8,128)(2,1)S(1)} %get-tuple-element.57, bf16[64,2048]{1,0:T(8,128)(2,1)S(1)} %get-tuple-element.54), kind=kOutput, calls=%fused_computation.2 | convolution fusion | flops 2152202240 | bytes 10485760 | tf_op jit(solution)/shard_map/dot_general | solution.py:64
  42.0 0.1 fusion.31
  42.1 1.6 %collective-permute-start.24 = (bf16[128,2048]{1,0:T(8,128)(2,1)S(1)}, bf16[128,2048]{1,0:T(8,128)(2,1)S(1)}, u32[]{:S(2)}, u32[]{:S(2)}) collective-permute-start(bf16[128,2048]{1,0:T(8,128)(2,1)S(1)} %get-tuple-element.53), channel_id=1, source_target_pairs={{0,1},{1,0},{2,3},{3,2},{4,5},{5,4},{6,7},{7,6},{8,11},{9,10},{10,... | collective-permute-start | bytes 1572872 | tf_op jit(solution)/shard_map/ppermute | solution.py:18
  43.7 2.3 %collective-permute-done.10 = bf16[32,2048]{1,0:T(8,128)(2,1)S(1)} collective-permute-done((bf16[32,2048]{1,0:T(8,128)(2,1)S(1)}, bf16[32,2048]{1,0:T(8,128)(2,1)S(1)}, u32[]{:S(2)}, u32[]{:S(2)}) %collective-permute-start.10) | collective-permute-done | bytes 131104 | tf_op jit(solution)/shard_map/ppermute | solution.py:18
  46.0 0.6 collective-permute-start.15
  46.7 0.9 collective-permute-done.17
  47.6 0.1 constant_dynamic-slice_fusion.11
  47.7 2.4 %convolution_convert_fusion.1 = bf16[256,2048]{1,0:T(8,128)(2,1)S(1)} fusion(bf16[2048,2048]{1,0:T(8,128)(2,1)S(1)} %bitcast.19, bf16[64,2048]{1,0:T(8,128)(2,1)S(1)} %get-tuple-element.49, bf16[64,2048]{1,0:T(8,128)(2,1)S(1)} %get-tuple-element.50, bf16[64,2048]{1,0:T(8,128)(2,1)S(1)} %get-tuple-element.51, bf16[64,2048]{1,0:T(8,128)(2,1)S(1)} %get-tuple-element.48), kind=kOutput, calls=%fused_computation.1 | convolution fusion | flops 2152202240 | bytes 10485760 | tf_op jit(solution)/shard_map/dot_general | solution.py:64
  50.1 0.1 fusion.30
  50.2 1.6 %collective-permute-start.26 = (bf16[128,2048]{1,0:T(8,128)(2,1)S(1)}, bf16[128,2048]{1,0:T(8,128)(2,1)S(1)}, u32[]{:S(2)}, u32[]{:S(2)}) collective-permute-start(bf16[128,2048]{1,0:T(8,128)(2,1)S(1)} %get-tuple-element.47), channel_id=1, source_target_pairs={{0,1},{1,0},{2,3},{3,2},{4,5},{5,4},{6,7},{7,6},{8,11},{9,10},{10,... | collective-permute-start | bytes 1572872 | tf_op jit(solution)/shard_map/ppermute | solution.py:18
  51.8 0.1 pad_maximum_fusion
  52.2 2.9 %convolution_convert_fusion = bf16[320,2048]{1,0:T(8,128)(2,1)S(1)} fusion(bf16[320,2048]{1,0:T(8,128)(2,1)S(1)} %fusion.22, bf16[2048,2048]{1,0:T(8,128)(2,1)S(1)} %bitcast.19), kind=kOutput, calls=%fused_computation | convolution fusion | flops 2685009920 | bytes 11010048 | tf_op jit(solution)/shard_map/dot_general | solution.py:64
  55.1 0.1 fusion.29
  55.2 0.1 pad_maximum_fusion.1
  55.3 0.1 constant_dynamic-slice_fusion.7
  55.4 0.1 broadcast_select_fusion
  55.6 1.4 %collective-permute-start.21 = (bf16[128,2048]{1,0:T(8,128)(2,1)S(1)}, bf16[128,2048]{1,0:T(8,128)(2,1)S(1)}, u32[]{:S(2)}, u32[]{:S(2)}) collective-permute-start(bf16[128,2048]{1,0:T(8,128)(2,1)S(1)} %broadcast_select_fusion), channel_id=1, source_target_pairs={{0,4},{1,5},{2,6},{3,7},{4,0},{5,1},{6,2},{7,3},{8,12},{9,13},{10,... | collective-permute-start | bytes 1572872 | tf_op jit(solution)/shard_map/ppermute | solution.py:18
  57.0 0.8 collective-permute-start.18
  57.8 0.1 convert_add_fusion.1
  58.0 2.8 %collective-permute-start.25 = (bf16[64,2048]{1,0:T(8,128)(2,1)S(1)}, bf16[64,2048]{1,0:T(8,128)(2,1)S(1)}, u32[]{:S(2)}, u32[]{:S(2)}) collective-permute-start(bf16[64,2048]{1,0:T(8,128)(2,1)S(1)} %slice.180), channel_id=1, source_target_pairs={{0,3},{1,2},{2,1},{3,0},{4,7},{5,6},{6,5},{7,4},{8,9},{9,8},{10,11... | collective-permute-start | bytes 786440 | tf_op jit(solution)/shard_map/ppermute | solution.py:18
  60.8 0.1 convert_add_fusion
  61.0 1.5 %collective-permute-start.27 = (bf16[64,2048]{1,0:T(8,128)(2,1)S(1)}, bf16[64,2048]{1,0:T(8,128)(2,1)S(1)}, u32[]{:S(2)}, u32[]{:S(2)}) collective-permute-start(bf16[64,2048]{1,0:T(8,128)(2,1)S(1)} %slice.179), channel_id=1, source_target_pairs={{0,3},{1,2},{2,1},{3,0},{4,7},{5,6},{6,5},{7,4},{8,9},{9,8},{10,11... | collective-permute-start | bytes 786440 | tf_op jit(solution)/shard_map/ppermute | solution.py:18
  62.4 7.8 %collective-permute-done.21 = bf16[128,2048]{1,0:T(8,128)(2,1)S(1)} collective-permute-done((bf16[128,2048]{1,0:T(8,128)(2,1)S(1)}, bf16[128,2048]{1,0:T(8,128)(2,1)S(1)}, u32[]{:S(2)}, u32[]{:S(2)}) %collective-permute-start.21) | collective-permute-done | bytes 524320 | tf_op jit(solution)/shard_map/ppermute | solution.py:18
  70.3 0.2 convert_add_fusion.2
  70.5 0.6 collective-permute-start.22
  71.2 0.6 collective-permute-done.18
  71.7 0.1 fusion.28
  71.9 1.5 %collective-permute-start.19 = (bf16[64,2048]{1,0:T(8,128)(2,1)S(1)}, bf16[64,2048]{1,0:T(8,128)(2,1)S(1)}, u32[]{:S(2)}, u32[]{:S(2)}) collective-permute-start(bf16[64,2048]{1,0:T(8,128)(2,1)S(1)} %pad_maximum_fusion.7), channel_id=1, source_target_pairs={{0,3},{1,2},{2,1},{3,0},{4,7},{5,6},{6,5},{7,4},{8,9},{9,8},{10,11... | collective-permute-start | bytes 786440 | tf_op jit(solution)/shard_map/ppermute | solution.py:18
  73.5 0.1 select_convert_fusion
  73.6 0.8 collective-permute-start.28
  74.4 5.9 %collective-permute-done.19 = bf16[64,2048]{1,0:T(8,128)(2,1)S(1)} collective-permute-done((bf16[64,2048]{1,0:T(8,128)(2,1)S(1)}, bf16[64,2048]{1,0:T(8,128)(2,1)S(1)}, u32[]{:S(2)}, u32[]{:S(2)}) %collective-permute-start.19) | collective-permute-done | bytes 262176 | tf_op jit(solution)/shard_map/ppermute | solution.py:18
  80.3 0.1 select_convert_fusion.1
  80.4 1.4 %collective-permute-start.20 = (bf16[32,2048]{1,0:T(8,128)(2,1)S(1)}, bf16[32,2048]{1,0:T(8,128)(2,1)S(1)}, u32[]{:S(2)}, u32[]{:S(2)}) collective-permute-start(bf16[32,2048]{1,0:T(8,128)(2,1)S(1)} %select_convert_fusion.1), channel_id=1, source_target_pairs={{0,4},{1,5},{2,6},{3,7},{4,0},{5,1},{6,2},{7,3},{8,12},{9,13},{10,... | collective-permute-start | bytes 393224 | tf_op jit(solution)/shard_map/ppermute | solution.py:18
  81.8 0.4 collective-permute-start.23
  82.2 3.3 %collective-permute-done.20 = bf16[32,2048]{1,0:T(8,128)(2,1)S(1)} collective-permute-done((bf16[32,2048]{1,0:T(8,128)(2,1)S(1)}, bf16[32,2048]{1,0:T(8,128)(2,1)S(1)}, u32[]{:S(2)}, u32[]{:S(2)}) %collective-permute-start.20) | collective-permute-done | bytes 131104 | tf_op jit(solution)/shard_map/ppermute | solution.py:18
  85.5 0.1 convert_add_fusion.5
  85.5 2.6 %collective-permute-done.23 = bf16[32,2048]{1,0:T(8,128)(2,1)S(1)} collective-permute-done((bf16[32,2048]{1,0:T(8,128)(2,1)S(1)}, bf16[32,2048]{1,0:T(8,128)(2,1)S(1)}, u32[]{:S(2)}, u32[]{:S(2)}) %collective-permute-start.23) | collective-permute-done | bytes 131104 | tf_op jit(solution)/shard_map/ppermute | solution.py:18
  88.1 0.2 convert_add_fusion.4
  88.3 1.1 %maximum_select_fusion = f32[128,2048]{1,0:T(8,128)} fusion(f32[64,2048]{1,0:T(8,128)S(1)} %convert_add_fusion.4, f32[32,2048]{1,0:T(8,128)S(1)} %slice_add_fusion.3, f32[32,2048]{1,0:T(8,128)S(1)} %convert_add_fusion.5, pred[]{:T(512)S(6)} %eq.114), kind=kLoop, calls=%fused_computation.22 | loop fusion | flops 1310720 | bytes 2097153 | tf_op jit(solution)/shard_map/jit(_where)/select_n | solution.py:177
  (59 shorter events, 0.9 us)
Async XLA Ops:
  0.0 1.6 %copy-start = (bf16[4,512,512]{2,1,0:T(8,128)(2,1)S(1)}, bf16[4,512,512]{2,1,0:T(8,128)(2,1)}, u32[]{:S(2)}) copy-start(bf16[4,512,512]{2,1,0:T(8,128)(2,1)} %param.5) | copy-start | bytes 6291460
  3.0 1.4 %collective-permute-start = (bf16[32,2048]{1,0:T(8,128)(2,1)S(1)}, bf16[32,2048]{1,0:T(8,128)(2,1)S(1)}, u32[]{:S(2)}, u32[]{:S(2)}) collective-permute-start(bf16[32,2048]{1,0:T(8,128)(2,1)S(1)} %bitcast.14), channel_id=1, source_target_pairs={{0,8},{1,9},{2,10},{3,11},{4,12},{5,13},{6,14},{7,15},{8,0},{9,1},... | collective-permute-start | bytes 393224 | tf_op jit(solution)/shard_map/ppermute | solution.py:18
  4.4 11.1 %collective-permute-start.2 = (bf16[64,2048]{1,0:T(8,128)(2,1)S(1)}, bf16[64,2048]{1,0:T(8,128)(2,1)S(1)}, u32[]{:S(2)}, u32[]{:S(2)}) collective-permute-start(bf16[64,2048]{1,0:T(8,128)(2,1)S(1)} %maximum_select_fusion.1), channel_id=1, source_target_pairs={{0,16},{1,17},{2,18},{3,19},{4,20},{5,21},{6,22},{7,23},{8,120},{9... | collective-permute-start | bytes 786440 | tf_op jit(solution)/shard_map/ppermute | solution.py:18
  6.4 6.5 %collective-permute-start.1 = (bf16[32,2048]{1,0:T(8,128)(2,1)S(1)}, bf16[32,2048]{1,0:T(8,128)(2,1)S(1)}, u32[]{:S(2)}, u32[]{:S(2)}) collective-permute-start(bf16[32,2048]{1,0:T(8,128)(2,1)S(1)} %bitcast.16), channel_id=1, source_target_pairs={{0,128},{1,129},{2,130},{3,131},{4,132},{5,133},{6,134},{7,135},{8... | collective-permute-start | bytes 393224 | tf_op jit(solution)/shard_map/ppermute | solution.py:18
  12.9 5.6 %collective-permute-start.3 = (bf16[32,2048]{1,0:T(8,128)(2,1)S(1)}, bf16[32,2048]{1,0:T(8,128)(2,1)S(1)}, u32[]{:S(2)}, u32[]{:S(2)}) collective-permute-start(bf16[32,2048]{1,0:T(8,128)(2,1)S(1)} %collective-permute-done.1), channel_id=1, source_target_pairs={{0,8},{1,9},{2,10},{3,11},{4,12},{5,13},{6,14},{7,15},{8,0},{9,1},... | collective-permute-start | bytes 393224 | tf_op jit(solution)/shard_map/ppermute | solution.py:18
  15.6 7.6 %collective-permute-start.5 = (bf16[64,2048]{1,0:T(8,128)(2,1)S(1)}, bf16[64,2048]{1,0:T(8,128)(2,1)S(1)}, u32[]{:S(2)}, u32[]{:S(2)}) collective-permute-start(bf16[64,2048]{1,0:T(8,128)(2,1)S(1)} %collective-permute-done.2), channel_id=1, source_target_pairs={{0,16},{1,17},{2,18},{3,19},{4,20},{5,21},{6,22},{7,23},{8,120},{9... | collective-permute-start | bytes 786440 | tf_op jit(solution)/shard_map/ppermute | solution.py:18
  15.6 8.1 %collective-permute-start.12 = (bf16[64,2048]{1,0:T(8,128)(2,1)S(1)}, bf16[64,2048]{1,0:T(8,128)(2,1)S(1)}, u32[]{:S(2)}, u32[]{:S(2)}) collective-permute-start(bf16[64,2048]{1,0:T(8,128)(2,1)S(1)} %collective-permute-done.2), channel_id=1, source_target_pairs={{0,8},{1,9},{2,10},{3,11},{4,12},{5,13},{6,14},{7,15},{8,0},{9,1},... | collective-permute-start | bytes 786440 | tf_op jit(solution)/shard_map/ppermute | solution.py:18
  18.6 15.3 %collective-permute-start.7 = (bf16[64,2048]{1,0:T(8,128)(2,1)S(1)}, bf16[64,2048]{1,0:T(8,128)(2,1)S(1)}, u32[]{:S(2)}, u32[]{:S(2)}) collective-permute-start(bf16[64,2048]{1,0:T(8,128)(2,1)S(1)} %maximum_select_fusion.2), channel_id=1, source_target_pairs={{0,32},{1,33},{2,34},{3,35},{4,36},{5,37},{6,38},{7,39},{8,104},{9... | collective-permute-start | bytes 786440 | tf_op jit(solution)/shard_map/ppermute | solution.py:18
  19.6 15.2 %collective-permute-start.4 = (bf16[64,2048]{1,0:T(8,128)(2,1)S(1)}, bf16[64,2048]{1,0:T(8,128)(2,1)S(1)}, u32[]{:S(2)}, u32[]{:S(2)}) collective-permute-start(bf16[64,2048]{1,0:T(8,128)(2,1)S(1)} %maximum_select_fusion.2), channel_id=1, source_target_pairs={{0,16},{1,17},{2,18},{3,19},{4,20},{5,21},{6,22},{7,23},{8,120},{9... | collective-permute-start | bytes 786440 | tf_op jit(solution)/shard_map/ppermute | solution.py:18
  23.2 4.1 %collective-permute-start.6 = (bf16[64,2048]{1,0:T(8,128)(2,1)S(1)}, bf16[64,2048]{1,0:T(8,128)(2,1)S(1)}, u32[]{:S(2)}, u32[]{:S(2)}) collective-permute-start(bf16[64,2048]{1,0:T(8,128)(2,1)S(1)} %collective-permute-done.5), channel_id=1, source_target_pairs={{0,8},{1,9},{2,10},{3,11},{4,12},{5,13},{6,14},{7,15},{8,0},{9,1},... | collective-permute-start | bytes 786440 | tf_op jit(solution)/shard_map/ppermute | solution.py:18
  23.2 18.9 %collective-permute-start.11 = (bf16[32,2048]{1,0:T(8,128)(2,1)S(1)}, bf16[32,2048]{1,0:T(8,128)(2,1)S(1)}, u32[]{:S(2)}, u32[]{:S(2)}) collective-permute-start(bf16[32,2048]{1,0:T(8,128)(2,1)S(1)} %constant_dynamic-slice_fusion.16), channel_id=1, source_target_pairs={{0,32},{1,33},{2,34},{3,35},{4,36},{5,37},{6,38},{7,39},{8,104},{9... | collective-permute-start | bytes 393224 | tf_op jit(solution)/shard_map/ppermute | solution.py:18
  23.7 13.5 %collective-permute-start.13 = (bf16[64,2048]{1,0:T(8,128)(2,1)S(1)}, bf16[64,2048]{1,0:T(8,128)(2,1)S(1)}, u32[]{:S(2)}, u32[]{:S(2)}) collective-permute-start(bf16[64,2048]{1,0:T(8,128)(2,1)S(1)} %collective-permute-done.5), channel_id=1, source_target_pairs={{0,16},{1,17},{2,18},{3,19},{4,20},{5,21},{6,22},{7,23},{8,120},{9... | collective-permute-start | bytes 786440 | tf_op jit(solution)/shard_map/ppermute | solution.py:18
  27.2 12.3 %slice-start = ((s8[8388608]{0:T(1024)(128)(4,1)}), s8[4194304]{0:T(1024)(128)(4,1)S(1)}, s32[]{:S(2)}) async-start(s8[8388608]{0:T(1024)(128)(4,1)} %bitcast.18), calls=%async_computation | async-start | bytes 8388608
  27.3 12.3 %slice-start.1 = ((s8[8388608]{0:T(1024)(128)(4,1)}), s8[4194304]{0:T(1024)(128)(4,1)S(1)}, s32[]{:S(2)}) async-start(s8[8388608]{0:T(1024)(128)(4,1)} %bitcast.18), calls=%async_computation.1 | async-start | bytes 8388608
  33.8 12.2 %collective-permute-start.9 = (bf16[64,2048]{1,0:T(8,128)(2,1)S(1)}, bf16[64,2048]{1,0:T(8,128)(2,1)S(1)}, u32[]{:S(2)}, u32[]{:S(2)}) collective-permute-start(bf16[64,2048]{1,0:T(8,128)(2,1)S(1)} %collective-permute-done.7), channel_id=1, source_target_pairs={{0,16},{1,17},{2,18},{3,19},{4,20},{5,21},{6,22},{7,23},{8,120},{9... | collective-permute-start | bytes 786440 | tf_op jit(solution)/shard_map/ppermute | solution.py:18
  37.2 1.5 %collective-permute-start.14 = (bf16[64,2048]{1,0:T(8,128)(2,1)S(1)}, bf16[64,2048]{1,0:T(8,128)(2,1)S(1)}, u32[]{:S(2)}, u32[]{:S(2)}) collective-permute-start(bf16[64,2048]{1,0:T(8,128)(2,1)S(1)} %collective-permute-done.13), channel_id=1, source_target_pairs={{0,8},{1,9},{2,10},{3,11},{4,12},{5,13},{6,14},{7,15},{8,0},{9,1},... | collective-permute-start | bytes 786440 | tf_op jit(solution)/shard_map/ppermute | solution.py:18
  37.2 9.4 %collective-permute-start.16 = (bf16[64,2048]{1,0:T(8,128)(2,1)S(1)}, bf16[64,2048]{1,0:T(8,128)(2,1)S(1)}, u32[]{:S(2)}, u32[]{:S(2)}) collective-permute-start(bf16[64,2048]{1,0:T(8,128)(2,1)S(1)} %collective-permute-done.4), channel_id=1, source_target_pairs={{0,8},{1,9},{2,10},{3,11},{4,12},{5,13},{6,14},{7,15},{8,0},{9,1},... | collective-permute-start | bytes 786440 | tf_op jit(solution)/shard_map/ppermute | solution.py:18
  37.8 14.0 %collective-permute-start.8 = (bf16[64,2048]{1,0:T(8,128)(2,1)S(1)}, bf16[64,2048]{1,0:T(8,128)(2,1)S(1)}, u32[]{:S(2)}, u32[]{:S(2)}) collective-permute-start(bf16[64,2048]{1,0:T(8,128)(2,1)S(1)} %collective-permute-done.7), channel_id=1, source_target_pairs={{0,8},{1,9},{2,10},{3,11},{4,12},{5,13},{6,14},{7,15},{8,0},{9,1},... | collective-permute-start | bytes 786440 | tf_op jit(solution)/shard_map/ppermute | solution.py:18
  38.7 7.3 %collective-permute-start.10 = (bf16[32,2048]{1,0:T(8,128)(2,1)S(1)}, bf16[32,2048]{1,0:T(8,128)(2,1)S(1)}, u32[]{:S(2)}, u32[]{:S(2)}) collective-permute-start(bf16[32,2048]{1,0:T(8,128)(2,1)S(1)} %constant_dynamic-slice_fusion.17), channel_id=1, source_target_pairs={{0,32},{1,33},{2,34},{3,35},{4,36},{5,37},{6,38},{7,39},{8,104},{9... | collective-permute-start | bytes 393224 | tf_op jit(solution)/shard_map/ppermute | solution.py:18
  42.1 15.7 %collective-permute-start.24 = (bf16[128,2048]{1,0:T(8,128)(2,1)S(1)}, bf16[128,2048]{1,0:T(8,128)(2,1)S(1)}, u32[]{:S(2)}, u32[]{:S(2)}) collective-permute-start(bf16[128,2048]{1,0:T(8,128)(2,1)S(1)} %get-tuple-element.53), channel_id=1, source_target_pairs={{0,1},{1,0},{2,3},{3,2},{4,5},{5,4},{6,7},{7,6},{8,11},{9,10},{10,... | collective-permute-start | bytes 1572872 | tf_op jit(solution)/shard_map/ppermute | solution.py:18
  46.0 1.5 %collective-permute-start.17 = (bf16[64,2048]{1,0:T(8,128)(2,1)S(1)}, bf16[64,2048]{1,0:T(8,128)(2,1)S(1)}, u32[]{:S(2)}, u32[]{:S(2)}) collective-permute-start(bf16[64,2048]{1,0:T(8,128)(2,1)S(1)} %collective-permute-done.9), channel_id=1, source_target_pairs={{0,8},{1,9},{2,10},{3,11},{4,12},{5,13},{6,14},{7,15},{8,0},{9,1},... | collective-permute-start | bytes 786440 | tf_op jit(solution)/shard_map/ppermute | solution.py:18
  46.0 5.7 %collective-permute-start.15 = (bf16[64,2048]{1,0:T(8,128)(2,1)S(1)}, bf16[64,2048]{1,0:T(8,128)(2,1)S(1)}, u32[]{:S(2)}, u32[]{:S(2)}) collective-permute-start(bf16[64,2048]{1,0:T(8,128)(2,1)S(1)} %pad_maximum_fusion.5), channel_id=1, source_target_pairs={{0,8},{1,9},{2,10},{3,11},{4,12},{5,13},{6,14},{7,15},{8,0},{9,1},... | collective-permute-start | bytes 786440 | tf_op jit(solution)/shard_map/ppermute | solution.py:18
  50.2 10.7 %collective-permute-start.26 = (bf16[128,2048]{1,0:T(8,128)(2,1)S(1)}, bf16[128,2048]{1,0:T(8,128)(2,1)S(1)}, u32[]{:S(2)}, u32[]{:S(2)}) collective-permute-start(bf16[128,2048]{1,0:T(8,128)(2,1)S(1)} %get-tuple-element.47), channel_id=1, source_target_pairs={{0,1},{1,0},{2,3},{3,2},{4,5},{5,4},{6,7},{7,6},{8,11},{9,10},{10,... | collective-permute-start | bytes 1572872 | tf_op jit(solution)/shard_map/ppermute | solution.py:18
  55.6 14.7 %collective-permute-start.21 = (bf16[128,2048]{1,0:T(8,128)(2,1)S(1)}, bf16[128,2048]{1,0:T(8,128)(2,1)S(1)}, u32[]{:S(2)}, u32[]{:S(2)}) collective-permute-start(bf16[128,2048]{1,0:T(8,128)(2,1)S(1)} %broadcast_select_fusion), channel_id=1, source_target_pairs={{0,4},{1,5},{2,6},{3,7},{4,0},{5,1},{6,2},{7,3},{8,12},{9,13},{10,... | collective-permute-start | bytes 1572872 | tf_op jit(solution)/shard_map/ppermute | solution.py:18
  57.0 14.8 %collective-permute-start.18 = (bf16[128,2048]{1,0:T(8,128)(2,1)S(1)}, bf16[128,2048]{1,0:T(8,128)(2,1)S(1)}, u32[]{:S(2)}, u32[]{:S(2)}) collective-permute-start(bf16[128,2048]{1,0:T(8,128)(2,1)S(1)} %pad_maximum_fusion.2), channel_id=1, source_target_pairs={{0,1},{1,0},{2,3},{3,2},{4,5},{5,4},{6,7},{7,6},{8,11},{9,10},{10,... | collective-permute-start | bytes 1572872 | tf_op jit(solution)/shard_map/ppermute | solution.py:18
  58.0 15.5 %collective-permute-start.25 = (bf16[64,2048]{1,0:T(8,128)(2,1)S(1)}, bf16[64,2048]{1,0:T(8,128)(2,1)S(1)}, u32[]{:S(2)}, u32[]{:S(2)}) collective-permute-start(bf16[64,2048]{1,0:T(8,128)(2,1)S(1)} %slice.180), channel_id=1, source_target_pairs={{0,3},{1,2},{2,1},{3,0},{4,7},{5,6},{6,5},{7,4},{8,9},{9,8},{10,11... | collective-permute-start | bytes 786440 | tf_op jit(solution)/shard_map/ppermute | solution.py:18
  61.0 12.5 %collective-permute-start.27 = (bf16[64,2048]{1,0:T(8,128)(2,1)S(1)}, bf16[64,2048]{1,0:T(8,128)(2,1)S(1)}, u32[]{:S(2)}, u32[]{:S(2)}) collective-permute-start(bf16[64,2048]{1,0:T(8,128)(2,1)S(1)} %slice.179), channel_id=1, source_target_pairs={{0,3},{1,2},{2,1},{3,0},{4,7},{5,6},{6,5},{7,4},{8,9},{9,8},{10,11... | collective-permute-start | bytes 786440 | tf_op jit(solution)/shard_map/ppermute | solution.py:18
  70.5 11.2 %collective-permute-start.22 = (bf16[64,2048]{1,0:T(8,128)(2,1)S(1)}, bf16[64,2048]{1,0:T(8,128)(2,1)S(1)}, u32[]{:S(2)}, u32[]{:S(2)}) collective-permute-start(bf16[64,2048]{1,0:T(8,128)(2,1)S(1)} %slice.181), channel_id=1, source_target_pairs={{0,1},{1,0},{2,3},{3,2},{4,5},{5,4},{6,7},{7,6},{8,11},{9,10},{10,... | collective-permute-start | bytes 786440 | tf_op jit(solution)/shard_map/ppermute | solution.py:18
  71.9 8.4 %collective-permute-start.19 = (bf16[64,2048]{1,0:T(8,128)(2,1)S(1)}, bf16[64,2048]{1,0:T(8,128)(2,1)S(1)}, u32[]{:S(2)}, u32[]{:S(2)}) collective-permute-start(bf16[64,2048]{1,0:T(8,128)(2,1)S(1)} %pad_maximum_fusion.7), channel_id=1, source_target_pairs={{0,3},{1,2},{2,1},{3,0},{4,7},{5,6},{6,5},{7,4},{8,9},{9,8},{10,11... | collective-permute-start | bytes 786440 | tf_op jit(solution)/shard_map/ppermute | solution.py:18
  73.6 14.5 %collective-permute-start.28 = (bf16[64,2048]{1,0:T(8,128)(2,1)S(1)}, bf16[64,2048]{1,0:T(8,128)(2,1)S(1)}, u32[]{:S(2)}, u32[]{:S(2)}) collective-permute-start(bf16[64,2048]{1,0:T(8,128)(2,1)S(1)} %select_convert_fusion), channel_id=1, source_target_pairs={{0,4},{1,5},{2,6},{3,7},{4,0},{5,1},{6,2},{7,3},{8,12},{9,13},{10,... | collective-permute-start | bytes 786440 | tf_op jit(solution)/shard_map/ppermute | solution.py:18
  80.4 5.1 %collective-permute-start.20 = (bf16[32,2048]{1,0:T(8,128)(2,1)S(1)}, bf16[32,2048]{1,0:T(8,128)(2,1)S(1)}, u32[]{:S(2)}, u32[]{:S(2)}) collective-permute-start(bf16[32,2048]{1,0:T(8,128)(2,1)S(1)} %select_convert_fusion.1), channel_id=1, source_target_pairs={{0,4},{1,5},{2,6},{3,7},{4,0},{5,1},{6,2},{7,3},{8,12},{9,13},{10,... | collective-permute-start | bytes 393224 | tf_op jit(solution)/shard_map/ppermute | solution.py:18
  81.8 6.3 %collective-permute-start.23 = (bf16[32,2048]{1,0:T(8,128)(2,1)S(1)}, bf16[32,2048]{1,0:T(8,128)(2,1)S(1)}, u32[]{:S(2)}, u32[]{:S(2)}) collective-permute-start(bf16[32,2048]{1,0:T(8,128)(2,1)S(1)} %slice.182), channel_id=1, source_target_pairs={{0,3},{1,2},{2,1},{3,0},{4,7},{5,6},{6,5},{7,4},{8,9},{9,8},{10,11... | collective-permute-start | bytes 393224 | tf_op jit(solution)/shard_map/ppermute | solution.py:18
